TPU v7x, 128 devices: a whole 4x4x4 slice. The times are simulated.
128 devices in a mesh: row: 4 (over x), col: 8 (over y_lo, z), depth: 4 (over y_hi, core).
Axes of the slice: x: 4, y: 4 (y_hi: 2, y_lo: 2; y = y_hi * 2 + y_lo), z: 4, core: 2. Of those that a mesh axis runs over, the one named last changes fastest.
Arguments:
- inputs: bfloat16 [20480, 1664], P(('row', 'col', 'depth')), may hold values from -6 to 6
- upstream: bfloat16 [20480, 1664], P(('row', 'col', 'depth')), may hold values from -6 to 6
- norm_gain: float32 [1664], replicated, may hold values from 0.5 to 1.5
- norm_shift: float32 [1664], replicated, may hold values from -3 to 3
- expand_weight: bfloat16 [1664, 8192], P(('row', 'depth'), 'col'), may hold values from -0.15625 to 0.15625
- expand_bias: float32 [8192], P('col'), may hold values from -3 to 3
- shrink_weight: bfloat16 [1664, 8192], P(('row', 'depth'), 'col'), may hold values from -0.0625 to 0.0625
Outputs:
- inputs_grad: bfloat16 [20480, 1664], P(('row', 'col', 'depth'))
- gain_grad: float32 [1664], replicated
- shift_grad: float32 [1664], replicated
- expand_grad: float32 [1664, 8192], P(('row', 'depth'), 'col')
- bias_grad: float32 [8192], P('col')
- shrink_grad: float32 [1664, 8192], P(('row', 'depth'), 'col')
All inputs are finite; a program needn't handle non-finite values.
Results may differ from a plain program's by a relative error of at most 0.007.
Values may be sent and summed in bfloat16 or wider, within the bound.
No kernel may reach another device: no remote copies, remote signals or barrier semaphores. Data moves between devices by JAX's collectives and lax.ppermute only.
A program may use at most 128 MiB of HBM per device.

v0:
```python
import functools

import jax
import jax.numpy as jnp
from jax import lax
from jax.experimental import pallas as pl
from jax.experimental.pallas import tpu as pltpu
from jax.sharding import Mesh, PartitionSpec as P

EPSILON = 1e-06
ROOT_HALF = 0.7071067811865476
INV_ROOT_TWO_PI = 0.3989422804014327

AXES = ("x", "ylo", "z", "yhi", "core")
PLANE_Y = ("ylo", "yhi")
f32, bf16 = jnp.float32, jnp.bfloat16


def y_index(y):
    return (y % 2) * 2 + y // 2


def shift(value, axis, by):
    if axis == "y":
        pairs = [(y_index(y), y_index((y + by) % 4)) for y in range(4)]
        return lax.ppermute(value, PLANE_Y, pairs)
    return lax.ppermute(value, axis, [(i, (i + by) % 4) for i in range(4)])


def swap(value):
    return lax.ppermute(value, "core", [(0, 1), (1, 0)])


def after(value, *others):
    return lax.optimization_barrier((value, *others))[0]


def both_ways(ahead, behind, axis):
    return shift(ahead, axis, 1), shift(behind, axis, -1)


def ring_sum(value, axis):
    return (value + shift(value, axis, 2)) + (shift(value, axis, 1) + shift(value, axis, -1))


def parts_of(vector):
    high = lax.reduce_precision(vector, 8, 7)
    return jnp.concatenate([high, lax.reduce_precision(vector - high, 8, 7)], 0).astype(bf16)


def from_parts(rows):
    return rows[:16].astype(f32) + rows[16:].astype(f32)


def direct_scatter(block, axis, vector=None):
    rows = block(0).shape[0]
    riding = [] if vector is None else [parts_of(vector)]
    got = [shift(jnp.concatenate([block(by).astype(bf16), *riding], 0), axis, by) for by in (1, 2, 3)]
    ahead, far, behind = (part[:rows].astype(f32) for part in got)
    summed = block(0) + ahead + behind + far
    if vector is None:
        return summed, None
    own, v_ahead, v_far, v_behind = (from_parts(part) for part in (*riding, *(p[rows:] for p in got)))
    return summed, (own + v_far) + (v_ahead + v_behind)


def assemble_kernel(first, own, right, far_low, far_high, left, whole):
    x, y = place()
    rows, half = own.shape[0] // 4, own.shape[1]
    for far_second in range(4):
        for far_first in range(4):
            if far_second == 2:
                bundle, at = (far_low, far_first) if far_first < 2 else (far_high, far_first - 2)
            else:
                bundle, at = {0: own, 1: right, 3: left}[far_second], far_first
            far_x, far_y = (far_first, far_second) if first == "x" else (far_second, far_first)
            px, py = lax.rem(x + far_x, 4), lax.rem(y + far_y, 4)
            row = pl.multiple_of((2 * px + lax.div(py, 2)) * rows, 16)
            column = pl.multiple_of(lax.rem(py, 2) * half, 128)
            whole[pl.ds(row, rows), pl.ds(column, half)] = bundle[at * rows : (at + 1) * rows, :]


def place():
    return lax.axis_index("x"), 2 * lax.axis_index("yhi") + lax.axis_index("ylo")


def gelu_parts(pre):
    cdf = 0.5 * (1.0 + lax.erf(pre * ROOT_HALF))
    density = INV_ROOT_TWO_PI * jnp.exp(-0.5 * pre * pre)
    return pre * cdf, cdf + pre * density


def dot(left, right, dims=((1,), (0,))):
    return lax.dot_general(left, right, (dims, ((), ())), preferred_element_type=f32)


def call(kernel, outs, args, scratch=(), aliases=None, limit=16):
    return pl.pallas_call(
        kernel,
        out_shape=[jax.ShapeDtypeStruct(shape, dtype) for shape, dtype in outs],
        in_specs=[pl.BlockSpec(memory_space=pltpu.VMEM)] * len(args),
        out_specs=[pl.BlockSpec(memory_space=pltpu.VMEM)] * len(outs),
        scratch_shapes=list(scratch),
        input_output_aliases=aliases or {},
        compiler_params=pltpu.CompilerParams(vmem_limit_bytes=limit * 2**20),
        cost_estimate=pl.CostEstimate(flops=10**6, bytes_accessed=10**6, transcendentals=0),
    )(*args)


def norm_kernel(half, part, gain, shift_by, *refs):
    normed, centre, scale, normed_t, up_t, turned = refs[-6:]
    tokens, width = part.shape[2:]
    to, rows = pl.ds(half * 4 * tokens, 4 * tokens), width // 8

    def normalise(k, _):
        at = pl.ds(pl.multiple_of(k * tokens, 16), tokens)
        features = part[k, 0].astype(f32)
        mean = jnp.mean(features, axis=1, keepdims=True)
        shifted = features - mean
        inv = lax.rsqrt(jnp.mean(shifted * shifted, axis=1, keepdims=True) + EPSILON)
        normed[at, :] = (shifted * inv * gain[...] + shift_by[...]).astype(bf16)
        centre[at, :] = mean
        scale[at, :] = inv
        return 0

    def turn(c, _):
        lanes = pl.ds(pl.multiple_of(c * 128, 128), 128)
        up_t[lanes, to] = jnp.concatenate([part[k, 1, :, lanes] for k in range(4)], 0).T
        turned[lanes, :] = normed[:, lanes].T
        return 0

    def order(b, _):
        at = pl.multiple_of((lax.rem(b, 2) * 4 + lax.div(b, 2)) * rows, 16)
        normed_t[pl.ds(at, rows), to] = turned[pl.ds(pl.multiple_of(b * rows, 16), rows), :]
        return 0

    lax.fori_loop(0, 4, normalise, 0)
    lax.fori_loop(0, width // 128, turn, 0)
    lax.fori_loop(0, 8, order, 0)


def hidden_kernel(half, part, normed, expand, shrink, bias, *refs):
    bias_sum, active, back, pre_tile, back_tile = refs[-5:]
    tokens, width = part.shape[2:]
    tile, to = 256, pl.ds(half * 4 * tokens, 4 * tokens)
    tiles = expand.shape[1] // tile

    def lanes_of(j):
        return pl.ds(pl.multiple_of(j * tile, tile), tile)

    def products(j, slot):
        lanes = lanes_of(j)
        pre_tile[slot] = dot(normed[...], expand[:, lanes])
        back_tile[slot] = dot(jnp.concatenate([part[k, 1] for k in range(4)], 0), shrink[:, lanes])

    def finish(j, slot):
        lanes = lanes_of(j)
        value, slope = gelu_parts(pre_tile[slot] + bias[:, lanes])
        active[to, lanes] = value.astype(bf16)
        grad = (back_tile[slot] * slope).astype(bf16)
        back[to, lanes] = grad
        bias_sum[:, lanes] = jnp.sum(grad.astype(f32), axis=0, keepdims=True)

    def step(j, _):
        products(2 * j + 1, 1)
        finish(2 * j, 0)
        following = lax.rem(2 * j + 2, tiles)
        products(following, 0)
        finish(2 * j + 1, 1)
        return 0

    products(0, 0)
    lax.fori_loop(0, tiles // 2, step, 0)


def shrink_tile(far, n, up_t, active):
    x, _ = place()
    rows, lanes = up_t.shape[0] // 4, pl.ds(pl.multiple_of(n * 256, 256), 256)
    return lanes, dot(up_t[pl.ds(pl.multiple_of(lax.rem(x + far, 4) * rows, 16), rows), :], active[:, lanes])


def expand_tile(far, n, normed_t, back):
    _, y = place()
    py = lax.rem(y + far, 4)
    rows, half = normed_t.shape[0] // 2, back.shape[1] // 2
    right = back[:, pl.ds(pl.multiple_of(lax.rem(py, 2) * half + n * 256, 256), 256)]
    left = normed_t[pl.ds(pl.multiple_of(lax.div(py, 2) * rows, 16), rows), :]
    return pl.ds(pl.multiple_of(n * 256, 256), 256), dot(left, right)


def far_kernel(up_t, active, normed_t, back, sums, bias, shrink_low, shrink_high, expand_low, expand_high, vector):
    def tile_of(make, left, right, low, high):
        def step(n, _):
            lanes, term = make(2, n, left, right)
            rows = term.shape[0] // 2
            low[pl.ds(0, rows), lanes] = term[:rows].astype(bf16)
            high[pl.ds(0, rows), lanes] = term[rows:].astype(bf16)
            return 0

        return step

    lax.fori_loop(0, active.shape[1] // 256, tile_of(shrink_tile, up_t, active, shrink_low, shrink_high), 0)
    lax.fori_loop(0, back.shape[1] // 512, tile_of(expand_tile, normed_t, back, expand_low, expand_high), 0)
    half, width = expand_low.shape[1], sums.shape[1]
    vector[...] = jnp.zeros_like(vector)
    for i in range(2):
        for j, start in enumerate(range(0, width, half)):
            size = min(half, width - start)
            vector[4 * i + j : 4 * i + j + 1, :size] = sums[i : i + 1, start : start + size]
        vector[8 + i : 9 + i, :] = bias[:, i * half : (i + 1) * half]
    high = vector[...].astype(bf16)
    riding = jnp.concatenate([high, (vector[...] - high.astype(f32)).astype(bf16)], 0)
    for to in (expand_low, expand_high):
        to[to.shape[0] - 32 :, :] = riding
    vector[...] = riding[:16].astype(f32) + riding[16:].astype(f32)


def near_kernel(up_t, active, normed_t, back, shrink_own, expand_own, shrink_terms, expand_terms):
    def tile_of(make, left, right, own, terms):
        def for_own(n, _):
            lanes, term = make(0, n, left, right)
            own[:, lanes] = term
            return 0

        def for_others(i, _):
            d, n = lax.rem(i, 2), lax.div(i, 2)
            lanes, term = make(1 + 2 * d, n, left, right)
            terms[d, :, lanes] = term
            return 0

        return for_own, for_others

    for make, left, right, own, terms in (
        (shrink_tile, up_t, active, shrink_own, shrink_terms),
        (expand_tile, normed_t, back, expand_own, expand_terms),
    ):
        tiles = own.shape[1] // 256
        for_own, for_others = tile_of(make, left, right, own, terms)
        lax.fori_loop(0, 2 * tiles, for_others, 0)
        lax.fori_loop(0, tiles, for_own, 0)


def pass_kernel(s_terms, e_terms, s_low, s_high, e_low, e_high, s_ahead, s_behind, e_ahead, e_behind):
    for terms, low, high, ahead, behind in (
        (s_terms, s_low, s_high, s_ahead, s_behind),
        (e_terms, e_low, e_high, e_ahead, e_behind),
    ):
        rows = terms.shape[1] // 2

        def step(i, _, rows=rows, terms=terms, low=low, high=high, ahead=ahead, behind=behind):
            at, then = pl.ds(pl.multiple_of(i * 16, 16), 16), pl.ds(pl.multiple_of(rows + i * 16, 16), 16)
            ahead[at, :] = (terms[0, at, :] + low[at, :].astype(f32)).astype(bf16)
            ahead[then, :] = terms[0, then, :].astype(bf16)
            behind[at, :] = terms[1, at, :].astype(bf16)
            behind[then, :] = (terms[1, then, :] + high[at, :].astype(f32)).astype(bf16)
            return 0

        lax.fori_loop(0, rows // 16, step, 0)
    rows = e_terms.shape[1]
    e_ahead[rows:, :] = e_low[rows // 2 :, :]


def rows_kernel(near, other, near_centre, other_centre, near_scale, other_scale, back, expand, mine, others, sums):
    tokens, width = near.shape[2:]

    def tile_of(lanes):
        gain = plain = 0.0
        for half, part, centre, scale in ((1, other, other_centre, other_scale), (0, near, near_centre, near_scale)):
            rows = dot(back[pl.ds(half * 4 * tokens, 4 * tokens), :], expand[lanes, :], ((1,), (1,)))
            features = jnp.concatenate([part[k, 0, :, lanes] for k in range(4)], 0).astype(f32)
            normed = (features - centre[...]) * scale[...]
            gain = gain + jnp.sum(rows * normed, axis=0, keepdims=True)
            plain = plain + jnp.sum(rows, axis=0, keepdims=True)
            if half:
                others[:, lanes] = rows.astype(bf16)
            else:
                mine[:, lanes] = rows
        sums[0:1, lanes] = gain
        sums[1:2, lanes] = plain

    def step(j, _):
        tile_of(pl.ds(pl.multiple_of(j * 256, 256), 256))
        return 0

    whole = width // 256
    lax.fori_loop(0, whole, step, 0)
    if width % 256:
        tile_of(slice(whole * 256, width))


def local(inputs, upstream, norm_gain, norm_shift, expand_weight, expand_bias, shrink_weight):
    tokens, width = inputs.shape
    rows, hidden = expand_weight.shape
    half = hidden // 2
    x, ylo, z, yhi, core = (lax.axis_index(name) for name in AXES)
    y = 2 * yhi + ylo

    def by_core(weight):
        kept = lax.dynamic_slice_in_dim(weight, core * half, half, 1)
        given = swap(lax.dynamic_slice_in_dim(weight, (1 - core) * half, half, 1))
        return jnp.where(core == 0, jnp.concatenate([kept, given], 0), jnp.concatenate([given, kept], 0))

    block_rows = 2 * rows

    bias_near = lax.ppermute(expand_bias, "ylo", [(0, 1), (1, 0)])
    a, b, bias_near = lax.optimization_barrier((by_core(expand_weight), by_core(shrink_weight), bias_near))

    near = lax.all_gather(jnp.stack([inputs, upstream])[None], "z", axis=0, tiled=True)

    (a_left, a_right), (b_left, b_right) = both_ways(a, a, "x"), both_ways(b, b, "y")
    a_low, a_high = both_ways(a_left[:rows], a_right[rows:], "x")
    b_low, b_high = both_ways(b_left[:rows], b_right[rows:], "y")
    a = jnp.concatenate([a, a_right, a_low, a_high, a_left], 0)
    b = jnp.concatenate([b, b_right, b_low, b_high, b_left], 0)
    (a_left, a_right), (b_left, b_right) = both_ways(a, a, "y"), both_ways(b, b, "x")
    halves = a_left[: 2 * block_rows], a_right[2 * block_rows :], b_left[: 2 * block_rows], b_right[2 * block_rows :]
    a_low, a_high = both_ways(*halves[:2], "y")
    b_low, b_high = both_ways(*halves[2:], "x")
    weight_shape = [((width, 2 * half), bf16)]
    (expand_all,) = call(functools.partial(assemble_kernel, "x"), weight_shape, (a, a_right, a_low, a_high, a_left))
    (shrink_all,) = call(functools.partial(assemble_kernel, "y"), weight_shape, (b, b_right, b_low, b_high, b_left))
    bias_both = jnp.where(ylo == 0, jnp.stack([expand_bias, bias_near]), jnp.stack([bias_near, expand_bias]))
    bias_own = lax.dynamic_slice_in_dim(bias_both, core * half, half, 1).reshape(1, 2 * half)

    near = after(near, a_low, a_high, b_low, b_high)
    other = swap(near)
    many = 8 * tokens
    tall, wide = ((width, many), bf16), ((many, 2 * half), bf16)
    column, own_normed_shape = ((4 * tokens, 1), f32), ((4 * tokens, width), bf16)
    gain, shift_by = norm_gain[None], norm_shift[None]

    def normalise(which, part, *so_far):
        return call(
            functools.partial(norm_kernel, which),
            [own_normed_shape, column, column, tall, tall],
            (part, gain, shift_by, *so_far),
            scratch=[pltpu.VMEM((width, 4 * tokens), bf16)],
            aliases={3: 3, 4: 4} if so_far else None,
        )

    def project(which, part, normed, *so_far):
        tiles = pltpu.VMEM((2, 4 * tokens, 256), f32)
        return call(
            functools.partial(hidden_kernel, which),
            [((1, 2 * half), f32), wide, wide],
            (part, normed, expand_all, shrink_all, bias_own, *so_far),
            scratch=[tiles, tiles],
            aliases={5: 1, 6: 2} if so_far else None,
        )

    normed, near_centre, near_scale, *turned = normalise(0, near)
    near_bias, *hidden_parts = project(0, near, normed)
    normed, other_centre, other_scale, normed_t, up_t = normalise(1, other, *turned)
    other_bias, active, back = project(1, other, normed, *hidden_parts)
    bias_part = near_bias + other_bias

    mine, others, norm_sums = call(
        rows_kernel,
        [((4 * tokens, width), f32), ((4 * tokens, width), bf16), ((2, width), f32)],
        (near, other, near_centre, other_centre, near_scale, other_scale, back, expand_all),
    )

    short, long = ((block_rows, 2 * half), bf16), ((2 * block_rows + 32, half), bf16)
    s_low, s_high, e_low, e_high, vector = call(
        far_kernel,
        [short, short, long, long, ((16, half), f32)],
        (up_t, active, normed_t, back, norm_sums, bias_part),
    )
    (s_low, s_high), (e_low, e_high), sent = both_ways(s_low, s_high, "x"), both_ways(e_low, e_high, "y"), s_low
    s_wide, e_wide = (2 * block_rows, 2 * half), (4 * block_rows, half)
    s_own, e_own, s_terms, e_terms = call(
        near_kernel,
        [(s_wide, f32), (e_wide, f32), ((2, *s_wide), f32), ((2, *e_wide), f32)],
        (up_t, active, normed_t, after(back, sent)),
    )
    s_ahead, s_behind, e_ahead, e_behind = call(
        pass_kernel,
        [(s_wide, bf16), (s_wide, bf16), ((4 * block_rows + 32, half), bf16), (e_wide, bf16)],
        (s_terms, e_terms, s_low, s_high, e_low, e_high),
    )
    (s_prev, s_next), (e_prev, e_next) = both_ways(s_ahead, s_behind, "x"), both_ways(e_ahead, e_behind, "y")

    both = after(mine, s_own) + swap(after(others, sent)).astype(f32)
    grad_normed = lax.psum_scatter(both.astype(bf16), "z", scatter_dimension=0, tiled=True).astype(f32)

    s_sum = s_own + s_prev.astype(f32) + s_next.astype(f32)
    e_sum = e_own + e_prev[: 4 * block_rows].astype(f32) + e_next.astype(f32)
    v_prev, v_next, v_far = (
        from_parts(part) for part in (e_low[2 * block_rows :], e_high[2 * block_rows :], e_prev[4 * block_rows :])
    )
    vector = (vector + v_far) + (v_prev + v_next)

    def shrink_block(far):
        py = (y + far) % 4
        return lax.dynamic_slice(s_sum, (py // 2 * block_rows, py % 2 * half), (block_rows, half))

    def expand_block(far):
        return lax.dynamic_slice_in_dim(e_sum, (x + far) % 4 * block_rows, block_rows, 0)

    def by_rows(block):
        kept = lax.dynamic_slice_in_dim(block, core * rows, rows, 0)
        got = swap(lax.dynamic_slice_in_dim(block, (1 - core) * rows, rows, 0))
        return jnp.where(core == 0, jnp.concatenate([kept, got], 1), jnp.concatenate([got, kept], 1))

    expand_own, vector = direct_scatter(expand_block, "x", vector)
    shrink_own, _ = direct_scatter(shrink_block, "y")
    norm_sums = ring_sum(vector[:8], "z")
    norm_sums = norm_sums + swap(norm_sums)
    gain_grad, shift_grad = (norm_sums[i : i + 4].reshape(-1)[:width] for i in (0, 4))
    bias_mine = lax.dynamic_index_in_dim(vector, 8 + ylo, 0, keepdims=False)
    bias_other = swap(bias_mine)
    bias_grad = jnp.where(
        core == 0, jnp.concatenate([bias_mine, bias_other]), jnp.concatenate([bias_other, bias_mine])
    )
    shrink_grad, expand_grad = by_rows(shrink_own), by_rows(expand_own)

    features = inputs.astype(f32)
    own_centre = jnp.mean(features, axis=1, keepdims=True)
    shifted = features - own_centre
    own_scale = lax.rsqrt(jnp.mean(shifted * shifted, axis=1, keepdims=True) + EPSILON)
    own_normed = shifted * own_scale
    weighted = grad_normed * norm_gain
    mean_one = jnp.sum(weighted, axis=1, keepdims=True) / width
    mean_two = jnp.sum(weighted * own_normed, axis=1, keepdims=True) / width
    result = own_scale * (weighted - mean_one - own_normed * mean_two)
    inputs_grad = (upstream.astype(f32) + result).astype(bf16)
    return inputs_grad, gain_grad, shift_grad, expand_grad, bias_grad, shrink_grad


def solution(mesh):
    fine = Mesh(mesh.devices.reshape(4, 2, 4, 2, 2), AXES)
    by_token = P(AXES, None)
    by_weight = P(("x", "yhi", "core"), ("ylo", "z"))
    by_hidden = P(("ylo", "z"))
    return jax.shard_map(
        local,
        mesh=fine,
        in_specs=(by_token, by_token, P(), P(), by_weight, by_hidden, by_weight),
        out_specs=(by_token, P(), P(), by_weight, by_hidden, by_weight),
        check_vma=False,
    )
```

profile of v0, /device:TPU:1, one launch (start us, length us, event | category | flops | bytes accessed | tf_op | source)
XLA Modules:
  0.0 202.9 jit_solution(7755854561036970942)
XLA Ops:
  7.2 2.4 %pad_maximum_fusion = bf16[2,160,1664]{2,1,0:T(8,128)(2,1)} fusion(bf16[1,160,1664]{2,1,0:T(8,128)(2,1)} %bitcast.25, bf16[1,160,1664]{2,1,0:T(8,128)(2,1)} %bitcast.24), kind=kLoop, calls=%fused_computation.15 | loop fusion | flops 532480 | bytes 2129920 | tf_op jit(solution)/shard_map/stack | solution.py:308
  9.8 1.5 collective-permute-start
  11.4 1.4 collective-permute-start.2
  13.0 1.0 collective-permute-done.2
  13.9 2.6 %collective-permute-start.3 = (bf16[208,512]{1,0:T(8,128)(2,1)S(1)}, bf16[208,512]{1,0:T(8,128)(2,1)S(1)}, u32[]{:S(2)}, u32[]{:S(2)}) collective-permute-start(bf16[208,512]{1,0:T(8,128)(2,1)S(1)} %maximum_select_fusion.2), channel_id=1, source_target_pairs={{0,96},{32,0},{64,32},{96,64},{1,97},{33,1},{65,33},{97,65},{2,98}... | collective-permute-start | bytes 638984 | tf_op jit(solution)/shard_map/ppermute | solution.py:27
  16.5 2.7 %collective-permute-start.11 = (bf16[208,512]{1,0:T(8,128)(2,1)S(1)}, bf16[208,512]{1,0:T(8,128)(2,1)S(1)}, u32[]{:S(2)}, u32[]{:S(2)}) collective-permute-start(bf16[208,512]{1,0:T(8,128)(2,1)S(1)} %maximum_select_fusion.3), channel_id=1, source_target_pairs={{0,18},{16,0},{2,16},{18,2},{1,19},{17,1},{3,17},{19,3},{4,22},{20... | collective-permute-start | bytes 638984 | tf_op jit(solution)/shard_map/ppermute | solution.py:26
  19.3 3.1 %collective-permute-done.4 = bf16[208,512]{1,0:T(8,128)(2,1)S(1)} collective-permute-done((bf16[208,512]{1,0:T(8,128)(2,1)S(1)}, bf16[208,512]{1,0:T(8,128)(2,1)S(1)}, u32[]{:S(2)}, u32[]{:S(2)}) %collective-permute-start.4) | collective-permute-done | bytes 213024 | tf_op jit(solution)/shard_map/ppermute | solution.py:27
  22.5 2.7 %collective-permute-start.6 = (bf16[104,512]{1,0:T(8,128)(2,1)S(1)}, bf16[104,512]{1,0:T(8,128)(2,1)S(1)}, u32[]{:S(2)}, u32[]{:S(2)}) collective-permute-start(bf16[104,512]{1,0:T(8,128)(2,1)S(1)} %slice.143), channel_id=1, source_target_pairs={{0,96},{32,0},{64,32},{96,64},{1,97},{33,1},{65,33},{97,65},{2,98}... | collective-permute-start | bytes 319496 | tf_op jit(solution)/shard_map/ppermute | solution.py:27
  25.3 1.4 collective-permute-start.13
  26.6 1.5 collective-permute-start.14
  28.7 2.4 %collective-permute-start.9 = (bf16[832,512]{1,0:T(8,128)(2,1)S(1)}, bf16[832,512]{1,0:T(8,128)(2,1)S(1)}, u32[]{:S(2)}, u32[]{:S(2)}) collective-permute-start(bf16[832,512]{1,0:T(8,128)(2,1)S(1)} %constant_dynamic-update-slice_fusion.own), channel_id=1, source_target_pairs={{0,18},{16,0},{2,16},{18,2},{1,19},{17,1},{3,17},{19,3},{4,22},{20... | collective-permute-start | bytes 2555912 | tf_op jit(solution)/shard_map/ppermute | solution.py:26
  31.2 2.7 %collective-permute-start.17 = (bf16[832,512]{1,0:T(8,128)(2,1)S(1)}, bf16[832,512]{1,0:T(8,128)(2,1)S(1)}, u32[]{:S(2)}, u32[]{:S(2)}) collective-permute-start(bf16[832,512]{1,0:T(8,128)(2,1)S(1)} %constant_dynamic-update-slice_fusion.5.own), channel_id=1, source_target_pairs={{0,96},{32,0},{64,32},{96,64},{1,97},{33,1},{65,33},{97,65},{2,98}... | collective-permute-start | bytes 2555912 | tf_op jit(solution)/shard_map/ppermute | solution.py:27
  33.9 14.5 %collective-permute-done.7.left = bf16[832,512]{1,0:T(8,128)(2,1)S(1)} collective-permute-done((bf16[832,512]{1,0:T(8,128)(2,1)S(1)}, bf16[832,512]{1,0:T(8,128)(2,1)S(1)}, u32[]{:S(2)}, u32[]{:S(2)}) %collective-permute-start.7) | collective-permute-done | bytes 852000 | tf_op jit(solution)/shard_map/ppermute | solution.py:26
  48.6 2.7 %collective-permute-start.10 = (bf16[416,512]{1,0:T(8,128)(2,1)S(1)}, bf16[416,512]{1,0:T(8,128)(2,1)S(1)}, u32[]{:S(2)}, u32[]{:S(2)}) collective-permute-start(bf16[416,512]{1,0:T(8,128)(2,1)S(1)} %slice.145), channel_id=1, source_target_pairs={{0,18},{16,0},{2,16},{18,2},{1,19},{17,1},{3,17},{19,3},{4,22},{20... | collective-permute-start | bytes 1277960 | tf_op jit(solution)/shard_map/ppermute | solution.py:26
  51.5 2.7 %collective-permute-start.18 = (bf16[416,512]{1,0:T(8,128)(2,1)S(1)}, bf16[416,512]{1,0:T(8,128)(2,1)S(1)}, u32[]{:S(2)}, u32[]{:S(2)}) collective-permute-start(bf16[416,512]{1,0:T(8,128)(2,1)S(1)} %slice.149), channel_id=1, source_target_pairs={{0,96},{32,0},{64,32},{96,64},{1,97},{33,1},{65,33},{97,65},{2,98}... | collective-permute-start | bytes 1277960 | tf_op jit(solution)/shard_map/ppermute | solution.py:27
  54.2 3.2 %collective-permute-done.8.far_low = bf16[416,512]{1,0:T(8,128)(2,1)S(1)} collective-permute-done((bf16[416,512]{1,0:T(8,128)(2,1)S(1)}, bf16[416,512]{1,0:T(8,128)(2,1)S(1)}, u32[]{:S(2)}, u32[]{:S(2)}) %collective-permute-start.8) | collective-permute-done | bytes 426016 | tf_op jit(solution)/shard_map/ppermute | solution.py:26
  57.4 0.8 copy-done.7
  58.2 0.8 copy-done.9
  58.9 1.0 collective-permute-done.16.far_low
  60.0 0.8 copy-done.11
  60.7 0.8 copy-done.13
  62.1 4.4 %collective-permute-start.19 = (bf16[4,2,160,1664]{3,2,1,0:T(8,128)(2,1)}, bf16[4,2,160,1664]{3,2,1,0:T(8,128)(2,1)}, u32[]{:S(2)}, u32[]{:S(2)}) collective-permute-start(bf16[4,2,160,1664]{3,2,1,0:T(8,128)(2,1)} %bitcast.18), channel_id=1, source_target_pairs={{0,1},{1,0},{2,3},{3,2},{4,5},{5,4},{6,7},{7,6},{8,9},{9,8},{10,11... | collective-permute-start | bytes 12779528 | tf_op jit(solution)/shard_map/ppermute | solution.py:31
  66.7 1.1 copy-done.4
  67.8 1.0 copy-done.8
  68.8 1.0 copy-done.10
  70.1 0.9 copy-done.2
  71.5 1.9 copy-done
  73.4 3.6 %shard_map.118 = (bf16[640,1664]{1,0:T(8,128)(2,1)S(1)}, f32[640,1]{1,0:T(8,128)S(1)}, f32[640,1]{1,0:T(8,128)S(1)}, bf16[1664,1280]{1,0:T(8,128)(2,1)S(1)}, bf16[1664,1280]{1,0:T(8,128)(2,1)S(1)}) custom-call(bf16[4,2,160,1664]{3,2,1,0:T(8,128)(2,1)S(1)} %bitcast.19, f32[1,1664]{1,0:T(1,128)S(1)} %broadcast_in_dim.7.gain, ...), custom_call_target="tpu_custom_call" | custom-call | flops 1000000 | bytes 1000000 | tf_op jit(solution)/shard_map/pallas_call | solution.py:98
  77.1 7.1 %shard_map.122 = (f32[1,1024]{1,0:T(1,128)S(1)}, bf16[1280,1024]{1,0:T(8,128)(2,1)S(1)}, bf16[1280,1024]{1,0:T(8,128)(2,1)S(1)}) custom-call(bf16[4,2,160,1664]{3,2,1,0:T(8,128)(2,1)S(1)} %bitcast.20, bf16[640,1664]{1,0:T(8,128)(2,1)S(1)} %get-tuple-element.56.normed, bf16[1664,1024]{1,0:T(8,128)(2,1)S(1)} %shard_map.120.expand, ...), custom_call_target="tpu_custom_call" | custom-call | flops 1000000 | bytes 1000000 | tf_op jit(solution)/shard_map/pallas_call | solution.py:98
  84.3 5.9 %shard_map.119 = (bf16[640,1664]{1,0:T(8,128)(2,1)S(1)}, f32[640,1]{1,0:T(8,128)S(1)}, f32[640,1]{1,0:T(8,128)S(1)}, bf16[1664,1280]{1,0:T(8,128)(2,1)S(1)}, bf16[1664,1280]{1,0:T(8,128)(2,1)S(1)}) custom-call(bf16[4,2,160,1664]{3,2,1,0:T(8,128)(2,1)} %collective-permute-done.19.part.other, ...), custom_call_target="tpu_custom_call", output_to_operand_aliasing={{3}: (3, {}), {4}: (4, {})} | custom-call | flops 1000000 | bytes 1000000 | tf_op jit(solution)/shard_map/pallas_call | solution.py:98
  90.1 9.3 %shard_map.123 = (f32[1,1024]{1,0:T(1,128)S(1)}, bf16[1280,1024]{1,0:T(8,128)(2,1)S(1)}, bf16[1280,1024]{1,0:T(8,128)(2,1)S(1)}) custom-call(bf16[4,2,160,1664]{3,2,1,0:T(8,128)(2,1)} %collective-permute-done.19.part.other, bf16[640,1664]{1,0:T(8,128)(2,1)S(1)} %get-tuple-element.54.normed, ...), custom_call_target="tpu_custom_call", output_to_operand_aliasing={{1}: (5, {}), {2}: (6, {})} | custom-call | flops 1000000 | bytes 1000000 | tf_op jit(solution)/shard_map/pallas_call | solution.py:98
  99.5 8.9 %shard_map.124 = (f32[640,1664]{1,0:T(8,128)S(1)}, bf16[640,1664]{1,0:T(8,128)(2,1)S(1)}, f32[2,1664]{1,0:T(2,128)S(1)}) custom-call(bf16[4,2,160,1664]{3,2,1,0:T(8,128)(2,1)S(1)} %bitcast.21, bf16[4,2,160,1664]{3,2,1,0:T(8,128)(2,1)} %collective-permute-done.19.part.other, f32[640,1]{1,0:T(8,128)S(1)} %get-tuple-element.48.near_centre, ...), custom_call_target="tpu_custom_call" | custom-call | flops 1000000 | bytes 1000000 | tf_op jit(solution)/shard_map/pallas_call | solution.py:98
  108.4 3.3 %shard_map.125 = (bf16[208,1024]{1,0:T(8,128)(2,1)S(1)}, bf16[208,1024]{1,0:T(8,128)(2,1)S(1)}, bf16[448,512]{1,0:T(8,128)(2,1)S(1)}, bf16[448,512]{1,0:T(8,128)(2,1)S(1)}, f32[16,512]{1,0:T(8,128)S(1)}) custom-call(bf16[1664,1280]{1,0:T(8,128)(2,1)S(1)} %get-tuple-element.61.up_t, bf16[1280,1024]{1,0:T(8,128)(2,1)S(1)} %get-tuple-element.62.active, ...), custom_call_target="tpu_custom_call" | custom-call | flops 1000000 | bytes 1000000 | tf_op jit(solution)/shard_map/pallas_call | solution.py:98
  111.8 0.8 collective-permute-start.24
  112.6 0.7 collective-permute-start.23
  113.3 2.7 %collective-permute-start.22 = (bf16[208,1024]{1,0:T(8,128)(2,1)S(1)}, bf16[208,1024]{1,0:T(8,128)(2,1)S(1)}, u32[]{:S(2)}, u32[]{:S(2)}) collective-permute-start(bf16[208,1024]{1,0:T(8,128)(2,1)S(1)} %get-tuple-element.76), channel_id=1, source_target_pairs={{0,96},{32,0},{64,32},{96,64},{1,97},{33,1},{65,33},{97,65},{2,98}... | collective-permute-start | bytes 1277960 | tf_op jit(solution)/shard_map/ppermute | solution.py:27
  116.0 9.9 %shard_map.126 = (f32[416,1024]{1,0:T(8,128)S(1)}, f32[832,512]{1,0:T(8,128)S(1)}, f32[2,416,1024]{2,1,0:T(8,128)S(1)}, f32[2,832,512]{2,1,0:T(8,128)S(1)}) custom-call(bf16[1664,1280]{1,0:T(8,128)(2,1)S(1)} %get-tuple-element.61.up_t, bf16[1280,1024]{1,0:T(8,128)(2,1)S(1)} %get-tuple-element.62.active, bf16[1664,1280]{1,0:T(8,128)(2,1)S(1)} %get-tuple-element.63.normed_t, ...), custom_call_target="tpu_custom_call" | custom-call | flops 1000000 | bytes 1000000 | tf_op jit(solution)/shard_map/pallas_call | solution.py:98
  126.0 1.9 shard_map.127
  127.9 0.9 copy-done.15
  128.8 1.5 collective-permute-start.37
  130.3 1.7 add_convert_fusion
  132.0 1.2 convert_reduce_fusion
  133.6 1.3 fusion.9
  134.9 2.5 %collective-permute-start.26 = (bf16[832,512]{1,0:T(8,128)(2,1)}, bf16[832,512]{1,0:T(8,128)(2,1)S(1)}, u32[]{:S(2)}, u32[]{:S(2)}) collective-permute-start(bf16[832,512]{1,0:T(8,128)(2,1)} %copy-done.16), channel_id=1, source_target_pairs={{0,18},{16,0},{2,16},{18,2},{1,19},{17,1},{3,17},{19,3},{4,22},{20... | collective-permute-start | bytes 2555912 | tf_op jit(solution)/shard_map/ppermute | solution.py:26
  137.4 10.6 %collective-permute-done.37 = bf16[416,1024]{1,0:T(8,128)(2,1)} collective-permute-done((bf16[416,1024]{1,0:T(8,128)(2,1)}, bf16[416,1024]{1,0:T(8,128)(2,1)}, u32[]{:S(2)}, u32[]{:S(2)}) %collective-permute-start.37) | collective-permute-done | bytes 852000 | tf_op jit(solution)/shard_map/ppermute | solution.py:27
  148.0 2.0 collective-permute-done.36
  150.0 1.8 convert_add_fusion
  151.9 0.9 collective-permute-start.40
  152.8 1.7 collective-permute-start.39
  154.5 0.8 reduce-precision_convert_fusion
  155.4 1.5 convert_add_fusion.1
  157.1 1.6 collective-permute-start.29
  158.9 1.7 collective-permute-start.27
  160.6 3.3 %collective-permute-done.39 = bf16[208,512]{1,0:T(8,128)(2,1)S(1)} collective-permute-done((bf16[208,512]{1,0:T(8,128)(2,1)S(1)}, bf16[208,512]{1,0:T(8,128)(2,1)S(1)}, u32[]{:S(2)}, u32[]{:S(2)}) %collective-permute-start.39) | collective-permute-done | bytes 213024 | tf_op jit(solution)/shard_map/ppermute | solution.py:26
  164.1 6.1 %collective-permute-start.41 = (f32[104,512]{1,0:T(8,128)S(1)}, f32[104,512]{1,0:T(8,128)S(1)}, u32[]{:S(2)}, u32[]{:S(2)}) collective-permute-start(f32[104,512]{1,0:T(8,128)S(1)} %get-tuple-element.95), channel_id=1, source_target_pairs={{0,1},{1,0},{2,3},{3,2},{4,5},{5,4},{6,7},{7,6},{8,9},{9,8},{10,11... | collective-permute-start | bytes 638984 | tf_op jit(solution)/shard_map/ppermute | solution.py:31
  170.3 1.6 collective-permute-start.31
  171.9 2.9 %collective-permute-start.32 = (f32[8,512]{1,0:T(8,128)S(1)}, f32[8,512]{1,0:T(8,128)S(1)}, u32[]{:S(2)}, u32[]{:S(2)}) collective-permute-start(f32[8,512]{1,0:T(8,128)S(1)} %slice.163), channel_id=1, source_target_pairs={{0,12},{4,0},{8,4},{12,8},{1,13},{5,1},{9,5},{13,9},{2,14},{6,2},{... | collective-permute-start | bytes 49160 | tf_op jit(solution)/shard_map/ppermute | solution.py:27
  174.8 1.1 collective-permute-start.30
  176.1 8.9 %collective-permute-start.34 = (f32[104,512]{1,0:T(8,128)S(1)}, f32[104,512]{1,0:T(8,128)S(1)}, u32[]{:S(2)}, u32[]{:S(2)}) collective-permute-start(f32[104,512]{1,0:T(8,128)S(1)} %get-tuple-element.97), channel_id=1, source_target_pairs={{0,1},{1,0},{2,3},{3,2},{4,5},{5,4},{6,7},{7,6},{8,9},{9,8},{10,11... | collective-permute-start | bytes 638984 | tf_op jit(solution)/shard_map/ppermute | solution.py:31
  185.1 3.5 %collective-permute-start.33 = (f32[8,512]{1,0:T(8,128)S(1)}, f32[8,512]{1,0:T(8,128)S(1)}, u32[]{:S(2)}, u32[]{:S(2)}) collective-permute-start(f32[8,512]{1,0:T(8,128)S(1)} %add_add_fusion.2), channel_id=1, source_target_pairs={{0,1},{1,0},{2,3},{3,2},{4,5},{5,4},{6,7},{7,6},{8,9},{9,8},{10,11... | collective-permute-start | bytes 49160 | tf_op jit(solution)/shard_map/ppermute | solution.py:31
  190.7 0.8 maximum_select_fusion.1
  191.5 0.8 maximum_select_fusion
  192.3 1.4 fusion.10
  193.7 2.4 %fusion.8 = bf16[160,1664]{1,0:T(8,128)(2,1)} fusion(bf16[160,1664]{1,0:T(8,128)(2,1)S(1)} %copy-done.17, bf16[160,1664]{1,0:T(8,128)(2,1)} %reduce-scatter.2.cloned.1.call-done, bf16[160,1664]{1,0:T(8,128)(2,1)S(1)} %copy-done.18, f32[160]{0:T(256)S(1)} %get-tuple-element.107, f32[160]{0:T(256)S(1)} %get-tuple-element.108, f32[1664]{0:T(1024)S(1)} %copy-done.21, ...), kind=kLoop, calls=%fused_computation.13 | loop fusion | flops 3194880 | bytes 2139136 | tf_op jit(solution)/shard_map/convert_element_type | solution.py:426
  (142 shorter events, 6.2 us)
Async XLA Ops:
  7.2 2.6 %copy-start.19 = (bf16[104,1024]{1,0:T(8,128)(2,1)S(1)}, bf16[104,1024]{1,0:T(8,128)(2,1)}, u32[]{:S(2)}) copy-start(bf16[104,1024]{1,0:T(8,128)(2,1)} %param.11) | copy-start | bytes 638980
  7.2 54.9 %all-gather.3.cloned.1.call-start = ((), (), s32[]{:S(2)}) async-start(), calls=%async_computation.2 | async-start | bytes 5324800 | tf_op jit(solution)/shard_map/all_gather | solution.py:308
  7.2 4.1 %copy-start.20 = (bf16[104,1024]{1,0:T(8,128)(2,1)S(1)}, bf16[104,1024]{1,0:T(8,128)(2,1)}, u32[]{:S(2)}) copy-start(bf16[104,1024]{1,0:T(8,128)(2,1)} %param.13) | copy-start | bytes 638980
  7.2 4.2 %copy-start.23 = (f32[1024]{0:T(1024)S(1)}, f32[1024]{0:T(1024)}, u32[]{:S(2)}) copy-start(f32[1024]{0:T(1024)} %param.12) | copy-start | bytes 12292
  9.7 182.6 %reduce-scatter.2.cloned.1.call-start = ((), (), s32[]{:S(2)}) async-start(), calls=%async_computation.1 | async-start | bytes 2662400 | tf_op jit(solution)/shard_map/reduce_scatter | solution.py:384
  9.8 3.1 %collective-permute-start = (bf16[104,512]{1,0:T(8,128)(2,1)S(1)}, bf16[104,512]{1,0:T(8,128)(2,1)S(1)}, u32[]{:S(2)}, u32[]{:S(2)}) collective-permute-start(bf16[104,512]{1,0:T(8,128)(2,1)S(1)} %get-tuple-element.101), channel_id=1, source_target_pairs={{0,1},{1,0},{2,3},{3,2},{4,5},{5,4},{6,7},{7,6},{8,9},{9,8},{10,11... | collective-permute-start | bytes 319496 | tf_op jit(solution)/shard_map/ppermute | solution.py:31
  11.3 1.6 collective-permute-start.1
  11.4 2.5 %collective-permute-start.2 = (f32[1024]{0:T(1024)S(1)}, f32[1024]{0:T(1024)S(1)}, u32[]{:S(2)}, u32[]{:S(2)}) collective-permute-start(f32[1024]{0:T(1024)S(1)} %copy-done.23), channel_id=1, source_target_pairs={{0,16},{16,0},{1,17},{17,1},{2,18},{18,2},{3,19},{19,3},{4,20},{20... | collective-permute-start | bytes 12296 | tf_op jit(solution)/shard_map/ppermute | solution.py:305
  13.9 8.6 %collective-permute-start.3 = (bf16[208,512]{1,0:T(8,128)(2,1)S(1)}, bf16[208,512]{1,0:T(8,128)(2,1)S(1)}, u32[]{:S(2)}, u32[]{:S(2)}) collective-permute-start(bf16[208,512]{1,0:T(8,128)(2,1)S(1)} %maximum_select_fusion.2), channel_id=1, source_target_pairs={{0,96},{32,0},{64,32},{96,64},{1,97},{33,1},{65,33},{97,65},{2,98}... | collective-permute-start | bytes 638984 | tf_op jit(solution)/shard_map/ppermute | solution.py:27
  16.5 5.9 %collective-permute-start.4 = (bf16[208,512]{1,0:T(8,128)(2,1)S(1)}, bf16[208,512]{1,0:T(8,128)(2,1)S(1)}, u32[]{:S(2)}, u32[]{:S(2)}) collective-permute-start(bf16[208,512]{1,0:T(8,128)(2,1)S(1)} %maximum_select_fusion.2), channel_id=1, source_target_pairs={{0,32},{32,64},{64,96},{96,0},{1,33},{33,65},{65,97},{97,1},{2,34}... | collective-permute-start | bytes 638984 | tf_op jit(solution)/shard_map/ppermute | solution.py:27
  16.5 10.1 %collective-permute-start.11 = (bf16[208,512]{1,0:T(8,128)(2,1)S(1)}, bf16[208,512]{1,0:T(8,128)(2,1)S(1)}, u32[]{:S(2)}, u32[]{:S(2)}) collective-permute-start(bf16[208,512]{1,0:T(8,128)(2,1)S(1)} %maximum_select_fusion.3), channel_id=1, source_target_pairs={{0,18},{16,0},{2,16},{18,2},{1,19},{17,1},{3,17},{19,3},{4,22},{20... | collective-permute-start | bytes 638984 | tf_op jit(solution)/shard_map/ppermute | solution.py:26
  19.2 6.0 %collective-permute-start.12 = (bf16[208,512]{1,0:T(8,128)(2,1)S(1)}, bf16[208,512]{1,0:T(8,128)(2,1)S(1)}, u32[]{:S(2)}, u32[]{:S(2)}) collective-permute-start(bf16[208,512]{1,0:T(8,128)(2,1)S(1)} %maximum_select_fusion.3), channel_id=1, source_target_pairs={{0,16},{16,2},{2,18},{18,0},{1,17},{17,3},{3,19},{19,1},{4,20},{20... | collective-permute-start | bytes 638984 | tf_op jit(solution)/shard_map/ppermute | solution.py:26
  22.4 5.8 %collective-permute-start.5 = (bf16[104,512]{1,0:T(8,128)(2,1)S(1)}, bf16[104,512]{1,0:T(8,128)(2,1)S(1)}, u32[]{:S(2)}, u32[]{:S(2)}) collective-permute-start(bf16[104,512]{1,0:T(8,128)(2,1)S(1)} %slice.142), channel_id=1, source_target_pairs={{0,32},{32,64},{64,96},{96,0},{1,33},{33,65},{65,97},{97,1},{2,34}... | collective-permute-start | bytes 319496 | tf_op jit(solution)/shard_map/ppermute | solution.py:27
  22.5 5.7 %collective-permute-start.6 = (bf16[104,512]{1,0:T(8,128)(2,1)S(1)}, bf16[104,512]{1,0:T(8,128)(2,1)S(1)}, u32[]{:S(2)}, u32[]{:S(2)}) collective-permute-start(bf16[104,512]{1,0:T(8,128)(2,1)S(1)} %slice.143), channel_id=1, source_target_pairs={{0,96},{32,0},{64,32},{96,64},{1,97},{33,1},{65,33},{97,65},{2,98}... | collective-permute-start | bytes 319496 | tf_op jit(solution)/shard_map/ppermute | solution.py:27
  25.3 5.8 %collective-permute-start.13 = (bf16[104,512]{1,0:T(8,128)(2,1)S(1)}, bf16[104,512]{1,0:T(8,128)(2,1)S(1)}, u32[]{:S(2)}, u32[]{:S(2)}) collective-permute-start(bf16[104,512]{1,0:T(8,128)(2,1)S(1)} %slice.146), channel_id=1, source_target_pairs={{0,16},{16,2},{2,18},{18,0},{1,17},{17,3},{3,19},{19,1},{4,20},{20... | collective-permute-start | bytes 319496 | tf_op jit(solution)/shard_map/ppermute | solution.py:26
  26.6 4.4 %collective-permute-start.14 = (bf16[104,512]{1,0:T(8,128)(2,1)S(1)}, bf16[104,512]{1,0:T(8,128)(2,1)S(1)}, u32[]{:S(2)}, u32[]{:S(2)}) collective-permute-start(bf16[104,512]{1,0:T(8,128)(2,1)S(1)} %slice.147), channel_id=1, source_target_pairs={{0,18},{16,0},{2,16},{18,2},{1,19},{17,1},{3,17},{19,3},{4,22},{20... | collective-permute-start | bytes 319496 | tf_op jit(solution)/shard_map/ppermute | solution.py:26
  28.3 23.0 %copy-start.3 = (bf16[832,512]{1,0:T(8,128)(2,1)}, bf16[832,512]{1,0:T(8,128)(2,1)S(1)}, u32[]{:S(2)}) copy-start(bf16[832,512]{1,0:T(8,128)(2,1)S(1)} %constant_dynamic-update-slice_fusion.own) | copy-start | bytes 2555908
  28.3 20.1 %collective-permute-start.7 = (bf16[832,512]{1,0:T(8,128)(2,1)S(1)}, bf16[832,512]{1,0:T(8,128)(2,1)S(1)}, u32[]{:S(2)}, u32[]{:S(2)}) collective-permute-start(bf16[832,512]{1,0:T(8,128)(2,1)S(1)} %constant_dynamic-update-slice_fusion.own), channel_id=1, source_target_pairs={{0,16},{16,2},{2,18},{18,0},{1,17},{17,3},{3,19},{19,1},{4,20},{20... | collective-permute-start | bytes 2555912 | tf_op jit(solution)/shard_map/ppermute | solution.py:26
  28.7 19.8 %collective-permute-start.9 = (bf16[832,512]{1,0:T(8,128)(2,1)S(1)}, bf16[832,512]{1,0:T(8,128)(2,1)S(1)}, u32[]{:S(2)}, u32[]{:S(2)}) collective-permute-start(bf16[832,512]{1,0:T(8,128)(2,1)S(1)} %constant_dynamic-update-slice_fusion.own), channel_id=1, source_target_pairs={{0,18},{16,0},{2,16},{18,2},{1,19},{17,1},{3,17},{19,3},{4,22},{20... | collective-permute-start | bytes 2555912 | tf_op jit(solution)/shard_map/ppermute | solution.py:26
  31.1 20.3 %copy-start.1 = (bf16[832,512]{1,0:T(8,128)(2,1)}, bf16[832,512]{1,0:T(8,128)(2,1)S(1)}, u32[]{:S(2)}) copy-start(bf16[832,512]{1,0:T(8,128)(2,1)S(1)} %constant_dynamic-update-slice_fusion.5.own) | copy-start | bytes 2555908
  31.1 35.4 %copy-start.21 = (f32[1664]{0:T(1024)S(1)}, f32[1664]{0:T(1024)}, u32[]{:S(2)}) copy-start(f32[1664]{0:T(1024)} %param.9) | copy-start | bytes 19972
  31.1 35.4 %copy-start.22 = (f32[1664]{0:T(1024)S(1)}, f32[1664]{0:T(1024)}, u32[]{:S(2)}) copy-start(f32[1664]{0:T(1024)} %param.10) | copy-start | bytes 19972
  31.2 20.1 %collective-permute-start.15 = (bf16[832,512]{1,0:T(8,128)(2,1)S(1)}, bf16[832,512]{1,0:T(8,128)(2,1)S(1)}, u32[]{:S(2)}, u32[]{:S(2)}) collective-permute-start(bf16[832,512]{1,0:T(8,128)(2,1)S(1)} %constant_dynamic-update-slice_fusion.5.own), channel_id=1, source_target_pairs={{0,32},{32,64},{64,96},{96,0},{1,33},{33,65},{65,97},{97,1},{2,34}... | collective-permute-start | bytes 2555912 | tf_op jit(solution)/shard_map/ppermute | solution.py:27
  31.2 20.2 %collective-permute-start.17 = (bf16[832,512]{1,0:T(8,128)(2,1)S(1)}, bf16[832,512]{1,0:T(8,128)(2,1)S(1)}, u32[]{:S(2)}, u32[]{:S(2)}) collective-permute-start(bf16[832,512]{1,0:T(8,128)(2,1)S(1)} %constant_dynamic-update-slice_fusion.5.own), channel_id=1, source_target_pairs={{0,96},{32,0},{64,32},{96,64},{1,97},{33,1},{65,33},{97,65},{2,98}... | collective-permute-start | bytes 2555912 | tf_op jit(solution)/shard_map/ppermute | solution.py:27
  48.4 9.0 %collective-permute-start.8 = (bf16[416,512]{1,0:T(8,128)(2,1)S(1)}, bf16[416,512]{1,0:T(8,128)(2,1)S(1)}, u32[]{:S(2)}, u32[]{:S(2)}) collective-permute-start(bf16[416,512]{1,0:T(8,128)(2,1)S(1)} %slice.144), channel_id=1, source_target_pairs={{0,16},{16,2},{2,18},{18,0},{1,17},{17,3},{3,19},{19,1},{4,20},{20... | collective-permute-start | bytes 1277960 | tf_op jit(solution)/shard_map/ppermute | solution.py:26
  48.6 9.6 %collective-permute-start.10 = (bf16[416,512]{1,0:T(8,128)(2,1)S(1)}, bf16[416,512]{1,0:T(8,128)(2,1)S(1)}, u32[]{:S(2)}, u32[]{:S(2)}) collective-permute-start(bf16[416,512]{1,0:T(8,128)(2,1)S(1)} %slice.145), channel_id=1, source_target_pairs={{0,18},{16,0},{2,16},{18,2},{1,19},{17,1},{3,17},{19,3},{4,22},{20... | collective-permute-start | bytes 1277960 | tf_op jit(solution)/shard_map/ppermute | solution.py:26
  51.3 8.7 %collective-permute-start.16 = (bf16[416,512]{1,0:T(8,128)(2,1)S(1)}, bf16[416,512]{1,0:T(8,128)(2,1)S(1)}, u32[]{:S(2)}, u32[]{:S(2)}) collective-permute-start(bf16[416,512]{1,0:T(8,128)(2,1)S(1)} %slice.148), channel_id=1, source_target_pairs={{0,32},{32,64},{64,96},{96,0},{1,33},{33,65},{65,97},{97,1},{2,34}... | collective-permute-start | bytes 1277960 | tf_op jit(solution)/shard_map/ppermute | solution.py:27
  51.5 9.3 %collective-permute-start.18 = (bf16[416,512]{1,0:T(8,128)(2,1)S(1)}, bf16[416,512]{1,0:T(8,128)(2,1)S(1)}, u32[]{:S(2)}, u32[]{:S(2)}) collective-permute-start(bf16[416,512]{1,0:T(8,128)(2,1)S(1)} %slice.149), channel_id=1, source_target_pairs={{0,96},{32,0},{64,32},{96,64},{1,97},{33,1},{65,33},{97,65},{2,98}... | collective-permute-start | bytes 1277960 | tf_op jit(solution)/shard_map/ppermute | solution.py:27
  62.1 22.2 %collective-permute-start.19 = (bf16[4,2,160,1664]{3,2,1,0:T(8,128)(2,1)}, bf16[4,2,160,1664]{3,2,1,0:T(8,128)(2,1)}, u32[]{:S(2)}, u32[]{:S(2)}) collective-permute-start(bf16[4,2,160,1664]{3,2,1,0:T(8,128)(2,1)} %bitcast.18), channel_id=1, source_target_pairs={{0,1},{1,0},{2,3},{3,2},{4,5},{5,4},{6,7},{7,6},{8,9},{9,8},{10,11... | collective-permute-start | bytes 12779528 | tf_op jit(solution)/shard_map/ppermute | solution.py:31
  66.7 1.2 copy-start.4
  67.8 1.0 copy-start.8
  68.8 1.0 copy-start.10
  69.8 1.2 copy-start.2
  69.8 1.3 copy-start.12
  69.8 1.4 copy-start.14
  71.2 2.2 %copy-start = (bf16[8,160,1664]{2,1,0:T(8,128)(2,1)S(1)}, bf16[8,160,1664]{2,1,0:T(8,128)(2,1)}, u32[]{:S(2)}) copy-start(bf16[8,160,1664]{2,1,0:T(8,128)(2,1)} %all-gather.3.cloned.1.call-done) | copy-start | bytes 12779524
  111.7 18.6 %collective-permute-start.20 = (bf16[640,1664]{1,0:T(8,128)(2,1)S(1)}, bf16[640,1664]{1,0:T(8,128)(2,1)S(1)}, u32[]{:S(2)}, u32[]{:S(2)}) collective-permute-start(bf16[640,1664]{1,0:T(8,128)(2,1)S(1)} %get-tuple-element.72), channel_id=1, source_target_pairs={{0,1},{1,0},{2,3},{3,2},{4,5},{5,4},{6,7},{7,6},{8,9},{9,8},{10,11... | collective-permute-start | bytes 6389768 | tf_op jit(solution)/shard_map/ppermute | solution.py:31
  111.8 14.2 %collective-permute-start.24 = (bf16[448,512]{1,0:T(8,128)(2,1)S(1)}, bf16[448,512]{1,0:T(8,128)(2,1)S(1)}, u32[]{:S(2)}, u32[]{:S(2)}) collective-permute-start(bf16[448,512]{1,0:T(8,128)(2,1)S(1)} %get-tuple-element.78), channel_id=1, source_target_pairs={{0,18},{16,0},{2,16},{18,2},{1,19},{17,1},{3,17},{19,3},{4,22},{20... | collective-permute-start | bytes 1376264 | tf_op jit(solution)/shard_map/ppermute | solution.py:26
  112.6 13.4 %collective-permute-start.23 = (bf16[448,512]{1,0:T(8,128)(2,1)S(1)}, bf16[448,512]{1,0:T(8,128)(2,1)S(1)}, u32[]{:S(2)}, u32[]{:S(2)}) collective-permute-start(bf16[448,512]{1,0:T(8,128)(2,1)S(1)} %get-tuple-element.77), channel_id=1, source_target_pairs={{0,16},{16,2},{2,18},{18,0},{1,17},{17,3},{3,19},{19,1},{4,20},{20... | collective-permute-start | bytes 1376264 | tf_op jit(solution)/shard_map/ppermute | solution.py:26
  113.3 12.6 %collective-permute-start.21 = (bf16[208,1024]{1,0:T(8,128)(2,1)S(1)}, bf16[208,1024]{1,0:T(8,128)(2,1)S(1)}, u32[]{:S(2)}, u32[]{:S(2)}) collective-permute-start(bf16[208,1024]{1,0:T(8,128)(2,1)S(1)} %get-tuple-element.67), channel_id=1, source_target_pairs={{0,32},{32,64},{64,96},{96,0},{1,33},{33,65},{65,97},{97,1},{2,34}... | collective-permute-start | bytes 1277960 | tf_op jit(solution)/shard_map/ppermute | solution.py:27
  113.3 12.6 %collective-permute-start.22 = (bf16[208,1024]{1,0:T(8,128)(2,1)S(1)}, bf16[208,1024]{1,0:T(8,128)(2,1)S(1)}, u32[]{:S(2)}, u32[]{:S(2)}) collective-permute-start(bf16[208,1024]{1,0:T(8,128)(2,1)S(1)} %get-tuple-element.76), channel_id=1, source_target_pairs={{0,96},{32,0},{64,32},{96,64},{1,97},{33,1},{65,33},{97,65},{2,98}... | collective-permute-start | bytes 1277960 | tf_op jit(solution)/shard_map/ppermute | solution.py:27
  126.0 1.9 copy-start.5
  126.0 1.9 copy-start.6
  127.9 0.9 copy-start.15
  127.9 2.4 %copy-start.16 = (bf16[832,512]{1,0:T(8,128)(2,1)}, bf16[832,512]{1,0:T(8,128)(2,1)S(1)}, u32[]{:S(2)}) copy-start(bf16[832,512]{1,0:T(8,128)(2,1)S(1)} %get-tuple-element.81) | copy-start | bytes 2555908
  128.8 19.2 %collective-permute-start.37 = (bf16[416,1024]{1,0:T(8,128)(2,1)}, bf16[416,1024]{1,0:T(8,128)(2,1)}, u32[]{:S(2)}, u32[]{:S(2)}) collective-permute-start(bf16[416,1024]{1,0:T(8,128)(2,1)} %get-tuple-element.83), channel_id=1, source_target_pairs={{0,96},{32,0},{64,32},{96,64},{1,97},{33,1},{65,33},{97,65},{2,98}... | collective-permute-start | bytes 2555912 | tf_op jit(solution)/shard_map/ppermute | solution.py:27
  130.3 19.7 %collective-permute-start.36 = (bf16[416,1024]{1,0:T(8,128)(2,1)}, bf16[416,1024]{1,0:T(8,128)(2,1)}, u32[]{:S(2)}, u32[]{:S(2)}) collective-permute-start(bf16[416,1024]{1,0:T(8,128)(2,1)} %get-tuple-element.82), channel_id=1, source_target_pairs={{0,32},{32,64},{64,96},{96,0},{1,33},{33,65},{65,97},{97,1},{2,34}... | collective-permute-start | bytes 2555912 | tf_op jit(solution)/shard_map/ppermute | solution.py:27
  133.2 21.3 %collective-permute-start.25 = (bf16[864,512]{1,0:T(8,128)(2,1)}, bf16[864,512]{1,0:T(8,128)(2,1)}, u32[]{:S(2)}, u32[]{:S(2)}) collective-permute-start(bf16[864,512]{1,0:T(8,128)(2,1)} %copy-done.15), channel_id=1, source_target_pairs={{0,16},{16,2},{2,18},{18,0},{1,17},{17,3},{3,19},{19,1},{4,20},{20... | collective-permute-start | bytes 2654216 | tf_op jit(solution)/shard_map/ppermute | solution.py:26
  134.9 20.5 %collective-permute-start.26 = (bf16[832,512]{1,0:T(8,128)(2,1)}, bf16[832,512]{1,0:T(8,128)(2,1)S(1)}, u32[]{:S(2)}, u32[]{:S(2)}) collective-permute-start(bf16[832,512]{1,0:T(8,128)(2,1)} %copy-done.16), channel_id=1, source_target_pairs={{0,18},{16,0},{2,16},{18,2},{1,19},{17,1},{3,17},{19,3},{4,22},{20... | collective-permute-start | bytes 2555912 | tf_op jit(solution)/shard_map/ppermute | solution.py:26
  151.9 7.0 %collective-permute-start.40 = (bf16[208,512]{1,0:T(8,128)(2,1)S(1)}, bf16[208,512]{1,0:T(8,128)(2,1)S(1)}, u32[]{:S(2)}, u32[]{:S(2)}) collective-permute-start(bf16[208,512]{1,0:T(8,128)(2,1)S(1)} %get-tuple-element.89), channel_id=1, source_target_pairs={{0,2},{16,18},{2,0},{18,16},{1,3},{17,19},{3,1},{19,17},{4,6},{20,... | collective-permute-start | bytes 638984 | tf_op jit(solution)/shard_map/ppermute | solution.py:26
  152.8 11.1 %collective-permute-start.39 = (bf16[208,512]{1,0:T(8,128)(2,1)S(1)}, bf16[208,512]{1,0:T(8,128)(2,1)S(1)}, u32[]{:S(2)}, u32[]{:S(2)}) collective-permute-start(bf16[208,512]{1,0:T(8,128)(2,1)S(1)} %get-tuple-element.90), channel_id=1, source_target_pairs={{0,18},{16,0},{2,16},{18,2},{1,19},{17,1},{3,17},{19,3},{4,22},{20... | collective-permute-start | bytes 638984 | tf_op jit(solution)/shard_map/ppermute | solution.py:26
  154.5 9.4 %collective-permute-start.38 = (bf16[208,512]{1,0:T(8,128)(2,1)S(1)}, bf16[208,512]{1,0:T(8,128)(2,1)S(1)}, u32[]{:S(2)}, u32[]{:S(2)}) collective-permute-start(bf16[208,512]{1,0:T(8,128)(2,1)S(1)} %get-tuple-element.88), channel_id=1, source_target_pairs={{0,16},{16,2},{2,18},{18,0},{1,17},{17,3},{3,19},{19,1},{4,20},{20... | collective-permute-start | bytes 638984 | tf_op jit(solution)/shard_map/ppermute | solution.py:26
  157.1 13.1 %collective-permute-start.29 = (bf16[240,512]{1,0:T(8,128)(2,1)S(1)}, bf16[240,512]{1,0:T(8,128)(2,1)S(1)}, u32[]{:S(2)}, u32[]{:S(2)}) collective-permute-start(bf16[240,512]{1,0:T(8,128)(2,1)S(1)} %get-tuple-element.104), channel_id=1, source_target_pairs={{0,96},{32,0},{64,32},{96,64},{1,97},{33,1},{65,33},{97,65},{2,98}... | collective-permute-start | bytes 737288 | tf_op jit(solution)/shard_map/ppermute | solution.py:27
  158.7 11.5 %collective-permute-start.28 = (bf16[240,512]{1,0:T(8,128)(2,1)S(1)}, bf16[240,512]{1,0:T(8,128)(2,1)S(1)}, u32[]{:S(2)}, u32[]{:S(2)}) collective-permute-start(bf16[240,512]{1,0:T(8,128)(2,1)S(1)} %get-tuple-element.103), channel_id=1, source_target_pairs={{0,32},{32,64},{64,96},{96,0},{1,33},{33,65},{65,97},{97,1},{2,34}... | collective-permute-start | bytes 737288 | tf_op jit(solution)/shard_map/ppermute | solution.py:27
  158.9 11.3 %collective-permute-start.27 = (bf16[240,512]{1,0:T(8,128)(2,1)S(1)}, bf16[240,512]{1,0:T(8,128)(2,1)S(1)}, u32[]{:S(2)}, u32[]{:S(2)}) collective-permute-start(bf16[240,512]{1,0:T(8,128)(2,1)S(1)} %get-tuple-element.102), channel_id=1, source_target_pairs={{0,64},{32,96},{64,0},{96,32},{1,65},{33,97},{65,1},{97,33},{2,66}... | collective-permute-start | bytes 737288 | tf_op jit(solution)/shard_map/ppermute | solution.py:27
  164.1 26.6 %collective-permute-start.41 = (f32[104,512]{1,0:T(8,128)S(1)}, f32[104,512]{1,0:T(8,128)S(1)}, u32[]{:S(2)}, u32[]{:S(2)}) collective-permute-start(f32[104,512]{1,0:T(8,128)S(1)} %get-tuple-element.95), channel_id=1, source_target_pairs={{0,1},{1,0},{2,3},{3,2},{4,5},{5,4},{6,7},{7,6},{8,9},{9,8},{10,11... | collective-permute-start | bytes 638984 | tf_op jit(solution)/shard_map/ppermute | solution.py:31
  170.3 14.7 %collective-permute-start.31 = (f32[8,512]{1,0:T(8,128)S(1)}, f32[8,512]{1,0:T(8,128)S(1)}, u32[]{:S(2)}, u32[]{:S(2)}) collective-permute-start(f32[8,512]{1,0:T(8,128)S(1)} %slice.163), channel_id=1, source_target_pairs={{0,4},{4,8},{8,12},{12,0},{1,5},{5,9},{9,13},{13,1},{2,6},{6,10},{... | collective-permute-start | bytes 49160 | tf_op jit(solution)/shard_map/ppermute | solution.py:27
  171.9 13.2 %collective-permute-start.32 = (f32[8,512]{1,0:T(8,128)S(1)}, f32[8,512]{1,0:T(8,128)S(1)}, u32[]{:S(2)}, u32[]{:S(2)}) collective-permute-start(f32[8,512]{1,0:T(8,128)S(1)} %slice.163), channel_id=1, source_target_pairs={{0,12},{4,0},{8,4},{12,8},{1,13},{5,1},{9,5},{13,9},{2,14},{6,2},{... | collective-permute-start | bytes 49160 | tf_op jit(solution)/shard_map/ppermute | solution.py:27
  174.8 10.3 %collective-permute-start.30 = (f32[8,512]{1,0:T(8,128)S(1)}, f32[8,512]{1,0:T(8,128)S(1)}, u32[]{:S(2)}, u32[]{:S(2)}) collective-permute-start(f32[8,512]{1,0:T(8,128)S(1)} %slice.163), channel_id=1, source_target_pairs={{0,8},{4,12},{8,0},{12,4},{1,9},{5,13},{9,1},{13,5},{2,10},{6,14},... | collective-permute-start | bytes 49160 | tf_op jit(solution)/shard_map/ppermute | solution.py:27
  176.0 16.3 %copy-start.17 = (bf16[160,1664]{1,0:T(8,128)(2,1)S(1)}, bf16[160,1664]{1,0:T(8,128)(2,1)}, u32[]{:S(2)}) copy-start(bf16[160,1664]{1,0:T(8,128)(2,1)} %param.7) | copy-start | bytes 1597444
  176.1 17.6 %copy-start.18 = (bf16[160,1664]{1,0:T(8,128)(2,1)S(1)}, bf16[160,1664]{1,0:T(8,128)(2,1)}, u32[]{:S(2)}) copy-start(bf16[160,1664]{1,0:T(8,128)(2,1)} %param.8) | copy-start | bytes 1597444
  176.1 15.4 %collective-permute-start.34 = (f32[104,512]{1,0:T(8,128)S(1)}, f32[104,512]{1,0:T(8,128)S(1)}, u32[]{:S(2)}, u32[]{:S(2)}) collective-permute-start(f32[104,512]{1,0:T(8,128)S(1)} %get-tuple-element.97), channel_id=1, source_target_pairs={{0,1},{1,0},{2,3},{3,2},{4,5},{5,4},{6,7},{7,6},{8,9},{9,8},{10,11... | collective-permute-start | bytes 638984 | tf_op jit(solution)/shard_map/ppermute | solution.py:31
  185.0 3.7 %collective-permute-start.35 = (f32[512]{0:T(512)S(1)}, f32[512]{0:T(512)S(1)}, u32[]{:S(2)}, u32[]{:S(2)}) collective-permute-start(f32[512]{0:T(512)S(1)} %bitcast.26), channel_id=1, source_target_pairs={{0,1},{1,0},{2,3},{3,2},{4,5},{5,4},{6,7},{7,6},{8,9},{9,8},{10,11... | collective-permute-start | bytes 6152 | tf_op jit(solution)/shard_map/ppermute | solution.py:31
  185.1 4.4 %collective-permute-start.33 = (f32[8,512]{1,0:T(8,128)S(1)}, f32[8,512]{1,0:T(8,128)S(1)}, u32[]{:S(2)}, u32[]{:S(2)}) collective-permute-start(f32[8,512]{1,0:T(8,128)S(1)} %add_add_fusion.2), channel_id=1, source_target_pairs={{0,1},{1,0},{2,3},{3,2},{4,5},{5,4},{6,7},{7,6},{8,9},{9,8},{10,11... | collective-permute-start | bytes 49160 | tf_op jit(solution)/shard_map/ppermute | solution.py:31
  (4 other events, 3.0 us)
Sparse Core Ops, SparseCore 0:
  9.8 52.2 all-gather.2
  132.2 33.6 reduce-scatter.1
where the time goes:
time: 204 us; the launch traced here: 203 us
  starting transfers between devices  68.2 us (33%)
  Pallas kernels  50.6 us (25%)
  waiting for transfers between devices  39.9 us (20%)
  other arithmetic  17.3 us (8%)
  between operations  14.9 us (7%)
  local copies, waits for them, and re-layouts  12 us (6%)
    pallas_call x10, Pallas kernels, call(): pl.pallas_call(kernel, out_shape=[jax.ShapeDtypeStruct(shape, dtype) for...  50.6 us
    ppermute x8, starting transfers between devices, swap(): return lax.ppermute(value, 'core', [(0, 1), (1, 0)])  24.8 us
    ppermute x18, starting transfers between devices, shift(): return lax.ppermute(value, axis, [(i, (i + by) % 4) for i in range(4)])  24 us
    ppermute x15, waiting for transfers between devices, shift(): return lax.ppermute(value, PLANE_Y, pairs)  21.3 us
    ppermute x15, starting transfers between devices, shift(): return lax.ppermute(value, PLANE_Y, pairs)  17.9 us
    ppermute x18, waiting for transfers between devices, shift(): return lax.ppermute(value, axis, [(i, (i + by) % 4) for i in range(4)])  16.8 us
    unnamed x60, local copies, waits for them, and re-layouts  11.5 us
  transfers between devices with their start and end apart: 44, of which 11 were waited for; matrix products, arithmetic and copies ran while one was open for 6% of the time, Pallas kernels for 11%

commit v1 on v0

--- a/solution.py
+++ b/solution.py
@@ -39,29 +39,18 @@
     return shift(ahead, axis, 1), shift(behind, axis, -1)
 
 
-def ring_sum(value, axis):
-    return (value + shift(value, axis, 2)) + (shift(value, axis, 1) + shift(value, axis, -1))
-
-
-def parts_of(vector):
-    high = lax.reduce_precision(vector, 8, 7)
-    return jnp.concatenate([high, lax.reduce_precision(vector - high, 8, 7)], 0).astype(bf16)
+def pair_sum(value, axis):
+    for bit in (1, 2):
+        value = value + lax.ppermute(value, axis, [(i, i ^ bit) for i in range(4)])
+    return value
 
 
 def from_parts(rows):
     return rows[:16].astype(f32) + rows[16:].astype(f32)
 
 
-def direct_scatter(block, axis, vector=None):
-    rows = block(0).shape[0]
-    riding = [] if vector is None else [parts_of(vector)]
-    got = [shift(jnp.concatenate([block(by).astype(bf16), *riding], 0), axis, by) for by in (1, 2, 3)]
-    ahead, far, behind = (part[:rows].astype(f32) for part in got)
-    summed = block(0) + ahead + behind + far
-    if vector is None:
-        return summed, None
-    own, v_ahead, v_far, v_behind = (from_parts(part) for part in (*riding, *(p[rows:] for p in got)))
-    return summed, (own + v_far) + (v_ahead + v_behind)
+def direct(ahead, far, behind, axis):
+    return shift(ahead, axis, 1), shift(far, axis, 2), shift(behind, axis, 3)
 
 
 def assemble_kernel(first, own, right, far_low, far_high, left, whole):
@@ -94,17 +83,46 @@
     return lax.dot_general(left, right, (dims, ((), ())), preferred_element_type=f32)
 
 
-def call(kernel, outs, args, scratch=(), aliases=None, limit=16):
+def call(kernel, outs, args, scratch=(), aliases=None, behind=(), mark=False, limit=16):
+    given, made = len(args), len(outs)
+
+    def body(*refs):
+        refs = refs[:given] + refs[given + len(behind) :]
+        if mark:
+            refs[given + made][...] = jnp.zeros_like(refs[given + made])
+            refs = refs[: given + made] + refs[given + made + 1 :]
+        kernel(*refs)
+
+    outs = [*outs, *[((8, 128), f32)] * mark]
+    whole = pl.BlockSpec(memory_space=pltpu.VMEM)
     return pl.pallas_call(
-        kernel,
+        body,
         out_shape=[jax.ShapeDtypeStruct(shape, dtype) for shape, dtype in outs],
-        in_specs=[pl.BlockSpec(memory_space=pltpu.VMEM)] * len(args),
-        out_specs=[pl.BlockSpec(memory_space=pltpu.VMEM)] * len(outs),
+        in_specs=[whole] * (given + len(behind)),
+        out_specs=[whole] * len(outs),
         scratch_shapes=list(scratch),
         input_output_aliases=aliases or {},
         compiler_params=pltpu.CompilerParams(vmem_limit_bytes=limit * 2**20),
         cost_estimate=pl.CostEstimate(flops=10**6, bytes_accessed=10**6, transcendentals=0),
-    )(*args)
+    )(*args, *behind)
+
+
+def stack_kernel(inputs, upstream, stacked):
+    stacked[0, 0] = inputs[...]
+    stacked[0, 1] = upstream[...]
+
+
+def nothing_kernel(*refs):
+    pass
+
+
+def add_kernel(mine, others, total):
+    def step(i, _):
+        at = pl.ds(pl.multiple_of(i * 32, 32), 32)
+        total[at, :] = (mine[at, :] + others[at, :].astype(f32)).astype(bf16)
+        return 0
+
+    lax.fori_loop(0, mine.shape[0] // 32, step, 0)
 
 
 def norm_kernel(half, part, gain, shift_by, *refs):
@@ -173,6 +191,12 @@
     lax.fori_loop(0, tiles // 2, step, 0)
 
 
+def second_kernel(part, gain, shift_by, bias, expand, shrink, normed_t_in, up_t_in, active_in, back_in, *refs):
+    centre, scale, normed_t, up_t, bias_sum, active, back, normed, turned, pre_tile, back_tile = refs
+    norm_kernel(1, part, gain, shift_by, normed, centre, scale, normed_t, up_t, turned)
+    hidden_kernel(1, part, normed, expand, shrink, bias, bias_sum, active, back, pre_tile, back_tile)
+
+
 def shrink_tile(far, n, up_t, active):
     x, _ = place()
     rows, lanes = up_t.shape[0] // 4, pl.ds(pl.multiple_of(n * 256, 256), 256)
@@ -201,16 +225,16 @@
 
     lax.fori_loop(0, active.shape[1] // 256, tile_of(shrink_tile, up_t, active, shrink_low, shrink_high), 0)
     lax.fori_loop(0, back.shape[1] // 512, tile_of(expand_tile, normed_t, back, expand_low, expand_high), 0)
-    half, width = expand_low.shape[1], sums.shape[1]
+    hidden, width = bias.shape[1], sums.shape[1]
     vector[...] = jnp.zeros_like(vector)
     for i in range(2):
-        for j, start in enumerate(range(0, width, half)):
-            size = min(half, width - start)
-            vector[4 * i + j : 4 * i + j + 1, :size] = sums[i : i + 1, start : start + size]
-        vector[8 + i : 9 + i, :] = bias[:, i * half : (i + 1) * half]
+        for j, start in enumerate(range(0, width, hidden)):
+            size = min(hidden, width - start)
+            vector[2 * i + j : 2 * i + j + 1, :size] = sums[i : i + 1, start : start + size]
+    vector[4:5, :] = bias[...]
     high = vector[...].astype(bf16)
     riding = jnp.concatenate([high, (vector[...] - high.astype(f32)).astype(bf16)], 0)
-    for to in (expand_low, expand_high):
+    for to in (shrink_low, shrink_high):
         to[to.shape[0] - 32 :, :] = riding
     vector[...] = riding[:16].astype(f32) + riding[16:].astype(f32)
 
@@ -256,8 +280,87 @@
             return 0
 
         lax.fori_loop(0, rows // 16, step, 0)
-    rows = e_terms.shape[1]
-    e_ahead[rows:, :] = e_low[rows // 2 :, :]
+    rows = s_terms.shape[1]
+    s_ahead[rows:, :] = s_low[rows // 2 :, :]
+
+
+def finish_shrink_kernel(own, prev, following, low, high, vector, mine, ahead, far, behind, sums, laid):
+    _, y = place()
+    rows, half = mine.shape
+    wide = own.shape[0]
+
+    def block(by):
+        py = lax.rem(y + by, 4)
+        at = pl.ds(pl.multiple_of(lax.div(py, 2) * rows, 16), rows)
+        lanes = pl.ds(pl.multiple_of(lax.rem(py, 2) * half, 128), half)
+        return own[at, lanes] + prev[at, lanes].astype(f32) + following[at, lanes].astype(f32)
+
+    v_prev, v_next, v_far = (from_parts(part[part.shape[0] - 32 :, :]) for part in (low, high, prev))
+    total = (vector[...] + v_far) + (v_prev + v_next)
+    laid[...] = jnp.zeros_like(laid)
+    for r in range(5):
+        for k in range(2):
+            laid[2 * r + k : 2 * r + k + 1, :] = total[r : r + 1, k * half : (k + 1) * half]
+    top = laid[...].astype(bf16)
+    riding = jnp.concatenate([top, (laid[...] - top.astype(f32)).astype(bf16)], 0)
+    sums[...] = from_parts(riding)
+    mine[...] = block(0)
+    for by, to in ((1, ahead), (2, far), (3, behind)):
+        to[:rows, :] = block(by).astype(bf16)
+        to[rows:, :] = riding
+
+
+def finish_expand_kernel(own, prev, following, mine, ahead, far, behind):
+    x, _ = place()
+    rows = mine.shape[0]
+
+    def block(by):
+        at = pl.ds(pl.multiple_of(lax.rem(x + by, 4) * rows, 16), rows)
+        return own[at, :] + prev[at, :].astype(f32) + following[at, :].astype(f32)
+
+    mine[...] = block(0)
+    for by, to in ((1, ahead), (2, far), (3, behind)):
+        to[...] = block(by).astype(bf16)
+
+
+def middle_kernel(mine, ahead, behind, total):
+    total[...] = mine[...] + ahead[...].astype(f32) + behind[...].astype(f32)
+
+
+def last_kernel(mine, *refs):
+    if len(refs) == 3:
+        got, (kept, given) = refs[:1], refs[1:]
+    else:
+        got, own, (kept, given, sums) = refs[:3], refs[3], refs[4:]
+        v_ahead, v_far, v_behind = (from_parts(part[part.shape[0] - 32 :, :]) for part in got)
+        sums[...] = (own[...] + v_far) + (v_ahead + v_behind)
+    rows = mine.shape[0]
+    total = mine[...]
+    for part in got:
+        total = total + part[:rows, :].astype(f32)
+    core = lax.axis_index("core")
+    top, bottom = total[: rows // 2], total[rows // 2 :]
+    kept[...] = jnp.where(core == 0, top, bottom)
+    given[...] = jnp.where(core == 0, bottom, top)
+
+
+def inputs_kernel(inputs, upstream, grad, gain, result):
+    tokens, width = inputs.shape
+
+    def step(i, _):
+        at = pl.ds(pl.multiple_of(i * 32, 32), 32)
+        features = inputs[at, :].astype(f32)
+        shifted = features - jnp.mean(features, axis=1, keepdims=True)
+        scale = lax.rsqrt(jnp.mean(shifted * shifted, axis=1, keepdims=True) + EPSILON)
+        normed = shifted * scale
+        weighted = grad[at, :].astype(f32) * gain[...]
+        mean_one = jnp.mean(weighted, axis=1, keepdims=True)
+        mean_two = jnp.mean(weighted * normed, axis=1, keepdims=True)
+        change = scale * (weighted - mean_one - normed * mean_two)
+        result[at, :] = (upstream[at, :].astype(f32) + change).astype(bf16)
+        return 0
+
+    lax.fori_loop(0, tokens // 32, step, 0)
 
 
 def rows_kernel(near, other, near_centre, other_centre, near_scale, other_scale, back, expand, mine, others, sums):
@@ -303,55 +406,60 @@
     block_rows = 2 * rows
 
     bias_near = lax.ppermute(expand_bias, "ylo", [(0, 1), (1, 0)])
-    a, b, bias_near = lax.optimization_barrier((by_core(expand_weight), by_core(shrink_weight), bias_near))
-
-    near = lax.all_gather(jnp.stack([inputs, upstream])[None], "z", axis=0, tiled=True)
+    a, b = by_core(expand_weight), by_core(shrink_weight)
+
+    (stacked,) = call(stack_kernel, [((1, 2, tokens, width), bf16)], (inputs, upstream))
+    near = lax.all_gather(stacked, "z", axis=0, tiled=True)
 
     (a_left, a_right), (b_left, b_right) = both_ways(a, a, "x"), both_ways(b, b, "y")
     a_low, a_high = both_ways(a_left[:rows], a_right[rows:], "x")
     b_low, b_high = both_ways(b_left[:rows], b_right[rows:], "y")
     a = jnp.concatenate([a, a_right, a_low, a_high, a_left], 0)
+    a, bias_near = lax.optimization_barrier((a, bias_near))
     b = jnp.concatenate([b, b_right, b_low, b_high, b_left], 0)
     (a_left, a_right), (b_left, b_right) = both_ways(a, a, "y"), both_ways(b, b, "x")
     halves = a_left[: 2 * block_rows], a_right[2 * block_rows :], b_left[: 2 * block_rows], b_right[2 * block_rows :]
     a_low, a_high = both_ways(*halves[:2], "y")
     b_low, b_high = both_ways(*halves[2:], "x")
-    weight_shape = [((width, 2 * half), bf16)]
-    (expand_all,) = call(functools.partial(assemble_kernel, "x"), weight_shape, (a, a_right, a_low, a_high, a_left))
-    (shrink_all,) = call(functools.partial(assemble_kernel, "y"), weight_shape, (b, b_right, b_low, b_high, b_left))
+    pieces = (a, a_right, a_low, a_high, a_left), (b, b_right, b_low, b_high, b_left)
     bias_both = jnp.where(ylo == 0, jnp.stack([expand_bias, bias_near]), jnp.stack([bias_near, expand_bias]))
     bias_own = lax.dynamic_slice_in_dim(bias_both, core * half, half, 1).reshape(1, 2 * half)
 
-    near = after(near, a_low, a_high, b_low, b_high)
+    (mark,) = call(nothing_kernel, [], (a_low, a_high, b_low, b_high), mark=True)
+    near, mark = lax.optimization_barrier((near, mark))
     other = swap(near)
     many = 8 * tokens
     tall, wide = ((width, many), bf16), ((many, 2 * half), bf16)
-    column, own_normed_shape = ((4 * tokens, 1), f32), ((4 * tokens, width), bf16)
+    column, half_tall, bias_row = ((4 * tokens, 1), f32), (4 * tokens, width), ((1, 2 * half), f32)
+    weight = ((width, 2 * half), bf16)
     gain, shift_by = norm_gain[None], norm_shift[None]
-
-    def normalise(which, part, *so_far):
-        return call(
-            functools.partial(norm_kernel, which),
-            [own_normed_shape, column, column, tall, tall],
-            (part, gain, shift_by, *so_far),
-            scratch=[pltpu.VMEM((width, 4 * tokens), bf16)],
-            aliases={3: 3, 4: 4} if so_far else None,
-        )
-
-    def project(which, part, normed, *so_far):
-        tiles = pltpu.VMEM((2, 4 * tokens, 256), f32)
-        return call(
-            functools.partial(hidden_kernel, which),
-            [((1, 2 * half), f32), wide, wide],
-            (part, normed, expand_all, shrink_all, bias_own, *so_far),
-            scratch=[tiles, tiles],
-            aliases={5: 1, 6: 2} if so_far else None,
-        )
-
-    normed, near_centre, near_scale, *turned = normalise(0, near)
-    near_bias, *hidden_parts = project(0, near, normed)
-    normed, other_centre, other_scale, normed_t, up_t = normalise(1, other, *turned)
-    other_bias, active, back = project(1, other, normed, *hidden_parts)
+    tile = pltpu.VMEM((2, 4 * tokens, 256), f32)
+    turned = pltpu.VMEM((width, 4 * tokens), bf16)
+    normed, near_centre, near_scale, normed_t, up_t, mark = call(
+        functools.partial(norm_kernel, 0),
+        [(half_tall, bf16), column, column, tall, tall],
+        (near, gain, shift_by),
+        scratch=[turned],
+        behind=(mark,),
+        mark=True,
+    )
+    expand_all, shrink_all = (
+        call(functools.partial(assemble_kernel, first), [weight], part, behind=(mark,))[0]
+        for first, part in zip("xy", pieces, strict=True)
+    )
+    near_bias, active, back = call(
+        functools.partial(hidden_kernel, 0),
+        [bias_row, wide, wide],
+        (near, normed, expand_all, shrink_all, bias_own),
+        scratch=[tile, tile],
+    )
+    other_centre, other_scale, normed_t, up_t, other_bias, active, back = call(
+        second_kernel,
+        [column, column, tall, tall, bias_row, wide, wide],
+        (other, gain, shift_by, bias_own, expand_all, shrink_all, normed_t, up_t, active, back),
+        scratch=[pltpu.VMEM(half_tall, bf16), turned, tile, tile],
+        aliases={6: 2, 7: 3, 8: 5, 9: 6},
+    )
     bias_part = near_bias + other_bias
 
     mine, others, norm_sums = call(
@@ -360,51 +468,59 @@
         (near, other, near_centre, other_centre, near_scale, other_scale, back, expand_all),
     )
 
-    short, long = ((block_rows, 2 * half), bf16), ((2 * block_rows + 32, half), bf16)
+    short, long = ((block_rows + 32, 2 * half), bf16), ((2 * block_rows, half), bf16)
     s_low, s_high, e_low, e_high, vector = call(
         far_kernel,
-        [short, short, long, long, ((16, half), f32)],
+        [short, short, long, long, ((16, 2 * half), f32)],
         (up_t, active, normed_t, back, norm_sums, bias_part),
     )
-    (s_low, s_high), (e_low, e_high), sent = both_ways(s_low, s_high, "x"), both_ways(e_low, e_high, "y"), s_low
+    (s_low, s_high), (e_low, e_high) = both_ways(s_low, s_high, "x"), both_ways(e_low, e_high, "y")
+
+    both, mark = call(add_kernel, [((4 * tokens, width), bf16)], (mine, swap(others)), behind=(vector,), mark=True)
+
     s_wide, e_wide = (2 * block_rows, 2 * half), (4 * block_rows, half)
     s_own, e_own, s_terms, e_terms = call(
         near_kernel,
         [(s_wide, f32), (e_wide, f32), ((2, *s_wide), f32), ((2, *e_wide), f32)],
-        (up_t, active, normed_t, after(back, sent)),
-    )
-    s_ahead, s_behind, e_ahead, e_behind = call(
+        (up_t, active, normed_t, back),
+        behind=(mark,),
+    )
+    s_ahead, s_behind, e_ahead, e_behind, mark = call(
         pass_kernel,
-        [(s_wide, bf16), (s_wide, bf16), ((4 * block_rows + 32, half), bf16), (e_wide, bf16)],
+        [((2 * block_rows + 32, 2 * half), bf16), (s_wide, bf16), (e_wide, bf16), (e_wide, bf16)],
         (s_terms, e_terms, s_low, s_high, e_low, e_high),
+        mark=True,
     )
     (s_prev, s_next), (e_prev, e_next) = both_ways(s_ahead, s_behind, "x"), both_ways(e_ahead, e_behind, "y")
 
-    both = after(mine, s_own) + swap(after(others, sent)).astype(f32)
-    grad_normed = lax.psum_scatter(both.astype(bf16), "z", scatter_dimension=0, tiled=True).astype(f32)
-
-    s_sum = s_own + s_prev.astype(f32) + s_next.astype(f32)
-    e_sum = e_own + e_prev[: 4 * block_rows].astype(f32) + e_next.astype(f32)
-    v_prev, v_next, v_far = (
-        from_parts(part) for part in (e_low[2 * block_rows :], e_high[2 * block_rows :], e_prev[4 * block_rows :])
-    )
-    vector = (vector + v_far) + (v_prev + v_next)
-
-    def shrink_block(far):
-        py = (y + far) % 4
-        return lax.dynamic_slice(s_sum, (py // 2 * block_rows, py % 2 * half), (block_rows, half))
-
-    def expand_block(far):
-        return lax.dynamic_slice_in_dim(e_sum, (x + far) % 4 * block_rows, block_rows, 0)
-
-    def by_rows(block):
-        kept = lax.dynamic_slice_in_dim(block, core * rows, rows, 0)
-        got = swap(lax.dynamic_slice_in_dim(block, (1 - core) * rows, rows, 0))
+    both, pass_mark = lax.optimization_barrier((both, mark))
+    grad_normed = lax.psum_scatter(both, "z", scatter_dimension=0, tiled=True)
+
+    block, riding = (block_rows, half), ((block_rows + 32, half), bf16)
+    s_mine, *s_blocks, vector = call(
+        finish_shrink_kernel,
+        [(block, f32), riding, riding, riding, ((16, half), f32)],
+        (s_own, s_prev, s_next, s_low, s_high, vector),
+        scratch=[pltpu.VMEM((16, half), f32)],
+        behind=(pass_mark,),
+    )
+    s_got = direct(*s_blocks, "y")
+    e_mine, *e_blocks = call(finish_expand_kernel, [(block, f32)] + [(block, bf16)] * 3, (e_own, e_prev, e_next))
+    e_ahead, e_far, e_behind = direct(*e_blocks, "x")
+    inputs_grad, done = call(
+        inputs_kernel, [((tokens, width), bf16)], (inputs, upstream, grad_normed, norm_gain[None]), mark=True
+    )
+    e_mine, mark = call(middle_kernel, [(block, f32)], (e_mine, e_ahead, e_far), behind=(done,), mark=True)
+    part = ((rows, half), f32)
+    s_kept, s_given, vector = call(last_kernel, [part, part, ((16, half), f32)], (s_mine, *s_got, vector), behind=(mark,))
+    e_kept, e_given = call(last_kernel, [part, part], (e_mine, e_behind))
+
+    def by_rows(kept, given):
+        got = swap(given)
         return jnp.where(core == 0, jnp.concatenate([kept, got], 1), jnp.concatenate([got, kept], 1))
 
-    expand_own, vector = direct_scatter(expand_block, "x", vector)
-    shrink_own, _ = direct_scatter(shrink_block, "y")
-    norm_sums = ring_sum(vector[:8], "z")
+    shrink_grad, expand_grad = by_rows(s_kept, s_given), by_rows(e_kept, e_given)
+    norm_sums = pair_sum(vector[:8], "z")
     norm_sums = norm_sums + swap(norm_sums)
     gain_grad, shift_grad = (norm_sums[i : i + 4].reshape(-1)[:width] for i in (0, 4))
     bias_mine = lax.dynamic_index_in_dim(vector, 8 + ylo, 0, keepdims=False)
@@ -412,18 +528,6 @@
     bias_grad = jnp.where(
         core == 0, jnp.concatenate([bias_mine, bias_other]), jnp.concatenate([bias_other, bias_mine])
     )
-    shrink_grad, expand_grad = by_rows(shrink_own), by_rows(expand_own)
-
-    features = inputs.astype(f32)
-    own_centre = jnp.mean(features, axis=1, keepdims=True)
-    shifted = features - own_centre
-    own_scale = lax.rsqrt(jnp.mean(shifted * shifted, axis=1, keepdims=True) + EPSILON)
-    own_normed = shifted * own_scale
-    weighted = grad_normed * norm_gain
-    mean_one = jnp.sum(weighted, axis=1, keepdims=True) / width
-    mean_two = jnp.sum(weighted * own_normed, axis=1, keepdims=True) / width
-    result = own_scale * (weighted - mean_one - own_normed * mean_two)
-    inputs_grad = (upstream.astype(f32) + result).astype(bf16)
     return inputs_grad, gain_grad, shift_grad, expand_grad, bias_grad, shrink_grad
 
 

time: 204 us -> 198 us (0.971)
  other arithmetic: 17.3 us -> 2.39 us
  starting transfers between devices: 68.2 us -> 56.4 us
  waiting for transfers between devices: 39.9 us -> 48.7 us
  local copies, waits for them, and re-layouts: 12 us -> 20.6 us
  Pallas kernels: 50.6 us -> 55 us
    ppermute x8, starting transfers between devices: 24.8 us -> 13.8 us  [swap(): return lax.ppermute(value, 'core', [(0, 1), (1, 0)])]
    ppermute x18 -> x15, waiting for transfers between devices: 16.8 us -> 25.1 us  [shift(): return lax.ppermute(value, axis, [(i, (i + by) % 4) for i in range(4)])]
    unnamed x60 -> x72, local copies, waits for them, and re-layouts: 11.5 us -> 19.4 us
    ppermute x0 -> x2, starting transfers between devices: none -> 4.97 us  [pair_sum(): value = value + lax.ppermute(value, axis, [(i, i ^ bit) for i in range(4)])]
    pallas_call x10 -> x18, Pallas kernels: 50.6 us -> 55 us  [call(): pl.pallas_call(body, out_shape=[jax.ShapeDtypeStruct(shape, dtype) for sh...]
    convert_element_type x2 -> x0, other arithmetic: 4.08 us -> none  [the longest x1 2.38 us: local(): inputs_grad = (upstream.astype(f32) + result).astype(bf16)]
    ppermute x18 -> x15, starting transfers between devices: 24 us -> 19.9 us  [shift(): return lax.ppermute(value, axis, [(i, (i + by) % 4) for i in range(4)])]
    reduce_sum x3 -> x0, other arithmetic: 3.95 us -> none  [the longest x1 1.42 us: local(): mean_one = jnp.sum(weighted, axis=1, keepdims=True) / width]
  transfers between devices with their start and end apart: 44 -> 43, of which waited for: 11 -> 14; matrix products, arithmetic and copies ran while one was open for 6% -> 2% of each run, Pallas kernels for 11% -> 16%
where the time goes in v1:
time: 198 us
  starting transfers between devices  56.4 us (28%)
  Pallas kernels  55 us (28%)
  waiting for transfers between devices  48.7 us (25%)
  local copies, waits for them, and re-layouts  20.6 us (10%)
  between operations  14.6 us (7%)
  other arithmetic  2.39 us (1%)
    pallas_call x18, Pallas kernels, call(): pl.pallas_call(body, out_shape=[jax.ShapeDtypeStruct(shape, dtype) for sh...  55 us
    ppermute x15, waiting for transfers between devices, shift(): return lax.ppermute(value, axis, [(i, (i + by) % 4) for i in range(4)])  25.1 us
    ppermute x15, waiting for transfers between devices, shift(): return lax.ppermute(value, PLANE_Y, pairs)  21.4 us
    ppermute x15, starting transfers between devices, shift(): return lax.ppermute(value, axis, [(i, (i + by) % 4) for i in range(4)])  19.9 us
    unnamed x72, local copies, waits for them, and re-layouts  19.4 us
    ppermute x15, starting transfers between devices, shift(): return lax.ppermute(value, PLANE_Y, pairs)  17.7 us
    ppermute x8, starting transfers between devices, swap(): return lax.ppermute(value, 'core', [(0, 1), (1, 0)])  13.8 us
    ppermute x2, starting transfers between devices, pair_sum(): value = value + lax.ppermute(value, axis, [(i, i ^ bit) for i in range(4)])  4.97 us
  transfers between devices with their start and end apart: 43, of which 14 were waited for; matrix products, arithmetic and copies ran while one was open for 2% of the time, Pallas kernels for 16%

profile of v1, /device:TPU:1, one launch (start us, length us, event | category | flops | bytes accessed | tf_op | source)
XLA Modules:
  0.0 197.7 jit_solution(2508528276678444665)
XLA Ops:
  7.2 1.0 copy-done.1
  8.3 1.0 copy-done.3
  9.3 1.1 shard_map.118
  10.5 1.0 constant_dynamic-slice_fusion.1
  11.4 1.5 collective-permute-start.10
  13.1 0.8 collective-permute-done.10
  13.9 1.4 collective-permute-start.12
  15.4 1.5 collective-permute-start.11
  17.0 1.3 collective-permute-start.2
  18.3 1.5 collective-permute-start.1
  19.7 2.3 %collective-permute-done.12 = bf16[208,512]{1,0:T(8,128)(2,1)S(1)} collective-permute-done((bf16[208,512]{1,0:T(8,128)(2,1)S(1)}, bf16[208,512]{1,0:T(8,128)(2,1)S(1)}, u32[]{:S(2)}, u32[]{:S(2)}) %collective-permute-start.12) | collective-permute-done | bytes 213024 | tf_op jit(solution)/shard_map/ppermute | solution.py:26
  22.1 2.7 %collective-permute-start.14 = (bf16[104,512]{1,0:T(8,128)(2,1)S(1)}, bf16[104,512]{1,0:T(8,128)(2,1)S(1)}, u32[]{:S(2)}, u32[]{:S(2)}) collective-permute-start(bf16[104,512]{1,0:T(8,128)(2,1)S(1)} %slice.57), channel_id=1, source_target_pairs={{0,18},{16,0},{2,16},{18,2},{1,19},{17,1},{3,17},{19,3},{4,22},{20... | collective-permute-start | bytes 319496 | tf_op jit(solution)/shard_map/ppermute | solution.py:26
  24.9 1.2 collective-permute-start.3
  26.1 1.6 collective-permute-start.4
  27.8 2.3 %collective-permute-done.3 = bf16[104,512]{1,0:T(8,128)(2,1)S(1)} collective-permute-done((bf16[104,512]{1,0:T(8,128)(2,1)S(1)}, bf16[104,512]{1,0:T(8,128)(2,1)S(1)}, u32[]{:S(2)}, u32[]{:S(2)}) %collective-permute-start.3) | collective-permute-done | bytes 106528 | tf_op jit(solution)/shard_map/ppermute | solution.py:27
  30.8 1.0 collective-permute-start.6
  31.8 2.8 %collective-permute-start.17 = (bf16[832,512]{1,0:T(8,128)(2,1)S(1)}, bf16[832,512]{1,0:T(8,128)(2,1)S(1)}, u32[]{:S(2)}, u32[]{:S(2)}) collective-permute-start(bf16[832,512]{1,0:T(8,128)(2,1)S(1)} %constant_dynamic-update-slice_fusion.5.refs_0_), channel_id=1, source_target_pairs={{0,96},{32,0},{64,32},{96,64},{1,97},{33,1},{65,33},{97,65},{2,98}... | collective-permute-start | bytes 2555912 | tf_op jit(solution)/shard_map/ppermute | solution.py:27
  34.6 13.5 %collective-permute-done.8.refs_1_ = bf16[832,512]{1,0:T(8,128)(2,1)S(1)} collective-permute-done((bf16[832,512]{1,0:T(8,128)(2,1)S(1)}, bf16[832,512]{1,0:T(8,128)(2,1)S(1)}, u32[]{:S(2)}, u32[]{:S(2)}) %collective-permute-start.8) | collective-permute-done | bytes 852000 | tf_op jit(solution)/shard_map/ppermute | solution.py:26
  48.2 1.8 collective-permute-start.9
  50.1 3.2 %collective-permute-start.18 = (bf16[416,512]{1,0:T(8,128)(2,1)S(1)}, bf16[416,512]{1,0:T(8,128)(2,1)S(1)}, u32[]{:S(2)}, u32[]{:S(2)}) collective-permute-start(bf16[416,512]{1,0:T(8,128)(2,1)S(1)} %slice.59), channel_id=1, source_target_pairs={{0,96},{32,0},{64,32},{96,64},{1,97},{33,1},{65,33},{97,65},{2,98}... | collective-permute-start | bytes 1277960 | tf_op jit(solution)/shard_map/ppermute | solution.py:27
  53.4 3.1 %collective-permute-done.9.refs_1_.refs_3_ = bf16[416,512]{1,0:T(8,128)(2,1)S(1)} collective-permute-done((bf16[416,512]{1,0:T(8,128)(2,1)S(1)}, bf16[416,512]{1,0:T(8,128)(2,1)S(1)}, u32[]{:S(2)}, u32[]{:S(2)}) %collective-permute-start.9) | collective-permute-done | bytes 426016 | tf_op jit(solution)/shard_map/ppermute | solution.py:26
  56.5 2.4 %collective-permute-done.7.refs_0_.refs_2_ = bf16[416,512]{1,0:T(8,128)(2,1)S(1)} collective-permute-done((bf16[416,512]{1,0:T(8,128)(2,1)S(1)}, bf16[416,512]{1,0:T(8,128)(2,1)S(1)}, u32[]{:S(2)}, u32[]{:S(2)}) %collective-permute-start.7) | collective-permute-done | bytes 426016 | tf_op jit(solution)/shard_map/ppermute | solution.py:26
  58.9 3.1 %collective-permute-done.16.refs_2_ = bf16[416,512]{1,0:T(8,128)(2,1)S(1)} collective-permute-done((bf16[416,512]{1,0:T(8,128)(2,1)S(1)}, bf16[416,512]{1,0:T(8,128)(2,1)S(1)}, u32[]{:S(2)}, u32[]{:S(2)}) %collective-permute-start.16) | collective-permute-done | bytes 426016 | tf_op jit(solution)/shard_map/ppermute | solution.py:27
  62.0 0.8 copy-done.7
  62.8 0.8 copy-done.9
  64.3 0.8 copy-done.13
  65.0 5.0 %collective-permute-start.19 = (bf16[4,2,160,1664]{3,2,1,0:T(8,128)(2,1)}, bf16[4,2,160,1664]{3,2,1,0:T(8,128)(2,1)}, u32[]{:S(2)}, u32[]{:S(2)}) collective-permute-start(bf16[4,2,160,1664]{3,2,1,0:T(8,128)(2,1)} %all-gather.2.cloned.1.call-done.refs_0_), channel_id=1, source_target_pairs={{0,1},{1,0},{2,3},{3,2},{4,5},{5,4},{6,7},{7,6},{8,9},{9,8},{10,11... | collective-permute-start | bytes 12779528 | tf_op jit(solution)/shard_map/ppermute | solution.py:31
  70.2 2.2 %copy-done = bf16[4,2,160,1664]{3,2,1,0:T(8,128)(2,1)S(1)} copy-done((bf16[4,2,160,1664]{3,2,1,0:T(8,128)(2,1)S(1)}, bf16[4,2,160,1664]{3,2,1,0:T(8,128)(2,1)}, u32[]{:S(2)}) %copy-start) | copy-done | bytes 4259864
  72.4 3.6 %shard_map.120 = (bf16[640,1664]{1,0:T(8,128)(2,1)S(1)}, f32[640,1]{1,0:T(8,128)S(1)}, f32[640,1]{1,0:T(8,128)S(1)}, bf16[1664,1280]{1,0:T(8,128)(2,1)S(1)}, bf1...) custom-call(bf16[4,2,160,1664]{3,2,1,0:T(8,128)(2,1)S(1)} %copy-done, f32[1,1664]{1,0:T(1,128)S(1)} %broadcast_in_dim.7.refs_1_.refs_3_, ...), custom_call_target="tpu_custom_call" | custom-call | flops 1000000 | bytes 1000000 | tf_op jit(solution)/shard_map/pallas_call | solution.py:98
  76.1 1.0 copy-done.8
  77.1 1.0 copy-done.10
  78.1 1.2 copy-done.20
  80.9 7.3 %shard_map.123 = (f32[1,1024]{1,0:T(1,128)S(1)}, bf16[1280,1024]{1,0:T(8,128)(2,1)S(1)}, bf16[1280,1024]{1,0:T(8,128)(2,1)S(1)}) custom-call(bf16[4,2,160,1664]{3,2,1,0:T(8,128)(2,1)S(1)} %bitcast.16, bf16[640,1664]{1,0:T(8,128)(2,1)S(1)} %get-tuple-element.73.refs_1_, bf16[1664,1024]{1,0:T(8,128)(2,1)S(1)} %shard_map.121.refs_2_.refs_4_.refs_7_, ...), custom_call_target="tpu_custom_call" | custom-call | flops 1000000 | bytes 1000000 | tf_op jit(solution)/shard_map/pallas_call | solution.py:98
  88.3 13.0 %shard_map.124 = (f32[640,1]{1,0:T(8,128)S(1)}, f32[640,1]{1,0:T(8,128)S(1)}, bf16[1664,1280]{1,0:T(8,128)(2,1)S(1)}, bf16[1664,1280]{1,0:T(8,128)(2,1)S(1)}, f3...) custom-call(bf16[4,2,160,1664]{3,2,1,0:T(8,128)(2,1)} %collective-pe, ...), custom_call_target="tpu_custom_call", output_to_operand_aliasing={{2}: (6, {}), {3}: (7, {}), {5}: (8, {}), {6}: (9, {})} | custom-call | flops 1000000 | bytes 1000000 | tf_op jit(solution)/shard_map/pallas_call | solution.py:98
  101.3 8.9 %shard_map.125 = (f32[640,1664]{1,0:T(8,128)S(1)}, bf16[640,1664]{1,0:T(8,128)(2,1)S(1)}, f32[2,1664]{1,0:T(2,128)S(1)}) custom-call(bf16[4,2,160,1664]{3,2,1,0:T(8,128)(2,1)S(1)} %bitcast.16, bf16[4,2,160,1664]{3,2,1,0:T(8,128)(2,1)} %collective-permute-done.19.refs_0_.refs_1_, f32[640,1]{1,0:T(8,128)S(1)} %get-tuple-element.68.refs_2_, ...), custom_call_target="tpu_custom_call" | custom-call | flops 1000000 | bytes 1000000 | tf_op jit(solution)/shard_map/pallas_call | solution.py:98
  110.3 3.3 %shard_map.126 = (bf16[240,1024]{1,0:T(8,128)(2,1)S(1)}, bf16[240,1024]{1,0:T(8,128)(2,1)S(1)}, bf16[416,512]{1,0:T(8,128)(2,1)S(1)}, bf16[416,512]{1,0:T(8,128)(2,1)S(1)}, f32[16,1024]{1,0:T(8,128)S(1)}) custom-call(bf16[1664,1280]{1,0:T(8,128)(2,1)S(1)} %get-tuple-element.82.refs_0_, bf16[1280,1024]{1,0:T(8,128)(2,1)S(1)} %get-tuple-element.83.refs_1_, ...), custom_call_target="tpu_custom_call" | custom-call | flops 1000000 | bytes 1000000 | tf_op jit(solution)/shard_map/pallas_call | solution.py:98
  113.7 2.7 %collective-permute-start.22 = (bf16[240,1024]{1,0:T(8,128)(2,1)S(1)}, bf16[240,1024]{1,0:T(8,128)(2,1)S(1)}, u32[]{:S(2)}, u32[]{:S(2)}) collective-permute-start(bf16[240,1024]{1,0:T(8,128)(2,1)S(1)} %get-tuple-element.94), channel_id=1, source_target_pairs={{0,96},{32,0},{64,32},{96,64},{1,97},{33,1},{65,33},{97,65},{2,98}... | collective-permute-start | bytes 1474568 | tf_op jit(solution)/shard_map/ppermute | solution.py:27
  116.5 2.6 %collective-permute-start.24 = (bf16[416,512]{1,0:T(8,128)(2,1)S(1)}, bf16[416,512]{1,0:T(8,128)(2,1)S(1)}, u32[]{:S(2)}, u32[]{:S(2)}) collective-permute-start(bf16[416,512]{1,0:T(8,128)(2,1)S(1)} %get-tuple-element.96), channel_id=1, source_target_pairs={{0,18},{16,0},{2,16},{18,2},{1,19},{17,1},{3,17},{19,3},{4,22},{20... | collective-permute-start | bytes 1277960 | tf_op jit(solution)/shard_map/ppermute | solution.py:26
  119.1 1.8 shard_map.127
  120.9 10.0 %shard_map.128 = (f32[416,1024]{1,0:T(8,128)S(1)}, f32[832,512]{1,0:T(8,128)S(1)}, f32[2,416,1024]{2,1,0:T(8,128)S(1)}, f32[2,832,512]{2,1,0:T(8,128)S(1)}) custom-call(bf16[1664,1280]{1,0:T(8,128)(2,1)S(1)} %get-tuple-element.82.refs_0_, bf16[1280,1024]{1,0:T(8,128)(2,1)S(1)} %get-tuple-element.83.refs_1_, ...), custom_call_target="tpu_custom_call" | custom-call | flops 1000000 | bytes 1000000 | tf_op jit(solution)/shard_map/pallas_call | solution.py:98
  132.6 0.9 copy-done.22
  133.6 1.0 copy-done.23
  134.6 1.0 copy-done.24
  135.7 2.7 %collective-permute-start.26 = (bf16[416,1024]{1,0:T(8,128)(2,1)}, bf16[416,1024]{1,0:T(8,128)(2,1)S(1)}, u32[]{:S(2)}, u32[]{:S(2)}) collective-permute-start(bf16[416,1024]{1,0:T(8,128)(2,1)} %copy-done.24), channel_id=1, source_target_pairs={{0,96},{32,0},{64,32},{96,64},{1,97},{33,1},{65,33},{97,65},{2,98}... | collective-permute-start | bytes 2555912 | tf_op jit(solution)/shard_map/ppermute | solution.py:27
  138.3 2.7 %collective-permute-start.31 = (bf16[832,512]{1,0:T(8,128)(2,1)}, bf16[832,512]{1,0:T(8,128)(2,1)S(1)}, u32[]{:S(2)}, u32[]{:S(2)}) collective-permute-start(bf16[832,512]{1,0:T(8,128)(2,1)} %copy-done.22), channel_id=1, source_target_pairs={{0,18},{16,0},{2,16},{18,2},{1,19},{17,1},{3,17},{19,3},{4,22},{20... | collective-permute-start | bytes 2555912 | tf_op jit(solution)/shard_map/ppermute | solution.py:26
  141.0 14.0 %collective-permute-done.26.refs_2_ = bf16[416,1024]{1,0:T(8,128)(2,1)S(1)} collective-permute-done((bf16[416,1024]{1,0:T(8,128)(2,1)}, bf16[416,1024]{1,0:T(8,128)(2,1)S(1)}, u32[]{:S(2)}, u32[]{:S(2)}) %collective-permute-start.26) | collective-permute-done | bytes 852000 | tf_op jit(solution)/shard_map/ppermute | solution.py:27
  155.0 2.2 %collective-permute-done.25.refs_1_ = bf16[448,1024]{1,0:T(8,128)(2,1)S(1)} collective-permute-done((bf16[448,1024]{1,0:T(8,128)(2,1)S(1)}, bf16[448,1024]{1,0:T(8,128)(2,1)S(1)}, u32[]{:S(2)}, u32[]{:S(2)}) %collective-permute-start.25) | collective-permute-done | bytes 917536 | tf_op jit(solution)/shard_map/ppermute | solution.py:27
  157.2 1.5 copy-done.6
  158.7 1.1 shard_map.131
  159.9 2.3 %collective-permute-start.28 = (bf16[240,512]{1,0:T(8,128)(2,1)}, bf16[240,512]{1,0:T(8,128)(2,1)S(1)}, u32[]{:S(2)}, u32[]{:S(2)}) collective-permute-start(bf16[240,512]{1,0:T(8,128)(2,1)} %get-tuple-element.106), channel_id=1, source_target_pairs={{0,2},{16,18},{2,0},{18,16},{1,3},{17,19},{3,1},{19,17},{4,6},{20,... | collective-permute-start | bytes 737288 | tf_op jit(solution)/shard_map/ppermute | solution.py:26
  162.2 0.9 collective-permute-start.29
  163.0 1.0 shard_map.132
  164.0 2.4 %collective-permute-start.33 = (bf16[208,512]{1,0:T(8,128)(2,1)}, bf16[208,512]{1,0:T(8,128)(2,1)S(1)}, u32[]{:S(2)}, u32[]{:S(2)}) collective-permute-start(bf16[208,512]{1,0:T(8,128)(2,1)} %get-tuple-element.114), channel_id=1, source_target_pairs={{0,64},{32,96},{64,0},{96,32},{1,65},{33,97},{65,1},{97,33},{2,66}... | collective-permute-start | bytes 638984 | tf_op jit(solution)/shard_map/ppermute | solution.py:27
  166.4 1.0 copy-done.21
  167.5 2.4 %shard_map.130 = (bf16[160,1664]{1,0:T(8,128)(2,1)}, f32[8,128]{1,0:T(8,128)S(1)}) custom-call(bf16[160,1664]{1,0:T(8,128)(2,1)S(1)} %copy-done.2, bf16[160,1664]{1,0:T(8,128)(2,1)S(1)} %copy-done.4, bf16[160,1664]{1,0:T(8,128)(2,1)S(1)} %copy-done.21, f32[1,1664]{1,0:T(1,128)S(1)} %broadcast_in_dim.7.refs_1_.refs_3_), custom_call_target="tpu_custom_call" | custom-call | flops 1000000 | bytes 1000000 | tf_op jit(solution)/shard_map/pallas_call | solution.py:98
  169.9 2.4 %collective-permute-done.32.refs_1_ = bf16[208,512]{1,0:T(8,128)(2,1)S(1)} collective-permute-done((bf16[208,512]{1,0:T(8,128)(2,1)}, bf16[208,512]{1,0:T(8,128)(2,1)S(1)}, u32[]{:S(2)}, u32[]{:S(2)}) %collective-permute-start.32) | collective-permute-done | bytes 213024 | tf_op jit(solution)/shard_map/ppermute | solution.py:27
  172.3 1.0 collective-permute-done.33.refs_2_
  173.6 1.5 collective-permute-start.34
  175.5 1.1 collective-permute-done.34
  176.6 3.5 %collective-permute-start.35 = (f32[8,512]{1,0:T(8,128)S(1)}, f32[8,512]{1,0:T(8,128)S(1)}, u32[]{:S(2)}, u32[]{:S(2)}) collective-permute-start(f32[8,512]{1,0:T(8,128)S(1)} %slice_add_fusion), channel_id=1, source_target_pairs={{0,8},{4,12},{8,0},{12,4},{1,9},{5,13},{9,1},{13,5},{2,10},{6,14},... | collective-permute-start | bytes 49160 | tf_op jit(solution)/shard_map/ppermute | solution.py:44
  180.1 5.4 %collective-permute-start.39 = (f32[512]{0:T(512)S(1)}, f32[512]{0:T(512)S(1)}, u32[]{:S(2)}, u32[]{:S(2)}) collective-permute-start(f32[512]{0:T(512)S(1)} %bitcast.19), channel_id=1, source_target_pairs={{0,1},{1,0},{2,3},{3,2},{4,5},{5,4},{6,7},{7,6},{8,9},{9,8},{10,11... | collective-permute-start | bytes 6152 | tf_op jit(solution)/shard_map/ppermute | solution.py:31
  186.2 1.1 collective-permute-start.36
  189.3 0.8 maximum_select_fusion
  190.1 0.8 maximum_select_fusion.1
  (141 shorter events, 9.5 us)
Async XLA Ops:
  7.2 57.9 %all-gather.2.cloned.1.call-start = ((), (), s32[]{:S(2)}) async-start(), calls=%async_computation.1 | async-start | bytes 5324800 | tf_op jit(solution)/shard_map/all_gather | solution.py:412
  7.2 1.0 copy-start.1
  8.3 1.0 copy-start.3
  9.3 3.6 %copy-start.25 = (bf16[104,1024]{1,0:T(8,128)(2,1)S(1)}, bf16[104,1024]{1,0:T(8,128)(2,1)}, u32[]{:S(2)}) copy-start(bf16[104,1024]{1,0:T(8,128)(2,1)} %param.11) | copy-start | bytes 638980
  9.3 10.4 %copy-start.28 = (f32[1024]{0:T(1024)S(1)}, f32[1024]{0:T(1024)}, u32[]{:S(2)}) copy-start(f32[1024]{0:T(1024)} %param.12) | copy-start | bytes 12292
  10.4 156.0 %reduce-scatter.2.cloned.1.call-start = ((), (), s32[]{:S(2)}) async-start(), calls=%async_computation.2 | async-start | bytes 2662400 | tf_op jit(solution)/shard_map/reduce_scatter | solution.py:497
  11.4 2.5 %collective-permute-start.10 = (bf16[104,512]{1,0:T(8,128)(2,1)S(1)}, bf16[104,512]{1,0:T(8,128)(2,1)S(1)}, u32[]{:S(2)}, u32[]{:S(2)}) collective-permute-start(bf16[104,512]{1,0:T(8,128)(2,1)S(1)} %get-tuple-element.128), channel_id=1, source_target_pairs={{0,1},{1,0},{2,3},{3,2},{4,5},{5,4},{6,7},{7,6},{8,9},{9,8},{10,11... | collective-permute-start | bytes 319496 | tf_op jit(solution)/shard_map/ppermute | solution.py:31
  13.0 4.0 %collective-permute-start = (bf16[104,512]{1,0:T(8,128)(2,1)S(1)}, bf16[104,512]{1,0:T(8,128)(2,1)S(1)}, u32[]{:S(2)}, u32[]{:S(2)}) collective-permute-start(bf16[104,512]{1,0:T(8,128)(2,1)S(1)} %get-tuple-element.130), channel_id=1, source_target_pairs={{0,1},{1,0},{2,3},{3,2},{4,5},{5,4},{6,7},{7,6},{8,9},{9,8},{10,11... | collective-permute-start | bytes 319496 | tf_op jit(solution)/shard_map/ppermute | solution.py:31
  13.9 8.1 %collective-permute-start.12 = (bf16[208,512]{1,0:T(8,128)(2,1)S(1)}, bf16[208,512]{1,0:T(8,128)(2,1)S(1)}, u32[]{:S(2)}, u32[]{:S(2)}) collective-permute-start(bf16[208,512]{1,0:T(8,128)(2,1)S(1)} %get-tuple-element.125), channel_id=1, source_target_pairs={{0,16},{16,2},{2,18},{18,0},{1,17},{17,3},{3,19},{19,1},{4,20},{20... | collective-permute-start | bytes 638984 | tf_op jit(solution)/shard_map/ppermute | solution.py:26
  15.4 6.7 %collective-permute-start.11 = (bf16[208,512]{1,0:T(8,128)(2,1)S(1)}, bf16[208,512]{1,0:T(8,128)(2,1)S(1)}, u32[]{:S(2)}, u32[]{:S(2)}) collective-permute-start(bf16[208,512]{1,0:T(8,128)(2,1)S(1)} %get-tuple-element.125), channel_id=1, source_target_pairs={{0,18},{16,0},{2,16},{18,2},{1,19},{17,1},{3,17},{19,3},{4,22},{20... | collective-permute-start | bytes 638984 | tf_op jit(solution)/shard_map/ppermute | solution.py:26
  17.0 7.9 %collective-permute-start.2 = (bf16[208,512]{1,0:T(8,128)(2,1)S(1)}, bf16[208,512]{1,0:T(8,128)(2,1)S(1)}, u32[]{:S(2)}, u32[]{:S(2)}) collective-permute-start(bf16[208,512]{1,0:T(8,128)(2,1)S(1)} %get-tuple-element.127), channel_id=1, source_target_pairs={{0,32},{32,64},{64,96},{96,0},{1,33},{33,65},{65,97},{97,1},{2,34}... | collective-permute-start | bytes 638984 | tf_op jit(solution)/shard_map/ppermute | solution.py:27
  18.3 7.8 %collective-permute-start.1 = (bf16[208,512]{1,0:T(8,128)(2,1)S(1)}, bf16[208,512]{1,0:T(8,128)(2,1)S(1)}, u32[]{:S(2)}, u32[]{:S(2)}) collective-permute-start(bf16[208,512]{1,0:T(8,128)(2,1)S(1)} %get-tuple-element.127), channel_id=1, source_target_pairs={{0,96},{32,0},{64,32},{96,64},{1,97},{33,1},{65,33},{97,65},{2,98}... | collective-permute-start | bytes 638984 | tf_op jit(solution)/shard_map/ppermute | solution.py:27
  19.7 10.5 %collective-permute-start.5 = (f32[1024]{0:T(1024)S(1)}, f32[1024]{0:T(1024)S(1)}, u32[]{:S(2)}, u32[]{:S(2)}) collective-permute-start(f32[1024]{0:T(1024)S(1)} %copy-done.28), channel_id=1, source_target_pairs={{0,16},{16,0},{1,17},{17,1},{2,18},{18,2},{3,19},{19,3},{4,20},{20... | collective-permute-start | bytes 12296 | tf_op jit(solution)/shard_map/ppermute | solution.py:408
  22.0 9.7 %collective-permute-start.13 = (bf16[104,512]{1,0:T(8,128)(2,1)S(1)}, bf16[104,512]{1,0:T(8,128)(2,1)S(1)}, u32[]{:S(2)}, u32[]{:S(2)}) collective-permute-start(bf16[104,512]{1,0:T(8,128)(2,1)S(1)} %slice.56), channel_id=1, source_target_pairs={{0,16},{16,2},{2,18},{18,0},{1,17},{17,3},{3,19},{19,1},{4,20},{20... | collective-permute-start | bytes 319496 | tf_op jit(solution)/shard_map/ppermute | solution.py:26
  22.1 9.6 %collective-permute-start.14 = (bf16[104,512]{1,0:T(8,128)(2,1)S(1)}, bf16[104,512]{1,0:T(8,128)(2,1)S(1)}, u32[]{:S(2)}, u32[]{:S(2)}) collective-permute-start(bf16[104,512]{1,0:T(8,128)(2,1)S(1)} %slice.57), channel_id=1, source_target_pairs={{0,18},{16,0},{2,16},{18,2},{1,19},{17,1},{3,17},{19,3},{4,22},{20... | collective-permute-start | bytes 319496 | tf_op jit(solution)/shard_map/ppermute | solution.py:26
  24.9 5.2 %collective-permute-start.3 = (bf16[104,512]{1,0:T(8,128)(2,1)S(1)}, bf16[104,512]{1,0:T(8,128)(2,1)S(1)}, u32[]{:S(2)}, u32[]{:S(2)}) collective-permute-start(bf16[104,512]{1,0:T(8,128)(2,1)S(1)} %slice.52), channel_id=1, source_target_pairs={{0,32},{32,64},{64,96},{96,0},{1,33},{33,65},{65,97},{97,1},{2,34}... | collective-permute-start | bytes 319496 | tf_op jit(solution)/shard_map/ppermute | solution.py:27
  26.1 4.0 %collective-permute-start.4 = (bf16[104,512]{1,0:T(8,128)(2,1)S(1)}, bf16[104,512]{1,0:T(8,128)(2,1)S(1)}, u32[]{:S(2)}, u32[]{:S(2)}) collective-permute-start(bf16[104,512]{1,0:T(8,128)(2,1)S(1)} %slice.53), channel_id=1, source_target_pairs={{0,96},{32,0},{64,32},{96,64},{1,97},{33,1},{65,33},{97,65},{2,98}... | collective-permute-start | bytes 319496 | tf_op jit(solution)/shard_map/ppermute | solution.py:27
  27.8 42.3 %copy-start.26 = (f32[1664]{0:T(1024)S(1)}, f32[1664]{0:T(1024)}, u32[]{:S(2)}) copy-start(f32[1664]{0:T(1024)} %param.9) | copy-start | bytes 19972
  27.8 42.3 %copy-start.27 = (f32[1664]{0:T(1024)S(1)}, f32[1664]{0:T(1024)}, u32[]{:S(2)}) copy-start(f32[1664]{0:T(1024)} %param.10) | copy-start | bytes 19972
  30.2 28.7 %copy-start.19 = (bf16[832,512]{1,0:T(8,128)(2,1)}, bf16[832,512]{1,0:T(8,128)(2,1)S(1)}, u32[]{:S(2)}) copy-start(bf16[832,512]{1,0:T(8,128)(2,1)S(1)} %constant_dynamic-update-slice_fusion.refs_0_) | copy-start | bytes 2555908
  30.2 17.9 %collective-permute-start.8 = (bf16[832,512]{1,0:T(8,128)(2,1)S(1)}, bf16[832,512]{1,0:T(8,128)(2,1)S(1)}, u32[]{:S(2)}, u32[]{:S(2)}) collective-permute-start(bf16[832,512]{1,0:T(8,128)(2,1)S(1)} %constant_dynamic-update-slice_fusion.refs_0_), channel_id=1, source_target_pairs={{0,18},{16,0},{2,16},{18,2},{1,19},{17,1},{3,17},{19,3},{4,22},{20... | collective-permute-start | bytes 2555912 | tf_op jit(solution)/shard_map/ppermute | solution.py:26
  30.8 19.2 %collective-permute-start.6 = (bf16[832,512]{1,0:T(8,128)(2,1)S(1)}, bf16[832,512]{1,0:T(8,128)(2,1)S(1)}, u32[]{:S(2)}, u32[]{:S(2)}) collective-permute-start(bf16[832,512]{1,0:T(8,128)(2,1)S(1)} %constant_dynamic-update-slice_fusion.refs_0_), channel_id=1, source_target_pairs={{0,16},{16,2},{2,18},{18,0},{1,17},{17,3},{3,19},{19,1},{4,20},{20... | collective-permute-start | bytes 2555912 | tf_op jit(solution)/shard_map/ppermute | solution.py:26
  31.8 21.5 %copy-start.17 = (bf16[832,512]{1,0:T(8,128)(2,1)}, bf16[832,512]{1,0:T(8,128)(2,1)S(1)}, u32[]{:S(2)}) copy-start(bf16[832,512]{1,0:T(8,128)(2,1)S(1)} %constant_dynamic-update-slice_fusion.5.refs_0_) | copy-start | bytes 2555908
  31.8 18.3 %collective-permute-start.17 = (bf16[832,512]{1,0:T(8,128)(2,1)S(1)}, bf16[832,512]{1,0:T(8,128)(2,1)S(1)}, u32[]{:S(2)}, u32[]{:S(2)}) collective-permute-start(bf16[832,512]{1,0:T(8,128)(2,1)S(1)} %constant_dynamic-update-slice_fusion.5.refs_0_), channel_id=1, source_target_pairs={{0,96},{32,0},{64,32},{96,64},{1,97},{33,1},{65,33},{97,65},{2,98}... | collective-permute-start | bytes 2555912 | tf_op jit(solution)/shard_map/ppermute | solution.py:27
  34.6 18.7 %collective-permute-start.15 = (bf16[832,512]{1,0:T(8,128)(2,1)S(1)}, bf16[832,512]{1,0:T(8,128)(2,1)S(1)}, u32[]{:S(2)}, u32[]{:S(2)}) collective-permute-start(bf16[832,512]{1,0:T(8,128)(2,1)S(1)} %constant_dynamic-update-slice_fusion.5.refs_0_), channel_id=1, source_target_pairs={{0,32},{32,64},{64,96},{96,0},{1,33},{33,65},{65,97},{97,1},{2,34}... | collective-permute-start | bytes 2555912 | tf_op jit(solution)/shard_map/ppermute | solution.py:27
  48.2 8.3 %collective-permute-start.9 = (bf16[416,512]{1,0:T(8,128)(2,1)S(1)}, bf16[416,512]{1,0:T(8,128)(2,1)S(1)}, u32[]{:S(2)}, u32[]{:S(2)}) collective-permute-start(bf16[416,512]{1,0:T(8,128)(2,1)S(1)} %slice.55), channel_id=1, source_target_pairs={{0,18},{16,0},{2,16},{18,2},{1,19},{17,1},{3,17},{19,3},{4,22},{20... | collective-permute-start | bytes 1277960 | tf_op jit(solution)/shard_map/ppermute | solution.py:26
  50.0 8.9 %collective-permute-start.7 = (bf16[416,512]{1,0:T(8,128)(2,1)S(1)}, bf16[416,512]{1,0:T(8,128)(2,1)S(1)}, u32[]{:S(2)}, u32[]{:S(2)}) collective-permute-start(bf16[416,512]{1,0:T(8,128)(2,1)S(1)} %slice.54), channel_id=1, source_target_pairs={{0,16},{16,2},{2,18},{18,0},{1,17},{17,3},{3,19},{19,1},{4,20},{20... | collective-permute-start | bytes 1277960 | tf_op jit(solution)/shard_map/ppermute | solution.py:26
  50.1 8.8 %collective-permute-start.18 = (bf16[416,512]{1,0:T(8,128)(2,1)S(1)}, bf16[416,512]{1,0:T(8,128)(2,1)S(1)}, u32[]{:S(2)}, u32[]{:S(2)}) collective-permute-start(bf16[416,512]{1,0:T(8,128)(2,1)S(1)} %slice.59), channel_id=1, source_target_pairs={{0,96},{32,0},{64,32},{96,64},{1,97},{33,1},{65,33},{97,65},{2,98}... | collective-permute-start | bytes 1277960 | tf_op jit(solution)/shard_map/ppermute | solution.py:27
  53.3 8.7 %collective-permute-start.16 = (bf16[416,512]{1,0:T(8,128)(2,1)S(1)}, bf16[416,512]{1,0:T(8,128)(2,1)S(1)}, u32[]{:S(2)}, u32[]{:S(2)}) collective-permute-start(bf16[416,512]{1,0:T(8,128)(2,1)S(1)} %slice.58), channel_id=1, source_target_pairs={{0,32},{32,64},{64,96},{96,0},{1,33},{33,65},{65,97},{97,1},{2,34}... | collective-permute-start | bytes 1277960 | tf_op jit(solution)/shard_map/ppermute | solution.py:27
  65.0 23.3 %collective-permute-start.19 = (bf16[4,2,160,1664]{3,2,1,0:T(8,128)(2,1)}, bf16[4,2,160,1664]{3,2,1,0:T(8,128)(2,1)}, u32[]{:S(2)}, u32[]{:S(2)}) collective-permute-start(bf16[4,2,160,1664]{3,2,1,0:T(8,128)(2,1)} %all-gather.2.cloned.1.call-done.refs_0_), channel_id=1, source_target_pairs={{0,1},{1,0},{2,3},{3,2},{4,5},{5,4},{6,7},{7,6},{8,9},{9,8},{10,11... | collective-permute-start | bytes 12779528 | tf_op jit(solution)/shard_map/ppermute | solution.py:31
  70.2 2.2 %copy-start = (bf16[4,2,160,1664]{3,2,1,0:T(8,128)(2,1)S(1)}, bf16[4,2,160,1664]{3,2,1,0:T(8,128)(2,1)}, u32[]{:S(2)}) copy-start(bf16[4,2,160,1664]{3,2,1,0:T(8,128)(2,1)} %all-gather.2.cloned.1.call-done.refs_0_) | copy-start | bytes 12779524
  72.4 8.5 %slice-start = ((s8[4259840]{0:T(1024)(128)(4,1)}), s8[4194304]{0:T(1024)(128)(4,1)S(1)}, s32[]{:S(2)}) async-start(s8[4259840]{0:T(1024)(128)(4,1)} %bitcast.15), calls=%async_computation.3 | async-start | bytes 8388608
  78.1 1.2 copy-start.20
  79.2 1.1 copy-start.14
  79.2 1.4 copy-start.18
  79.2 1.7 slice-start.1
  110.2 8.9 %collective-permute-start.20 = (bf16[640,1664]{1,0:T(8,128)(2,1)S(1)}, bf16[640,1664]{1,0:T(8,128)(2,1)S(1)}, u32[]{:S(2)}, u32[]{:S(2)}) collective-permute-start(bf16[640,1664]{1,0:T(8,128)(2,1)S(1)} %get-tuple-element.81), channel_id=1, source_target_pairs={{0,1},{1,0},{2,3},{3,2},{4,5},{5,4},{6,7},{7,6},{8,9},{9,8},{10,11... | collective-permute-start | bytes 6389768 | tf_op jit(solution)/shard_map/ppermute | solution.py:31
  113.6 17.3 %collective-permute-start.21 = (bf16[240,1024]{1,0:T(8,128)(2,1)S(1)}, bf16[240,1024]{1,0:T(8,128)(2,1)S(1)}, u32[]{:S(2)}, u32[]{:S(2)}) collective-permute-start(bf16[240,1024]{1,0:T(8,128)(2,1)S(1)} %get-tuple-element.93), channel_id=1, source_target_pairs={{0,32},{32,64},{64,96},{96,0},{1,33},{33,65},{65,97},{97,1},{2,34}... | collective-permute-start | bytes 1474568 | tf_op jit(solution)/shard_map/ppermute | solution.py:27
  113.7 17.2 %collective-permute-start.22 = (bf16[240,1024]{1,0:T(8,128)(2,1)S(1)}, bf16[240,1024]{1,0:T(8,128)(2,1)S(1)}, u32[]{:S(2)}, u32[]{:S(2)}) collective-permute-start(bf16[240,1024]{1,0:T(8,128)(2,1)S(1)} %get-tuple-element.94), channel_id=1, source_target_pairs={{0,96},{32,0},{64,32},{96,64},{1,97},{33,1},{65,33},{97,65},{2,98}... | collective-permute-start | bytes 1474568 | tf_op jit(solution)/shard_map/ppermute | solution.py:27
  116.4 14.5 %collective-permute-start.23 = (bf16[416,512]{1,0:T(8,128)(2,1)S(1)}, bf16[416,512]{1,0:T(8,128)(2,1)S(1)}, u32[]{:S(2)}, u32[]{:S(2)}) collective-permute-start(bf16[416,512]{1,0:T(8,128)(2,1)S(1)} %get-tuple-element.95), channel_id=1, source_target_pairs={{0,16},{16,2},{2,18},{18,0},{1,17},{17,3},{3,19},{19,1},{4,20},{20... | collective-permute-start | bytes 1277960 | tf_op jit(solution)/shard_map/ppermute | solution.py:26
  116.5 14.4 %collective-permute-start.24 = (bf16[416,512]{1,0:T(8,128)(2,1)S(1)}, bf16[416,512]{1,0:T(8,128)(2,1)S(1)}, u32[]{:S(2)}, u32[]{:S(2)}) collective-permute-start(bf16[416,512]{1,0:T(8,128)(2,1)S(1)} %get-tuple-element.96), channel_id=1, source_target_pairs={{0,18},{16,0},{2,16},{18,2},{1,19},{17,1},{3,17},{19,3},{4,22},{20... | collective-permute-start | bytes 1277960 | tf_op jit(solution)/shard_map/ppermute | solution.py:26
  130.9 1.2 copy-start.5
  130.9 1.8 copy-start.15
  135.6 21.6 %collective-permute-start.25 = (bf16[448,1024]{1,0:T(8,128)(2,1)S(1)}, bf16[448,1024]{1,0:T(8,128)(2,1)S(1)}, u32[]{:S(2)}, u32[]{:S(2)}) collective-permute-start(bf16[448,1024]{1,0:T(8,128)(2,1)S(1)} %get-tuple-element.101), channel_id=1, source_target_pairs={{0,32},{32,64},{64,96},{96,0},{1,33},{33,65},{65,97},{97,1},{2,34}... | collective-permute-start | bytes 2752520 | tf_op jit(solution)/shard_map/ppermute | solution.py:27
  135.7 19.3 %collective-permute-start.26 = (bf16[416,1024]{1,0:T(8,128)(2,1)}, bf16[416,1024]{1,0:T(8,128)(2,1)S(1)}, u32[]{:S(2)}, u32[]{:S(2)}) collective-permute-start(bf16[416,1024]{1,0:T(8,128)(2,1)} %copy-done.24), channel_id=1, source_target_pairs={{0,96},{32,0},{64,32},{96,64},{1,97},{33,1},{65,33},{97,65},{2,98}... | collective-permute-start | bytes 2555912 | tf_op jit(solution)/shard_map/ppermute | solution.py:27
  138.3 24.7 %collective-permute-start.30 = (bf16[832,512]{1,0:T(8,128)(2,1)}, bf16[832,512]{1,0:T(8,128)(2,1)S(1)}, u32[]{:S(2)}, u32[]{:S(2)}) collective-permute-start(bf16[832,512]{1,0:T(8,128)(2,1)} %copy-done.23), channel_id=1, source_target_pairs={{0,16},{16,2},{2,18},{18,0},{1,17},{17,3},{3,19},{19,1},{4,20},{20... | collective-permute-start | bytes 2555912 | tf_op jit(solution)/shard_map/ppermute | solution.py:26
  138.3 24.7 %collective-permute-start.31 = (bf16[832,512]{1,0:T(8,128)(2,1)}, bf16[832,512]{1,0:T(8,128)(2,1)S(1)}, u32[]{:S(2)}, u32[]{:S(2)}) collective-permute-start(bf16[832,512]{1,0:T(8,128)(2,1)} %copy-done.22), channel_id=1, source_target_pairs={{0,18},{16,0},{2,16},{18,2},{1,19},{17,1},{3,17},{19,3},{4,22},{20... | collective-permute-start | bytes 2555912 | tf_op jit(solution)/shard_map/ppermute | solution.py:26
  157.2 1.5 copy-start.6
  158.7 4.3 %copy-start.16 = (f32[832,512]{1,0:T(8,128)S(1)}, f32[832,512]{1,0:T(8,128)}, u32[]{:S(2)}) copy-start(f32[832,512]{1,0:T(8,128)} %copy-done.15) | copy-start | bytes 5111812
  158.7 7.7 %copy-start.2 = (bf16[160,1664]{1,0:T(8,128)(2,1)S(1)}, bf16[160,1664]{1,0:T(8,128)(2,1)}, u32[]{:S(2)}) copy-start(bf16[160,1664]{1,0:T(8,128)(2,1)} %refs_0_.3) | copy-start | bytes 1597444
  158.7 7.7 %copy-start.4 = (bf16[160,1664]{1,0:T(8,128)(2,1)S(1)}, bf16[160,1664]{1,0:T(8,128)(2,1)}, u32[]{:S(2)}) copy-start(bf16[160,1664]{1,0:T(8,128)(2,1)} %refs_1_.3) | copy-start | bytes 1597444
  159.9 13.5 %collective-permute-start.27 = (bf16[240,512]{1,0:T(8,128)(2,1)}, bf16[240,512]{1,0:T(8,128)(2,1)S(1)}, u32[]{:S(2)}, u32[]{:S(2)}) collective-permute-start(bf16[240,512]{1,0:T(8,128)(2,1)} %get-tuple-element.105), channel_id=1, source_target_pairs={{0,16},{16,2},{2,18},{18,0},{1,17},{17,3},{3,19},{19,1},{4,20},{20... | collective-permute-start | bytes 737288 | tf_op jit(solution)/shard_map/ppermute | solution.py:26
  159.9 13.5 %collective-permute-start.28 = (bf16[240,512]{1,0:T(8,128)(2,1)}, bf16[240,512]{1,0:T(8,128)(2,1)S(1)}, u32[]{:S(2)}, u32[]{:S(2)}) collective-permute-start(bf16[240,512]{1,0:T(8,128)(2,1)} %get-tuple-element.106), channel_id=1, source_target_pairs={{0,2},{16,18},{2,0},{18,16},{1,3},{17,19},{3,1},{19,17},{4,6},{20,... | collective-permute-start | bytes 737288 | tf_op jit(solution)/shard_map/ppermute | solution.py:26
  162.2 11.3 %collective-permute-start.29 = (bf16[240,512]{1,0:T(8,128)(2,1)}, bf16[240,512]{1,0:T(8,128)(2,1)S(1)}, u32[]{:S(2)}, u32[]{:S(2)}) collective-permute-start(bf16[240,512]{1,0:T(8,128)(2,1)} %get-tuple-element.107), channel_id=1, source_target_pairs={{0,18},{16,0},{2,16},{18,2},{1,19},{17,1},{3,17},{19,3},{4,22},{20... | collective-permute-start | bytes 737288 | tf_op jit(solution)/shard_map/ppermute | solution.py:26
  164.0 8.3 %collective-permute-start.32 = (bf16[208,512]{1,0:T(8,128)(2,1)}, bf16[208,512]{1,0:T(8,128)(2,1)S(1)}, u32[]{:S(2)}, u32[]{:S(2)}) collective-permute-start(bf16[208,512]{1,0:T(8,128)(2,1)} %get-tuple-element.113), channel_id=1, source_target_pairs={{0,32},{32,64},{64,96},{96,0},{1,33},{33,65},{65,97},{97,1},{2,34}... | collective-permute-start | bytes 638984 | tf_op jit(solution)/shard_map/ppermute | solution.py:27
  164.0 9.3 %collective-permute-start.33 = (bf16[208,512]{1,0:T(8,128)(2,1)}, bf16[208,512]{1,0:T(8,128)(2,1)S(1)}, u32[]{:S(2)}, u32[]{:S(2)}) collective-permute-start(bf16[208,512]{1,0:T(8,128)(2,1)} %get-tuple-element.114), channel_id=1, source_target_pairs={{0,64},{32,96},{64,0},{96,32},{1,65},{33,97},{65,1},{97,33},{2,66}... | collective-permute-start | bytes 638984 | tf_op jit(solution)/shard_map/ppermute | solution.py:27
  166.4 1.0 copy-start.21
  173.6 3.0 %collective-permute-start.34 = (f32[8,512]{1,0:T(8,128)S(1)}, f32[8,512]{1,0:T(8,128)S(1)}, u32[]{:S(2)}, u32[]{:S(2)}) collective-permute-start(f32[8,512]{1,0:T(8,128)S(1)} %slice.47), channel_id=1, source_target_pairs={{0,4},{4,0},{8,12},{12,8},{1,5},{5,1},{9,13},{13,9},{2,6},{6,2},{1... | collective-permute-start | bytes 49160 | tf_op jit(solution)/shard_map/ppermute | solution.py:44
  175.1 10.5 %collective-permute-start.37 = (bf16[208,512]{1,0:T(8,128)(2,1)S(1)}, bf16[208,512]{1,0:T(8,128)(2,1)S(1)}, u32[]{:S(2)}, u32[]{:S(2)}) collective-permute-start(bf16[208,512]{1,0:T(8,128)(2,1)S(1)} %get-tuple-element.119), channel_id=1, source_target_pairs={{0,96},{32,0},{64,32},{96,64},{1,97},{33,1},{65,33},{97,65},{2,98}... | collective-permute-start | bytes 638984 | tf_op jit(solution)/shard_map/ppermute | solution.py:27
  176.6 9.6 %collective-permute-start.35 = (f32[8,512]{1,0:T(8,128)S(1)}, f32[8,512]{1,0:T(8,128)S(1)}, u32[]{:S(2)}, u32[]{:S(2)}) collective-permute-start(f32[8,512]{1,0:T(8,128)S(1)} %slice_add_fusion), channel_id=1, source_target_pairs={{0,8},{4,12},{8,0},{12,4},{1,9},{5,13},{9,1},{13,5},{2,10},{6,14},... | collective-permute-start | bytes 49160 | tf_op jit(solution)/shard_map/ppermute | solution.py:44
  180.1 7.1 %collective-permute-start.39 = (f32[512]{0:T(512)S(1)}, f32[512]{0:T(512)S(1)}, u32[]{:S(2)}, u32[]{:S(2)}) collective-permute-start(f32[512]{0:T(512)S(1)} %bitcast.19), channel_id=1, source_target_pairs={{0,1},{1,0},{2,3},{3,2},{4,5},{5,4},{6,7},{7,6},{8,9},{9,8},{10,11... | collective-permute-start | bytes 6152 | tf_op jit(solution)/shard_map/ppermute | solution.py:31
  185.6 3.7 %collective-permute-start.38 = (f32[104,512]{1,0:T(8,128)S(1)}, f32[104,512]{1,0:T(8,128)S(1)}, u32[]{:S(2)}, u32[]{:S(2)}) collective-permute-start(f32[104,512]{1,0:T(8,128)S(1)} %get-tuple-element.121), channel_id=1, source_target_pairs={{0,1},{1,0},{2,3},{3,2},{4,5},{5,4},{6,7},{7,6},{8,9},{9,8},{10,11... | collective-permute-start | bytes 638984 | tf_op jit(solution)/shard_map/ppermute | solution.py:31
  185.8 4.3 %collective-permute-start.40 = (f32[104,512]{1,0:T(8,128)S(1)}, f32[104,512]{1,0:T(8,128)S(1)}, u32[]{:S(2)}, u32[]{:S(2)}) collective-permute-start(f32[104,512]{1,0:T(8,128)S(1)} %get-tuple-element.123), channel_id=1, source_target_pairs={{0,1},{1,0},{2,3},{3,2},{4,5},{5,4},{6,7},{7,6},{8,9},{9,8},{10,11... | collective-permute-start | bytes 638984 | tf_op jit(solution)/shard_map/ppermute | solution.py:31
  186.2 1.9 collective-permute-start.36
  (10 other events, 9.0 us)
Sparse Core Ops, SparseCore 0:
  10.5 52.2 all-gather.1
  135.7 29.3 reduce-scatter.1

commit v2 on v1

--- a/solution.py
+++ b/solution.py
@@ -110,10 +110,6 @@
 def stack_kernel(inputs, upstream, stacked):
     stacked[0, 0] = inputs[...]
     stacked[0, 1] = upstream[...]
-
-
-def nothing_kernel(*refs):
-    pass
 
 
 def add_kernel(mine, others, total):
@@ -425,27 +421,24 @@
     bias_both = jnp.where(ylo == 0, jnp.stack([expand_bias, bias_near]), jnp.stack([bias_near, expand_bias]))
     bias_own = lax.dynamic_slice_in_dim(bias_both, core * half, half, 1).reshape(1, 2 * half)
 
-    (mark,) = call(nothing_kernel, [], (a_low, a_high, b_low, b_high), mark=True)
-    near, mark = lax.optimization_barrier((near, mark))
+    (expand_all, first_mark), (shrink_all, second_mark) = (
+        call(functools.partial(assemble_kernel, first), [((width, 2 * half), bf16)], part, mark=True)
+        for first, part in zip("xy", pieces, strict=True)
+    )
+    near, first_mark, second_mark = lax.optimization_barrier((near, first_mark, second_mark))
     other = swap(near)
     many = 8 * tokens
     tall, wide = ((width, many), bf16), ((many, 2 * half), bf16)
     column, half_tall, bias_row = ((4 * tokens, 1), f32), (4 * tokens, width), ((1, 2 * half), f32)
-    weight = ((width, 2 * half), bf16)
     gain, shift_by = norm_gain[None], norm_shift[None]
     tile = pltpu.VMEM((2, 4 * tokens, 256), f32)
     turned = pltpu.VMEM((width, 4 * tokens), bf16)
-    normed, near_centre, near_scale, normed_t, up_t, mark = call(
+    normed, near_centre, near_scale, normed_t, up_t = call(
         functools.partial(norm_kernel, 0),
         [(half_tall, bf16), column, column, tall, tall],
         (near, gain, shift_by),
         scratch=[turned],
-        behind=(mark,),
-        mark=True,
-    )
-    expand_all, shrink_all = (
-        call(functools.partial(assemble_kernel, first), [weight], part, behind=(mark,))[0]
-        for first, part in zip("xy", pieces, strict=True)
+        behind=(first_mark, second_mark),
     )
     near_bias, active, back = call(
         functools.partial(hidden_kernel, 0),

time: 198 us -> 193 us (0.975)
  local copies, waits for them, and re-layouts: 20.6 us -> 17 us
  waiting for transfers between devices: 48.7 us -> 46 us
    unnamed x72 -> x50, local copies, waits for them, and re-layouts: 19.4 us -> 15.8 us
    pallas_call x18 -> x17, Pallas kernels: 55 us -> 55 us  [call(): pl.pallas_call(body, out_shape=[jax.ShapeDtypeStruct(shape, dtype) for sh...]
  transfers between devices with their start and end apart: 43 -> 43, of which waited for: 14 -> 13; matrix products, arithmetic and copies ran while one was open for 2% -> 2% of each run, Pallas kernels for 16% -> 16%
where the time goes in v2:
time: 193 us; the launch traced here: 192 us
  starting transfers between devices  57.5 us (30%)
  Pallas kernels  55 us (28%)
  waiting for transfers between devices  46 us (24%)
  local copies, waits for them, and re-layouts  17 us (9%)
  between operations  14.5 us (8%)
  other arithmetic  2.39 us (1%)
    pallas_call x17, Pallas kernels, call(): pl.pallas_call(body, out_shape=[jax.ShapeDtypeStruct(shape, dtype) for sh...  55 us
    ppermute x15, waiting for transfers between devices, shift(): return lax.ppermute(value, axis, [(i, (i + by) % 4) for i in range(4)])  24.5 us
    ppermute x15, starting transfers between devices, shift(): return lax.ppermute(value, axis, [(i, (i + by) % 4) for i in range(4)])  20.2 us
    ppermute x15, waiting for transfers between devices, shift(): return lax.ppermute(value, PLANE_Y, pairs)  19.5 us
    ppermute x15, starting transfers between devices, shift(): return lax.ppermute(value, PLANE_Y, pairs)  19.3 us
    unnamed x50, local copies, waits for them, and re-layouts  15.8 us
    ppermute x8, starting transfers between devices, swap(): return lax.ppermute(value, 'core', [(0, 1), (1, 0)])  13.4 us
    ppermute x2, starting transfers between devices, pair_sum(): value = value + lax.ppermute(value, axis, [(i, i ^ bit) for i in range(4)])  4.52 us
  transfers between devices with their start and end apart: 43, of which 13 were waited for; matrix products, arithmetic and copies ran while one was open for 2% of the time, Pallas kernels for 16%

profile of v2, /device:TPU:1, one launch (start us, length us, event | category | flops | bytes accessed | tf_op | source)
XLA Modules:
  0.0 192.5 jit_solution(16456046001665602089)
XLA Ops:
  7.2 1.0 copy-done.4
  8.3 1.0 copy-done.6
  9.3 1.1 shard_map.118
  10.5 1.0 constant_dynamic-slice_fusion.1
  11.4 1.5 collective-permute-start.10
  13.1 0.8 collective-permute-done.10
  13.9 1.4 collective-permute-start.12
  15.4 1.5 collective-permute-start.11
  17.0 1.3 collective-permute-start.2
  18.2 1.5 collective-permute-start.1
  19.7 2.3 %collective-permute-done.12 = bf16[208,512]{1,0:T(8,128)(2,1)S(1)} collective-permute-done((bf16[208,512]{1,0:T(8,128)(2,1)S(1)}, bf16[208,512]{1,0:T(8,128)(2,1)S(1)}, u32[]{:S(2)}, u32[]{:S(2)}) %collective-permute-start.12) | collective-permute-done | bytes 213024 | tf_op jit(solution)/shard_map/ppermute | solution.py:26
  22.1 2.7 %collective-permute-start.14 = (bf16[104,512]{1,0:T(8,128)(2,1)S(1)}, bf16[104,512]{1,0:T(8,128)(2,1)S(1)}, u32[]{:S(2)}, u32[]{:S(2)}) collective-permute-start(bf16[104,512]{1,0:T(8,128)(2,1)S(1)} %slice.57), channel_id=1, source_target_pairs={{0,18},{16,0},{2,16},{18,2},{1,19},{17,1},{3,17},{19,3},{4,22},{20... | collective-permute-start | bytes 319496 | tf_op jit(solution)/shard_map/ppermute | solution.py:26
  24.9 1.2 collective-permute-start.3
  26.1 1.6 collective-permute-start.4
  27.7 2.4 %collective-permute-done.3 = bf16[104,512]{1,0:T(8,128)(2,1)S(1)} collective-permute-done((bf16[104,512]{1,0:T(8,128)(2,1)S(1)}, bf16[104,512]{1,0:T(8,128)(2,1)S(1)}, u32[]{:S(2)}, u32[]{:S(2)}) %collective-permute-start.3) | collective-permute-done | bytes 106528 | tf_op jit(solution)/shard_map/ppermute | solution.py:27
  30.3 2.7 %collective-permute-start.6 = (bf16[832,512]{1,0:T(8,128)(2,1)S(1)}, bf16[832,512]{1,0:T(8,128)(2,1)S(1)}, u32[]{:S(2)}, u32[]{:S(2)}) collective-permute-start(bf16[832,512]{1,0:T(8,128)(2,1)S(1)} %constant_dynamic-update-slice_fusion.refs_0_), channel_id=1, source_target_pairs={{0,18},{16,0},{2,16},{18,2},{1,19},{17,1},{3,17},{19,3},{4,22},{20... | collective-permute-start | bytes 2555912 | tf_op jit(solution)/shard_map/ppermute | solution.py:26
  33.0 1.2 collective-permute-start.16
  34.2 1.6 collective-permute-start.15
  35.9 13.5 %collective-permute-done.7.refs_4_ = bf16[832,512]{1,0:T(8,128)(2,1)S(1)} collective-permute-done((bf16[832,512]{1,0:T(8,128)(2,1)S(1)}, bf16[832,512]{1,0:T(8,128)(2,1)S(1)}, u32[]{:S(2)}, u32[]{:S(2)}) %collective-permute-start.7) | collective-permute-done | bytes 852000 | tf_op jit(solution)/shard_map/ppermute | solution.py:26
  49.5 2.7 %collective-permute-start.9 = (bf16[416,512]{1,0:T(8,128)(2,1)S(1)}, bf16[416,512]{1,0:T(8,128)(2,1)S(1)}, u32[]{:S(2)}, u32[]{:S(2)}) collective-permute-start(bf16[416,512]{1,0:T(8,128)(2,1)S(1)} %slice.55), channel_id=1, source_target_pairs={{0,18},{16,0},{2,16},{18,2},{1,19},{17,1},{3,17},{19,3},{4,22},{20... | collective-permute-start | bytes 1277960 | tf_op jit(solution)/shard_map/ppermute | solution.py:26
  52.3 1.2 collective-permute-start.17
  53.5 1.7 collective-permute-start.18
  55.3 3.3 %collective-permute-done.8.refs_2_ = bf16[416,512]{1,0:T(8,128)(2,1)S(1)} collective-permute-done((bf16[416,512]{1,0:T(8,128)(2,1)S(1)}, bf16[416,512]{1,0:T(8,128)(2,1)S(1)}, u32[]{:S(2)}, u32[]{:S(2)}) %collective-permute-start.8) | collective-permute-done | bytes 426016 | tf_op jit(solution)/shard_map/ppermute | solution.py:26
  58.9 2.3 %collective-permute-done.17.refs_2_ = bf16[416,512]{1,0:T(8,128)(2,1)S(1)} collective-permute-done((bf16[416,512]{1,0:T(8,128)(2,1)S(1)}, bf16[416,512]{1,0:T(8,128)(2,1)S(1)}, u32[]{:S(2)}, u32[]{:S(2)}) %collective-permute-start.17) | collective-permute-done | bytes 426016 | tf_op jit(solution)/shard_map/ppermute | solution.py:27
  61.4 1.8 copy-done.2
  63.2 4.9 %collective-permute-start.19 = (bf16[4,2,160,1664]{3,2,1,0:T(8,128)(2,1)}, bf16[4,2,160,1664]{3,2,1,0:T(8,128)(2,1)}, u32[]{:S(2)}, u32[]{:S(2)}) collective-permute-start(bf16[4,2,160,1664]{3,2,1,0:T(8,128)(2,1)} %all-gather.2.cloned.1.call-done.refs_0_), channel_id=1, source_target_pairs={{0,1},{1,0},{2,3},{3,2},{4,5},{5,4},{6,7},{7,6},{8,9},{9,8},{10,11... | collective-permute-start | bytes 12779528 | tf_op jit(solution)/shard_map/ppermute | solution.py:31
  68.3 2.2 %copy-done = bf16[4,2,160,1664]{3,2,1,0:T(8,128)(2,1)S(1)} copy-done((bf16[4,2,160,1664]{3,2,1,0:T(8,128)(2,1)S(1)}, bf16[4,2,160,1664]{3,2,1,0:T(8,128)(2,1)}, u32[]{:S(2)}) %copy-start) | copy-done | bytes 4259864
  70.5 3.6 %shard_map.121 = (bf16[640,1664]{1,0:T(8,128)(2,1)S(1)}, f32[640,1]{1,0:T(8,128)S(1)}, f32[640,1]{1,0:T(8,128)S(1)}, bf16[1664,1280]{1,0:T(8,128)(2,1)S(1)}, bf16[1664,1280]{1,0:T(8,128)(2,1)S(1)}) custom-call(bf16[4,2,160,1664]{3,2,1,0:T(8,128)(2,1)S(1)} %copy-done, f32[1,1664]{1,0:T(1,128)S(1)} %broadcast_in_dim.7.refs_1_.refs_3_, ...), custom_call_target="tpu_custom_call" | custom-call | flops 1000000 | bytes 1000000 | tf_op jit(solution)/shard_map/pallas_call | solution.py:98
  74.2 2.0 %copy-done.3 = bf16[1664,1024]{1,0:T(8,128)(2,1)S(1)} copy-done((bf16[1664,1024]{1,0:T(8,128)(2,1)S(1)}, bf16[1664,1024]{1,0:T(8,128)(2,1)}, u32[]{:S(2)}) %copy-start.3) | copy-done | bytes 3407896
  76.1 7.3 %shard_map.122 = (f32[1,1024]{1,0:T(1,128)S(1)}, bf16[1280,1024]{1,0:T(8,128)(2,1)S(1)}, bf16[1280,1024]{1,0:T(8,128)(2,1)S(1)}) custom-call(bf16[4,2,160,1664]{3,2,1,0:T(8,128)(2,1)S(1)} %copy-done.1, bf16[640,1664]{1,0:T(8,128)(2,1)S(1)} %get-tuple-element.81.refs_1_, bf16[1664,1024]{1,0:T(8,128)(2,1)S(1)} %get-tuple-element.77.refs_2_.refs_4_.refs_7_, ...), custom_call_target="tpu_custom_call" | custom-call | flops 1000000 | bytes 1000000 | tf_op jit(solution)/shard_map/pallas_call | solution.py:98
  83.5 13.0 %shard_map.123 = (f32[640,1]{1,0:T(8,128)S(1)}, f32[640,1]{1,0:T(8,128)S(1)}, bf16[1664,1280]{1,0:T(8,128)(2,1)S(1)}, bf16[1664,1280]{1,0:T(8,128)(2,1)S(1)}, f3...) custom-call(bf16[4,2,160,1664]{3,2,1,0:T(8,128)(2,1)} %collective-pe, ...), custom_call_target="tpu_custom_call", output_to_operand_aliasing={{2}: (6, {}), {3}: (7, {}), {5}: (8, {}), {6}: (9, {})} | custom-call | flops 1000000 | bytes 1000000 | tf_op jit(solution)/shard_map/pallas_call | solution.py:98
  96.5 8.9 %shard_map.124 = (f32[640,1664]{1,0:T(8,128)S(1)}, bf16[640,1664]{1,0:T(8,128)(2,1)S(1)}, f32[2,1664]{1,0:T(2,128)S(1)}) custom-call(bf16[4,2,160,1664]{3,2,1,0:T(8,128)(2,1)S(1)} %copy-done.1, bf16[4,2,160,1664]{3,2,1,0:T(8,128)(2,1)} %collective-permute-done.19.refs_0_.refs_1_, f32[640,1]{1,0:T(8,128)S(1)} %get-tuple-element.75.refs_2_, ...), custom_call_target="tpu_custom_call" | custom-call | flops 1000000 | bytes 1000000 | tf_op jit(solution)/shard_map/pallas_call | solution.py:98
  105.5 3.3 %shard_map.125 = (bf16[240,1024]{1,0:T(8,128)(2,1)S(1)}, bf16[240,1024]{1,0:T(8,128)(2,1)S(1)}, bf16[416,512]{1,0:T(8,128)(2,1)S(1)}, bf16[416,512]{1,0:T(8,128)(2,1)S(1)}, f32[16,1024]{1,0:T(8,128)S(1)}) custom-call(bf16[1664,1280]{1,0:T(8,128)(2,1)S(1)} %get-tuple-element.90.refs_0_, bf16[1280,1024]{1,0:T(8,128)(2,1)S(1)} %get-tuple-element.91.refs_1_, ...), custom_call_target="tpu_custom_call" | custom-call | flops 1000000 | bytes 1000000 | tf_op jit(solution)/shard_map/pallas_call | solution.py:98
  108.8 1.0 collective-permute-start.21
  109.8 1.9 collective-permute-start.22
  111.7 2.7 %collective-permute-start.24 = (bf16[416,512]{1,0:T(8,128)(2,1)S(1)}, bf16[416,512]{1,0:T(8,128)(2,1)S(1)}, u32[]{:S(2)}, u32[]{:S(2)}) collective-permute-start(bf16[416,512]{1,0:T(8,128)(2,1)S(1)} %get-tuple-element.104), channel_id=1, source_target_pairs={{0,18},{16,0},{2,16},{18,2},{1,19},{17,1},{3,17},{19,3},{4,22},{20... | collective-permute-start | bytes 1277960 | tf_op jit(solution)/shard_map/ppermute | solution.py:26
  114.4 1.8 shard_map.126
  116.2 10.0 %shard_map.127 = (f32[416,1024]{1,0:T(8,128)S(1)}, f32[832,512]{1,0:T(8,128)S(1)}, f32[2,416,1024]{2,1,0:T(8,128)S(1)}, f32[2,832,512]{2,1,0:T(8,128)S(1)}) custom-call(bf16[1664,1280]{1,0:T(8,128)(2,1)S(1)} %get-tuple-element.90.refs_0_, bf16[1280,1024]{1,0:T(8,128)(2,1)S(1)} %get-tuple-element.91.refs_1_, ...), custom_call_target="tpu_custom_call" | custom-call | flops 1000000 | bytes 1000000 | tf_op jit(solution)/shard_map/pallas_call | solution.py:98
  126.2 0.6 shard_map.128
  127.9 0.9 copy-done.13
  128.8 1.0 copy-done.14
  129.8 1.0 copy-done.15
  130.9 2.7 %collective-permute-start.26 = (bf16[416,1024]{1,0:T(8,128)(2,1)}, bf16[416,1024]{1,0:T(8,128)(2,1)S(1)}, u32[]{:S(2)}, u32[]{:S(2)}) collective-permute-start(bf16[416,1024]{1,0:T(8,128)(2,1)} %copy-done.15), channel_id=1, source_target_pairs={{0,96},{32,0},{64,32},{96,64},{1,97},{33,1},{65,33},{97,65},{2,98}... | collective-permute-start | bytes 2555912 | tf_op jit(solution)/shard_map/ppermute | solution.py:27
  133.5 2.7 %collective-permute-start.31 = (bf16[832,512]{1,0:T(8,128)(2,1)}, bf16[832,512]{1,0:T(8,128)(2,1)S(1)}, u32[]{:S(2)}, u32[]{:S(2)}) collective-permute-start(bf16[832,512]{1,0:T(8,128)(2,1)} %copy-done.13), channel_id=1, source_target_pairs={{0,18},{16,0},{2,16},{18,2},{1,19},{17,1},{3,17},{19,3},{4,22},{20... | collective-permute-start | bytes 2555912 | tf_op jit(solution)/shard_map/ppermute | solution.py:26
  136.2 14.1 %collective-permute-done.26.refs_2_ = bf16[416,1024]{1,0:T(8,128)(2,1)S(1)} collective-permute-done((bf16[416,1024]{1,0:T(8,128)(2,1)}, bf16[416,1024]{1,0:T(8,128)(2,1)S(1)}, u32[]{:S(2)}, u32[]{:S(2)}) %collective-permute-start.26) | collective-permute-done | bytes 852000 | tf_op jit(solution)/shard_map/ppermute | solution.py:27
  150.3 2.2 %collective-permute-done.25.refs_1_ = bf16[448,1024]{1,0:T(8,128)(2,1)S(1)} collective-permute-done((bf16[448,1024]{1,0:T(8,128)(2,1)S(1)}, bf16[448,1024]{1,0:T(8,128)(2,1)S(1)}, u32[]{:S(2)}, u32[]{:S(2)}) %collective-permute-start.25) | collective-permute-done | bytes 917536 | tf_op jit(solution)/shard_map/ppermute | solution.py:27
  152.5 1.5 copy-done.9
  154.0 1.1 shard_map.130
  155.2 1.5 collective-permute-start.28
  156.6 1.2 collective-permute-start.29
  157.9 1.0 shard_map.131
  158.9 2.4 %collective-permute-start.33 = (bf16[208,512]{1,0:T(8,128)(2,1)}, bf16[208,512]{1,0:T(8,128)(2,1)S(1)}, u32[]{:S(2)}, u32[]{:S(2)}) collective-permute-start(bf16[208,512]{1,0:T(8,128)(2,1)} %get-tuple-element.122), channel_id=1, source_target_pairs={{0,64},{32,96},{64,0},{96,32},{1,65},{33,97},{65,1},{97,33},{2,66}... | collective-permute-start | bytes 638984 | tf_op jit(solution)/shard_map/ppermute | solution.py:27
  161.3 1.0 copy-done.12
  162.3 2.4 %shard_map.129 = (bf16[160,1664]{1,0:T(8,128)(2,1)}, f32[8,128]{1,0:T(8,128)S(1)}) custom-call(bf16[160,1664]{1,0:T(8,128)(2,1)S(1)} %copy-done.5, bf16[160,1664]{1,0:T(8,128)(2,1)S(1)} %copy-done.7, bf16[160,1664]{1,0:T(8,128)(2,1)S(1)} %copy-done.12, f32[1,1664]{1,0:T(1,128)S(1)} %broadcast_in_dim.7.refs_1_.refs_3_), custom_call_target="tpu_custom_call" | custom-call | flops 1000000 | bytes 1000000 | tf_op jit(solution)/shard_map/pallas_call | solution.py:98
  164.7 2.4 %collective-permute-done.32.refs_1_ = bf16[208,512]{1,0:T(8,128)(2,1)S(1)} collective-permute-done((bf16[208,512]{1,0:T(8,128)(2,1)}, bf16[208,512]{1,0:T(8,128)(2,1)S(1)}, u32[]{:S(2)}, u32[]{:S(2)}) %collective-permute-start.32) | collective-permute-done | bytes 213024 | tf_op jit(solution)/shard_map/ppermute | solution.py:27
  167.1 1.2 collective-permute-done.33.refs_2_
  168.9 1.2 collective-permute-start.34
  170.1 0.9 collective-permute-start.37
  171.0 0.9 collective-permute-done.34
  171.9 3.3 %collective-permute-start.35 = (f32[8,512]{1,0:T(8,128)S(1)}, f32[8,512]{1,0:T(8,128)S(1)}, u32[]{:S(2)}, u32[]{:S(2)}) collective-permute-start(f32[8,512]{1,0:T(8,128)S(1)} %slice_add_fusion), channel_id=1, source_target_pairs={{0,8},{4,12},{8,0},{12,4},{1,9},{5,13},{9,1},{13,5},{2,10},{6,14},... | collective-permute-start | bytes 49160 | tf_op jit(solution)/shard_map/ppermute | solution.py:44
  175.2 5.1 %collective-permute-start.39 = (f32[512]{0:T(512)S(1)}, f32[512]{0:T(512)S(1)}, u32[]{:S(2)}, u32[]{:S(2)}) collective-permute-start(f32[512]{0:T(512)S(1)} %bitcast.17), channel_id=1, source_target_pairs={{0,1},{1,0},{2,3},{3,2},{4,5},{5,4},{6,7},{7,6},{8,9},{9,8},{10,11... | collective-permute-start | bytes 6152 | tf_op jit(solution)/shard_map/ppermute | solution.py:31
  180.9 1.1 collective-permute-start.36
  184.0 0.8 maximum_select_fusion
  184.8 0.8 maximum_select_fusion.1
  (117 shorter events, 6.1 us)
Async XLA Ops:
  7.2 56.1 %all-gather.2.cloned.1.call-start = ((), (), s32[]{:S(2)}) async-start(), calls=%async_computation.1 | async-start | bytes 5324800 | tf_op jit(solution)/shard_map/all_gather | solution.py:408
  7.2 1.0 copy-start.4
  8.3 1.0 copy-start.6
  9.3 3.6 %copy-start.16 = (bf16[104,1024]{1,0:T(8,128)(2,1)S(1)}, bf16[104,1024]{1,0:T(8,128)(2,1)}, u32[]{:S(2)}) copy-start(bf16[104,1024]{1,0:T(8,128)(2,1)} %param.11) | copy-start | bytes 638980
  9.3 10.4 %copy-start.19 = (f32[1024]{0:T(1024)S(1)}, f32[1024]{0:T(1024)}, u32[]{:S(2)}) copy-start(f32[1024]{0:T(1024)} %param.12) | copy-start | bytes 12292
  10.4 150.9 %reduce-scatter.2.cloned.1.call-start = ((), (), s32[]{:S(2)}) async-start(), calls=%async_computation.2 | async-start | bytes 2662400 | tf_op jit(solution)/shard_map/reduce_scatter | solution.py:490
  11.4 2.5 %collective-permute-start.10 = (bf16[104,512]{1,0:T(8,128)(2,1)S(1)}, bf16[104,512]{1,0:T(8,128)(2,1)S(1)}, u32[]{:S(2)}, u32[]{:S(2)}) collective-permute-start(bf16[104,512]{1,0:T(8,128)(2,1)S(1)} %get-tuple-element.136), channel_id=1, source_target_pairs={{0,1},{1,0},{2,3},{3,2},{4,5},{5,4},{6,7},{7,6},{8,9},{9,8},{10,11... | collective-permute-start | bytes 319496 | tf_op jit(solution)/shard_map/ppermute | solution.py:31
  13.0 4.0 %collective-permute-start = (bf16[104,512]{1,0:T(8,128)(2,1)S(1)}, bf16[104,512]{1,0:T(8,128)(2,1)S(1)}, u32[]{:S(2)}, u32[]{:S(2)}) collective-permute-start(bf16[104,512]{1,0:T(8,128)(2,1)S(1)} %get-tuple-element.138), channel_id=1, source_target_pairs={{0,1},{1,0},{2,3},{3,2},{4,5},{5,4},{6,7},{7,6},{8,9},{9,8},{10,11... | collective-permute-start | bytes 319496 | tf_op jit(solution)/shard_map/ppermute | solution.py:31
  13.9 8.1 %collective-permute-start.12 = (bf16[208,512]{1,0:T(8,128)(2,1)S(1)}, bf16[208,512]{1,0:T(8,128)(2,1)S(1)}, u32[]{:S(2)}, u32[]{:S(2)}) collective-permute-start(bf16[208,512]{1,0:T(8,128)(2,1)S(1)} %get-tuple-element.133), channel_id=1, source_target_pairs={{0,16},{16,2},{2,18},{18,0},{1,17},{17,3},{3,19},{19,1},{4,20},{20... | collective-permute-start | bytes 638984 | tf_op jit(solution)/shard_map/ppermute | solution.py:26
  15.4 6.7 %collective-permute-start.11 = (bf16[208,512]{1,0:T(8,128)(2,1)S(1)}, bf16[208,512]{1,0:T(8,128)(2,1)S(1)}, u32[]{:S(2)}, u32[]{:S(2)}) collective-permute-start(bf16[208,512]{1,0:T(8,128)(2,1)S(1)} %get-tuple-element.133), channel_id=1, source_target_pairs={{0,18},{16,0},{2,16},{18,2},{1,19},{17,1},{3,17},{19,3},{4,22},{20... | collective-permute-start | bytes 638984 | tf_op jit(solution)/shard_map/ppermute | solution.py:26
  17.0 7.9 %collective-permute-start.2 = (bf16[208,512]{1,0:T(8,128)(2,1)S(1)}, bf16[208,512]{1,0:T(8,128)(2,1)S(1)}, u32[]{:S(2)}, u32[]{:S(2)}) collective-permute-start(bf16[208,512]{1,0:T(8,128)(2,1)S(1)} %get-tuple-element.135), channel_id=1, source_target_pairs={{0,32},{32,64},{64,96},{96,0},{1,33},{33,65},{65,97},{97,1},{2,34}... | collective-permute-start | bytes 638984 | tf_op jit(solution)/shard_map/ppermute | solution.py:27
  18.2 7.8 %collective-permute-start.1 = (bf16[208,512]{1,0:T(8,128)(2,1)S(1)}, bf16[208,512]{1,0:T(8,128)(2,1)S(1)}, u32[]{:S(2)}, u32[]{:S(2)}) collective-permute-start(bf16[208,512]{1,0:T(8,128)(2,1)S(1)} %get-tuple-element.135), channel_id=1, source_target_pairs={{0,96},{32,0},{64,32},{96,64},{1,97},{33,1},{65,33},{97,65},{2,98}... | collective-permute-start | bytes 638984 | tf_op jit(solution)/shard_map/ppermute | solution.py:27
  19.7 10.5 %collective-permute-start.5 = (f32[1024]{0:T(1024)S(1)}, f32[1024]{0:T(1024)S(1)}, u32[]{:S(2)}, u32[]{:S(2)}) collective-permute-start(f32[1024]{0:T(1024)S(1)} %copy-done.19), channel_id=1, source_target_pairs={{0,16},{16,0},{1,17},{17,1},{2,18},{18,2},{3,19},{19,3},{4,20},{20... | collective-permute-start | bytes 12296 | tf_op jit(solution)/shard_map/ppermute | solution.py:404
  22.0 10.9 %collective-permute-start.13 = (bf16[104,512]{1,0:T(8,128)(2,1)S(1)}, bf16[104,512]{1,0:T(8,128)(2,1)S(1)}, u32[]{:S(2)}, u32[]{:S(2)}) collective-permute-start(bf16[104,512]{1,0:T(8,128)(2,1)S(1)} %slice.56), channel_id=1, source_target_pairs={{0,16},{16,2},{2,18},{18,0},{1,17},{17,3},{3,19},{19,1},{4,20},{20... | collective-permute-start | bytes 319496 | tf_op jit(solution)/shard_map/ppermute | solution.py:26
  22.1 10.8 %collective-permute-start.14 = (bf16[104,512]{1,0:T(8,128)(2,1)S(1)}, bf16[104,512]{1,0:T(8,128)(2,1)S(1)}, u32[]{:S(2)}, u32[]{:S(2)}) collective-permute-start(bf16[104,512]{1,0:T(8,128)(2,1)S(1)} %slice.57), channel_id=1, source_target_pairs={{0,18},{16,0},{2,16},{18,2},{1,19},{17,1},{3,17},{19,3},{4,22},{20... | collective-permute-start | bytes 319496 | tf_op jit(solution)/shard_map/ppermute | solution.py:26
  24.9 5.2 %collective-permute-start.3 = (bf16[104,512]{1,0:T(8,128)(2,1)S(1)}, bf16[104,512]{1,0:T(8,128)(2,1)S(1)}, u32[]{:S(2)}, u32[]{:S(2)}) collective-permute-start(bf16[104,512]{1,0:T(8,128)(2,1)S(1)} %slice.52), channel_id=1, source_target_pairs={{0,32},{32,64},{64,96},{96,0},{1,33},{33,65},{65,97},{97,1},{2,34}... | collective-permute-start | bytes 319496 | tf_op jit(solution)/shard_map/ppermute | solution.py:27
  26.1 4.0 %collective-permute-start.4 = (bf16[104,512]{1,0:T(8,128)(2,1)S(1)}, bf16[104,512]{1,0:T(8,128)(2,1)S(1)}, u32[]{:S(2)}, u32[]{:S(2)}) collective-permute-start(bf16[104,512]{1,0:T(8,128)(2,1)S(1)} %slice.53), channel_id=1, source_target_pairs={{0,96},{32,0},{64,32},{96,64},{1,97},{33,1},{65,33},{97,65},{2,98}... | collective-permute-start | bytes 319496 | tf_op jit(solution)/shard_map/ppermute | solution.py:27
  30.2 19.2 %collective-permute-start.7 = (bf16[832,512]{1,0:T(8,128)(2,1)S(1)}, bf16[832,512]{1,0:T(8,128)(2,1)S(1)}, u32[]{:S(2)}, u32[]{:S(2)}) collective-permute-start(bf16[832,512]{1,0:T(8,128)(2,1)S(1)} %constant_dynamic-update-slice_fusion.refs_0_), channel_id=1, source_target_pairs={{0,16},{16,2},{2,18},{18,0},{1,17},{17,3},{3,19},{19,1},{4,20},{20... | collective-permute-start | bytes 2555912 | tf_op jit(solution)/shard_map/ppermute | solution.py:26
  30.3 19.2 %collective-permute-start.6 = (bf16[832,512]{1,0:T(8,128)(2,1)S(1)}, bf16[832,512]{1,0:T(8,128)(2,1)S(1)}, u32[]{:S(2)}, u32[]{:S(2)}) collective-permute-start(bf16[832,512]{1,0:T(8,128)(2,1)S(1)} %constant_dynamic-update-slice_fusion.refs_0_), channel_id=1, source_target_pairs={{0,18},{16,0},{2,16},{18,2},{1,19},{17,1},{3,17},{19,3},{4,22},{20... | collective-permute-start | bytes 2555912 | tf_op jit(solution)/shard_map/ppermute | solution.py:26
  33.0 19.2 %collective-permute-start.16 = (bf16[832,512]{1,0:T(8,128)(2,1)S(1)}, bf16[832,512]{1,0:T(8,128)(2,1)S(1)}, u32[]{:S(2)}, u32[]{:S(2)}) collective-permute-start(bf16[832,512]{1,0:T(8,128)(2,1)S(1)} %constant_dynamic-update-slice_fusion.5.refs_0_), channel_id=1, source_target_pairs={{0,32},{32,64},{64,96},{96,0},{1,33},{33,65},{65,97},{97,1},{2,34}... | collective-permute-start | bytes 2555912 | tf_op jit(solution)/shard_map/ppermute | solution.py:27
  34.2 19.2 %collective-permute-start.15 = (bf16[832,512]{1,0:T(8,128)(2,1)S(1)}, bf16[832,512]{1,0:T(8,128)(2,1)S(1)}, u32[]{:S(2)}, u32[]{:S(2)}) collective-permute-start(bf16[832,512]{1,0:T(8,128)(2,1)S(1)} %constant_dynamic-update-slice_fusion.5.refs_0_), channel_id=1, source_target_pairs={{0,96},{32,0},{64,32},{96,64},{1,97},{33,1},{65,33},{97,65},{2,98}... | collective-permute-start | bytes 2555912 | tf_op jit(solution)/shard_map/ppermute | solution.py:27
  49.4 9.2 %collective-permute-start.8 = (bf16[416,512]{1,0:T(8,128)(2,1)S(1)}, bf16[416,512]{1,0:T(8,128)(2,1)S(1)}, u32[]{:S(2)}, u32[]{:S(2)}) collective-permute-start(bf16[416,512]{1,0:T(8,128)(2,1)S(1)} %slice.54), channel_id=1, source_target_pairs={{0,16},{16,2},{2,18},{18,0},{1,17},{17,3},{3,19},{19,1},{4,20},{20... | collective-permute-start | bytes 1277960 | tf_op jit(solution)/shard_map/ppermute | solution.py:26
  49.5 9.1 %collective-permute-start.9 = (bf16[416,512]{1,0:T(8,128)(2,1)S(1)}, bf16[416,512]{1,0:T(8,128)(2,1)S(1)}, u32[]{:S(2)}, u32[]{:S(2)}) collective-permute-start(bf16[416,512]{1,0:T(8,128)(2,1)S(1)} %slice.55), channel_id=1, source_target_pairs={{0,18},{16,0},{2,16},{18,2},{1,19},{17,1},{3,17},{19,3},{4,22},{20... | collective-permute-start | bytes 1277960 | tf_op jit(solution)/shard_map/ppermute | solution.py:26
  52.3 8.9 %collective-permute-start.17 = (bf16[416,512]{1,0:T(8,128)(2,1)S(1)}, bf16[416,512]{1,0:T(8,128)(2,1)S(1)}, u32[]{:S(2)}, u32[]{:S(2)}) collective-permute-start(bf16[416,512]{1,0:T(8,128)(2,1)S(1)} %slice.58), channel_id=1, source_target_pairs={{0,32},{32,64},{64,96},{96,0},{1,33},{33,65},{65,97},{97,1},{2,34}... | collective-permute-start | bytes 1277960 | tf_op jit(solution)/shard_map/ppermute | solution.py:27
  53.5 14.7 %copy-start.17 = (f32[1664]{0:T(1024)S(1)}, f32[1664]{0:T(1024)}, u32[]{:S(2)}) copy-start(f32[1664]{0:T(1024)} %param.9) | copy-start | bytes 19972
  53.5 14.7 %copy-start.18 = (f32[1664]{0:T(1024)S(1)}, f32[1664]{0:T(1024)}, u32[]{:S(2)}) copy-start(f32[1664]{0:T(1024)} %param.10) | copy-start | bytes 19972
  53.5 7.6 %collective-permute-start.18 = (bf16[416,512]{1,0:T(8,128)(2,1)S(1)}, bf16[416,512]{1,0:T(8,128)(2,1)S(1)}, u32[]{:S(2)}, u32[]{:S(2)}) collective-permute-start(bf16[416,512]{1,0:T(8,128)(2,1)S(1)} %slice.59), channel_id=1, source_target_pairs={{0,96},{32,0},{64,32},{96,64},{1,97},{33,1},{65,33},{97,65},{2,98}... | collective-permute-start | bytes 1277960 | tf_op jit(solution)/shard_map/ppermute | solution.py:27
  61.4 1.8 copy-start.2
  63.2 20.3 %collective-permute-start.19 = (bf16[4,2,160,1664]{3,2,1,0:T(8,128)(2,1)}, bf16[4,2,160,1664]{3,2,1,0:T(8,128)(2,1)}, u32[]{:S(2)}, u32[]{:S(2)}) collective-permute-start(bf16[4,2,160,1664]{3,2,1,0:T(8,128)(2,1)} %all-gather.2.cloned.1.call-done.refs_0_), channel_id=1, source_target_pairs={{0,1},{1,0},{2,3},{3,2},{4,5},{5,4},{6,7},{7,6},{8,9},{9,8},{10,11... | collective-permute-start | bytes 12779528 | tf_op jit(solution)/shard_map/ppermute | solution.py:31
  68.3 2.2 %copy-start = (bf16[4,2,160,1664]{3,2,1,0:T(8,128)(2,1)S(1)}, bf16[4,2,160,1664]{3,2,1,0:T(8,128)(2,1)}, u32[]{:S(2)}) copy-start(bf16[4,2,160,1664]{3,2,1,0:T(8,128)(2,1)} %all-gather.2.cloned.1.call-done.refs_0_) | copy-start | bytes 12779524
  70.5 3.7 %copy-start.1 = (bf16[4,2,160,1664]{3,2,1,0:T(8,128)(2,1)S(1)}, bf16[4,2,160,1664]{3,2,1,0:T(8,128)(2,1)}, u32[]{:S(2)}) copy-start(bf16[4,2,160,1664]{3,2,1,0:T(8,128)(2,1)} %all-gather.2.cloned.1.call-done.refs_0_) | copy-start | bytes 12779524
  74.2 2.0 %copy-start.3 = (bf16[1664,1024]{1,0:T(8,128)(2,1)S(1)}, bf16[1664,1024]{1,0:T(8,128)(2,1)}, u32[]{:S(2)}) copy-start(bf16[1664,1024]{1,0:T(8,128)(2,1)} %copy-done.2) | copy-start | bytes 10223620
  105.4 9.0 %collective-permute-start.20 = (bf16[640,1664]{1,0:T(8,128)(2,1)S(1)}, bf16[640,1664]{1,0:T(8,128)(2,1)S(1)}, u32[]{:S(2)}, u32[]{:S(2)}) collective-permute-start(bf16[640,1664]{1,0:T(8,128)(2,1)S(1)} %get-tuple-element.89), channel_id=1, source_target_pairs={{0,1},{1,0},{2,3},{3,2},{4,5},{5,4},{6,7},{7,6},{8,9},{9,8},{10,11... | collective-permute-start | bytes 6389768 | tf_op jit(solution)/shard_map/ppermute | solution.py:31
  108.8 17.4 %collective-permute-start.21 = (bf16[240,1024]{1,0:T(8,128)(2,1)S(1)}, bf16[240,1024]{1,0:T(8,128)(2,1)S(1)}, u32[]{:S(2)}, u32[]{:S(2)}) collective-permute-start(bf16[240,1024]{1,0:T(8,128)(2,1)S(1)} %get-tuple-element.101), channel_id=1, source_target_pairs={{0,32},{32,64},{64,96},{96,0},{1,33},{33,65},{65,97},{97,1},{2,34}... | collective-permute-start | bytes 1474568 | tf_op jit(solution)/shard_map/ppermute | solution.py:27
  109.8 16.4 %collective-permute-start.22 = (bf16[240,1024]{1,0:T(8,128)(2,1)S(1)}, bf16[240,1024]{1,0:T(8,128)(2,1)S(1)}, u32[]{:S(2)}, u32[]{:S(2)}) collective-permute-start(bf16[240,1024]{1,0:T(8,128)(2,1)S(1)} %get-tuple-element.102), channel_id=1, source_target_pairs={{0,96},{32,0},{64,32},{96,64},{1,97},{33,1},{65,33},{97,65},{2,98}... | collective-permute-start | bytes 1474568 | tf_op jit(solution)/shard_map/ppermute | solution.py:27
  111.7 14.5 %collective-permute-start.23 = (bf16[416,512]{1,0:T(8,128)(2,1)S(1)}, bf16[416,512]{1,0:T(8,128)(2,1)S(1)}, u32[]{:S(2)}, u32[]{:S(2)}) collective-permute-start(bf16[416,512]{1,0:T(8,128)(2,1)S(1)} %get-tuple-element.103), channel_id=1, source_target_pairs={{0,16},{16,2},{2,18},{18,0},{1,17},{17,3},{3,19},{19,1},{4,20},{20... | collective-permute-start | bytes 1277960 | tf_op jit(solution)/shard_map/ppermute | solution.py:26
  111.7 14.5 %collective-permute-start.24 = (bf16[416,512]{1,0:T(8,128)(2,1)S(1)}, bf16[416,512]{1,0:T(8,128)(2,1)S(1)}, u32[]{:S(2)}, u32[]{:S(2)}) collective-permute-start(bf16[416,512]{1,0:T(8,128)(2,1)S(1)} %get-tuple-element.104), channel_id=1, source_target_pairs={{0,18},{16,0},{2,16},{18,2},{1,19},{17,1},{3,17},{19,3},{4,22},{20... | collective-permute-start | bytes 1277960 | tf_op jit(solution)/shard_map/ppermute | solution.py:26
  126.1 1.3 copy-start.8
  126.2 1.8 copy-start.10
  127.9 0.9 copy-start.13
  128.8 1.0 copy-start.14
  129.8 1.0 copy-start.15
  130.8 21.7 %collective-permute-start.25 = (bf16[448,1024]{1,0:T(8,128)(2,1)S(1)}, bf16[448,1024]{1,0:T(8,128)(2,1)S(1)}, u32[]{:S(2)}, u32[]{:S(2)}) collective-permute-start(bf16[448,1024]{1,0:T(8,128)(2,1)S(1)} %get-tuple-element.109), channel_id=1, source_target_pairs={{0,32},{32,64},{64,96},{96,0},{1,33},{33,65},{65,97},{97,1},{2,34}... | collective-permute-start | bytes 2752520 | tf_op jit(solution)/shard_map/ppermute | solution.py:27
  130.9 19.5 %collective-permute-start.26 = (bf16[416,1024]{1,0:T(8,128)(2,1)}, bf16[416,1024]{1,0:T(8,128)(2,1)S(1)}, u32[]{:S(2)}, u32[]{:S(2)}) collective-permute-start(bf16[416,1024]{1,0:T(8,128)(2,1)} %copy-done.15), channel_id=1, source_target_pairs={{0,96},{32,0},{64,32},{96,64},{1,97},{33,1},{65,33},{97,65},{2,98}... | collective-permute-start | bytes 2555912 | tf_op jit(solution)/shard_map/ppermute | solution.py:27
  133.5 24.3 %collective-permute-start.30 = (bf16[832,512]{1,0:T(8,128)(2,1)}, bf16[832,512]{1,0:T(8,128)(2,1)S(1)}, u32[]{:S(2)}, u32[]{:S(2)}) collective-permute-start(bf16[832,512]{1,0:T(8,128)(2,1)} %copy-done.14), channel_id=1, source_target_pairs={{0,16},{16,2},{2,18},{18,0},{1,17},{17,3},{3,19},{19,1},{4,20},{20... | collective-permute-start | bytes 2555912 | tf_op jit(solution)/shard_map/ppermute | solution.py:26
  133.5 24.3 %collective-permute-start.31 = (bf16[832,512]{1,0:T(8,128)(2,1)}, bf16[832,512]{1,0:T(8,128)(2,1)S(1)}, u32[]{:S(2)}, u32[]{:S(2)}) collective-permute-start(bf16[832,512]{1,0:T(8,128)(2,1)} %copy-done.13), channel_id=1, source_target_pairs={{0,18},{16,0},{2,16},{18,2},{1,19},{17,1},{3,17},{19,3},{4,22},{20... | collective-permute-start | bytes 2555912 | tf_op jit(solution)/shard_map/ppermute | solution.py:26
  152.5 1.5 copy-start.9
  154.0 3.8 %copy-start.11 = (f32[832,512]{1,0:T(8,128)S(1)}, f32[832,512]{1,0:T(8,128)}, u32[]{:S(2)}) copy-start(f32[832,512]{1,0:T(8,128)} %copy-done.10) | copy-start | bytes 5111812
  154.0 7.2 %copy-start.5 = (bf16[160,1664]{1,0:T(8,128)(2,1)S(1)}, bf16[160,1664]{1,0:T(8,128)(2,1)}, u32[]{:S(2)}) copy-start(bf16[160,1664]{1,0:T(8,128)(2,1)} %refs_0_.3) | copy-start | bytes 1597444
  154.0 7.2 %copy-start.7 = (bf16[160,1664]{1,0:T(8,128)(2,1)S(1)}, bf16[160,1664]{1,0:T(8,128)(2,1)}, u32[]{:S(2)}) copy-start(bf16[160,1664]{1,0:T(8,128)(2,1)} %refs_1_.3) | copy-start | bytes 1597444
  155.2 13.2 %collective-permute-start.27 = (bf16[240,512]{1,0:T(8,128)(2,1)}, bf16[240,512]{1,0:T(8,128)(2,1)S(1)}, u32[]{:S(2)}, u32[]{:S(2)}) collective-permute-start(bf16[240,512]{1,0:T(8,128)(2,1)} %get-tuple-element.113), channel_id=1, source_target_pairs={{0,16},{16,2},{2,18},{18,0},{1,17},{17,3},{3,19},{19,1},{4,20},{20... | collective-permute-start | bytes 737288 | tf_op jit(solution)/shard_map/ppermute | solution.py:26
  155.2 13.2 %collective-permute-start.28 = (bf16[240,512]{1,0:T(8,128)(2,1)}, bf16[240,512]{1,0:T(8,128)(2,1)S(1)}, u32[]{:S(2)}, u32[]{:S(2)}) collective-permute-start(bf16[240,512]{1,0:T(8,128)(2,1)} %get-tuple-element.114), channel_id=1, source_target_pairs={{0,2},{16,18},{2,0},{18,16},{1,3},{17,19},{3,1},{19,17},{4,6},{20,... | collective-permute-start | bytes 737288 | tf_op jit(solution)/shard_map/ppermute | solution.py:26
  156.6 12.1 %collective-permute-start.29 = (bf16[240,512]{1,0:T(8,128)(2,1)}, bf16[240,512]{1,0:T(8,128)(2,1)S(1)}, u32[]{:S(2)}, u32[]{:S(2)}) collective-permute-start(bf16[240,512]{1,0:T(8,128)(2,1)} %get-tuple-element.115), channel_id=1, source_target_pairs={{0,18},{16,0},{2,16},{18,2},{1,19},{17,1},{3,17},{19,3},{4,22},{20... | collective-permute-start | bytes 737288 | tf_op jit(solution)/shard_map/ppermute | solution.py:26
  158.9 8.2 %collective-permute-start.32 = (bf16[208,512]{1,0:T(8,128)(2,1)}, bf16[208,512]{1,0:T(8,128)(2,1)S(1)}, u32[]{:S(2)}, u32[]{:S(2)}) collective-permute-start(bf16[208,512]{1,0:T(8,128)(2,1)} %get-tuple-element.121), channel_id=1, source_target_pairs={{0,32},{32,64},{64,96},{96,0},{1,33},{33,65},{65,97},{97,1},{2,34}... | collective-permute-start | bytes 638984 | tf_op jit(solution)/shard_map/ppermute | solution.py:27
  158.9 9.4 %collective-permute-start.33 = (bf16[208,512]{1,0:T(8,128)(2,1)}, bf16[208,512]{1,0:T(8,128)(2,1)S(1)}, u32[]{:S(2)}, u32[]{:S(2)}) collective-permute-start(bf16[208,512]{1,0:T(8,128)(2,1)} %get-tuple-element.122), channel_id=1, source_target_pairs={{0,64},{32,96},{64,0},{96,32},{1,65},{33,97},{65,1},{97,33},{2,66}... | collective-permute-start | bytes 638984 | tf_op jit(solution)/shard_map/ppermute | solution.py:27
  161.3 1.0 copy-start.12
  168.9 3.0 %collective-permute-start.34 = (f32[8,512]{1,0:T(8,128)S(1)}, f32[8,512]{1,0:T(8,128)S(1)}, u32[]{:S(2)}, u32[]{:S(2)}) collective-permute-start(f32[8,512]{1,0:T(8,128)S(1)} %slice.47), channel_id=1, source_target_pairs={{0,4},{4,0},{8,12},{12,8},{1,5},{5,1},{9,13},{13,9},{2,6},{6,2},{1... | collective-permute-start | bytes 49160 | tf_op jit(solution)/shard_map/ppermute | solution.py:44
  170.1 10.2 %collective-permute-start.37 = (bf16[208,512]{1,0:T(8,128)(2,1)S(1)}, bf16[208,512]{1,0:T(8,128)(2,1)S(1)}, u32[]{:S(2)}, u32[]{:S(2)}) collective-permute-start(bf16[208,512]{1,0:T(8,128)(2,1)S(1)} %get-tuple-element.127), channel_id=1, source_target_pairs={{0,96},{32,0},{64,32},{96,64},{1,97},{33,1},{65,33},{97,65},{2,98}... | collective-permute-start | bytes 638984 | tf_op jit(solution)/shard_map/ppermute | solution.py:27
  171.9 9.1 %collective-permute-start.35 = (f32[8,512]{1,0:T(8,128)S(1)}, f32[8,512]{1,0:T(8,128)S(1)}, u32[]{:S(2)}, u32[]{:S(2)}) collective-permute-start(f32[8,512]{1,0:T(8,128)S(1)} %slice_add_fusion), channel_id=1, source_target_pairs={{0,8},{4,12},{8,0},{12,4},{1,9},{5,13},{9,1},{13,5},{2,10},{6,14},... | collective-permute-start | bytes 49160 | tf_op jit(solution)/shard_map/ppermute | solution.py:44
  175.2 6.8 %collective-permute-start.39 = (f32[512]{0:T(512)S(1)}, f32[512]{0:T(512)S(1)}, u32[]{:S(2)}, u32[]{:S(2)}) collective-permute-start(f32[512]{0:T(512)S(1)} %bitcast.17), channel_id=1, source_target_pairs={{0,1},{1,0},{2,3},{3,2},{4,5},{5,4},{6,7},{7,6},{8,9},{9,8},{10,11... | collective-permute-start | bytes 6152 | tf_op jit(solution)/shard_map/ppermute | solution.py:31
  180.3 3.7 %collective-permute-start.38 = (f32[104,512]{1,0:T(8,128)S(1)}, f32[104,512]{1,0:T(8,128)S(1)}, u32[]{:S(2)}, u32[]{:S(2)}) collective-permute-start(f32[104,512]{1,0:T(8,128)S(1)} %get-tuple-element.129), channel_id=1, source_target_pairs={{0,1},{1,0},{2,3},{3,2},{4,5},{5,4},{6,7},{7,6},{8,9},{9,8},{10,11... | collective-permute-start | bytes 638984 | tf_op jit(solution)/shard_map/ppermute | solution.py:31
  180.5 4.4 %collective-permute-start.40 = (f32[104,512]{1,0:T(8,128)S(1)}, f32[104,512]{1,0:T(8,128)S(1)}, u32[]{:S(2)}, u32[]{:S(2)}) collective-permute-start(f32[104,512]{1,0:T(8,128)S(1)} %get-tuple-element.131), channel_id=1, source_target_pairs={{0,1},{1,0},{2,3},{3,2},{4,5},{5,4},{6,7},{7,6},{8,9},{9,8},{10,11... | collective-permute-start | bytes 638984 | tf_op jit(solution)/shard_map/ppermute | solution.py:31
  180.9 1.9 collective-permute-start.36
Sparse Core Ops, SparseCore 0:
  10.5 52.2 all-gather.1
  130.9 29.4 reduce-scatter.1

commit v3 on v2

--- a/solution.py
+++ b/solution.py
@@ -121,7 +121,7 @@
     lax.fori_loop(0, mine.shape[0] // 32, step, 0)
 
 
-def norm_kernel(half, part, gain, shift_by, *refs):
+def norm_kernel(half, part, gain, shift_by, *refs, unroll=False):
     normed, centre, scale, normed_t, up_t, turned = refs[-6:]
     tokens, width = part.shape[2:]
     to, rows = pl.ds(half * 4 * tokens, 4 * tokens), width // 8
@@ -148,19 +148,19 @@
         normed_t[pl.ds(at, rows), to] = turned[pl.ds(pl.multiple_of(b * rows, 16), rows), :]
         return 0
 
-    lax.fori_loop(0, 4, normalise, 0)
-    lax.fori_loop(0, width // 128, turn, 0)
-    lax.fori_loop(0, 8, order, 0)
-
-
-def hidden_kernel(half, part, normed, expand, shrink, bias, *refs):
+    lax.fori_loop(0, 4, normalise, 0, unroll=unroll)
+    lax.fori_loop(0, width // 128, turn, 0, unroll=unroll)
+    lax.fori_loop(0, 8, order, 0, unroll=unroll)
+
+
+def hidden_kernel(half, part, normed, expand, shrink, bias, *refs, unroll=False):
     bias_sum, active, back, pre_tile, back_tile = refs[-5:]
     tokens, width = part.shape[2:]
     tile, to = 256, pl.ds(half * 4 * tokens, 4 * tokens)
     tiles = expand.shape[1] // tile
 
     def lanes_of(j):
-        return pl.ds(pl.multiple_of(j * tile, tile), tile)
+        return slice(j * tile, (j + 1) * tile) if unroll else pl.ds(pl.multiple_of(j * tile, tile), tile)
 
     def products(j, slot):
         lanes = lanes_of(j)
@@ -176,15 +176,18 @@
         bias_sum[:, lanes] = jnp.sum(grad.astype(f32), axis=0, keepdims=True)
 
     def step(j, _):
-        products(2 * j + 1, 1)
-        finish(2 * j, 0)
-        following = lax.rem(2 * j + 2, tiles)
-        products(following, 0)
-        finish(2 * j + 1, 1)
-        return 0
-
-    products(0, 0)
-    lax.fori_loop(0, tiles // 2, step, 0)
+        products(j, 0)
+        finish(j, 0)
+        return 0
+
+    if unroll:
+        products(0, 0)
+        for j in range(1, tiles):
+            products(j, j % 2)
+            finish(j - 1, (j - 1) % 2)
+        finish(tiles - 1, (tiles - 1) % 2)
+    else:
+        lax.fori_loop(0, tiles, step, 0)
 
 
 def second_kernel(part, gain, shift_by, bias, expand, shrink, normed_t_in, up_t_in, active_in, back_in, *refs):
@@ -396,8 +399,9 @@
 
     def by_core(weight):
         kept = lax.dynamic_slice_in_dim(weight, core * half, half, 1)
-        given = swap(lax.dynamic_slice_in_dim(weight, (1 - core) * half, half, 1))
-        return jnp.where(core == 0, jnp.concatenate([kept, given], 0), jnp.concatenate([given, kept], 0))
+        given = lax.dynamic_slice_in_dim(weight, (1 - core) * half, half, 1)
+        got = swap(given)
+        return jnp.where(core == 0, jnp.concatenate([kept, got], 0), jnp.concatenate([got, kept], 0))
 
     block_rows = 2 * rows
 
@@ -434,14 +438,14 @@
     tile = pltpu.VMEM((2, 4 * tokens, 256), f32)
     turned = pltpu.VMEM((width, 4 * tokens), bf16)
     normed, near_centre, near_scale, normed_t, up_t = call(
-        functools.partial(norm_kernel, 0),
+        functools.partial(norm_kernel, 0, unroll=True),
         [(half_tall, bf16), column, column, tall, tall],
         (near, gain, shift_by),
         scratch=[turned],
         behind=(first_mark, second_mark),
     )
     near_bias, active, back = call(
-        functools.partial(hidden_kernel, 0),
+        functools.partial(hidden_kernel, 0, unroll=True),
         [bias_row, wide, wide],
         (near, normed, expand_all, shrink_all, bias_own),
         scratch=[tile, tile],

time: 193 us -> 189 us (0.979)
  Pallas kernels: 55 us -> 51.5 us
    pallas_call x17, Pallas kernels: 55 us -> 51.5 us  [call(): pl.pallas_call(body, out_shape=[jax.ShapeDtypeStruct(shape, dtype) for sh...]
  transfers between devices with their start and end apart: 43 -> 43, of which waited for: 13 -> 13; matrix products, arithmetic and copies ran while one was open for 2% -> 2% of each run, Pallas kernels for 16% -> 15%
where the time goes in v3:
time: 189 us
  starting transfers between devices  57.7 us (31%)
  Pallas kernels  51.5 us (27%)
  waiting for transfers between devices  45.9 us (24%)
  local copies, waits for them, and re-layouts  17 us (9%)
  between operations  14.5 us (8%)
  other arithmetic  2.39 us (1%)
    pallas_call x17, Pallas kernels, call(): pl.pallas_call(body, out_shape=[jax.ShapeDtypeStruct(shape, dtype) for sh...  51.5 us
    ppermute x15, waiting for transfers between devices, shift(): return lax.ppermute(value, axis, [(i, (i + by) % 4) for i in range(4)])  24.5 us
    ppermute x15, starting transfers between devices, shift(): return lax.ppermute(value, axis, [(i, (i + by) % 4) for i in range(4)])  20.3 us
    ppermute x15, waiting for transfers between devices, shift(): return lax.ppermute(value, PLANE_Y, pairs)  19.5 us
    ppermute x15, starting transfers between devices, shift(): return lax.ppermute(value, PLANE_Y, pairs)  19.3 us
    unnamed x50, local copies, waits for them, and re-layouts  15.8 us
    ppermute x8, starting transfers between devices, swap(): return lax.ppermute(value, 'core', [(0, 1), (1, 0)])  13.3 us
    ppermute x2, starting transfers between devices, pair_sum(): value = value + lax.ppermute(value, axis, [(i, i ^ bit) for i in range(4)])  4.71 us
  transfers between devices with their start and end apart: 43, of which 13 were waited for; matrix products, arithmetic and copies ran while one was open for 2% of the time, Pallas kernels for 15%

profile of v3, /device:TPU:1, one launch (start us, length us, event | category | flops | bytes accessed | tf_op | source)
XLA Modules:
  0.0 189.0 jit_solution(2316198183471576801)
XLA Ops:
  7.2 1.0 copy-done.4
  8.3 1.0 copy-done.6
  9.3 1.1 shard_map.118
  10.5 1.0 constant_dynamic-slice_fusion.1
  11.4 1.5 collective-permute-start.10
  13.1 0.8 collective-permute-done.10
  13.9 1.4 collective-permute-start.12
  15.4 1.5 collective-permute-start.11
  17.0 1.3 collective-permute-start.2
  18.2 1.5 collective-permute-start.1
  19.7 2.3 %collective-permute-done.12 = bf16[208,512]{1,0:T(8,128)(2,1)S(1)} collective-permute-done((bf16[208,512]{1,0:T(8,128)(2,1)S(1)}, bf16[208,512]{1,0:T(8,128)(2,1)S(1)}, u32[]{:S(2)}, u32[]{:S(2)}) %collective-permute-start.12) | collective-permute-done | bytes 213024 | tf_op jit(solution)/shard_map/ppermute | solution.py:26
  22.1 2.7 %collective-permute-start.14 = (bf16[104,512]{1,0:T(8,128)(2,1)S(1)}, bf16[104,512]{1,0:T(8,128)(2,1)S(1)}, u32[]{:S(2)}, u32[]{:S(2)}) collective-permute-start(bf16[104,512]{1,0:T(8,128)(2,1)S(1)} %slice.57), channel_id=1, source_target_pairs={{0,18},{16,0},{2,16},{18,2},{1,19},{17,1},{3,17},{19,3},{4,22},{20... | collective-permute-start | bytes 319496 | tf_op jit(solution)/shard_map/ppermute | solution.py:26
  24.9 1.2 collective-permute-start.3
  26.1 1.6 collective-permute-start.4
  27.7 2.4 %collective-permute-done.3 = bf16[104,512]{1,0:T(8,128)(2,1)S(1)} collective-permute-done((bf16[104,512]{1,0:T(8,128)(2,1)S(1)}, bf16[104,512]{1,0:T(8,128)(2,1)S(1)}, u32[]{:S(2)}, u32[]{:S(2)}) %collective-permute-start.3) | collective-permute-done | bytes 106528 | tf_op jit(solution)/shard_map/ppermute | solution.py:27
  30.3 2.7 %collective-permute-start.6 = (bf16[832,512]{1,0:T(8,128)(2,1)S(1)}, bf16[832,512]{1,0:T(8,128)(2,1)S(1)}, u32[]{:S(2)}, u32[]{:S(2)}) collective-permute-start(bf16[832,512]{1,0:T(8,128)(2,1)S(1)} %constant_dynamic-update-slice_fusion.refs_0_), channel_id=1, source_target_pairs={{0,18},{16,0},{2,16},{18,2},{1,19},{17,1},{3,17},{19,3},{4,22},{20... | collective-permute-start | bytes 2555912 | tf_op jit(solution)/shard_map/ppermute | solution.py:26
  33.0 1.2 collective-permute-start.16
  34.2 1.6 collective-permute-start.15
  35.9 13.5 %collective-permute-done.7.refs_4_ = bf16[832,512]{1,0:T(8,128)(2,1)S(1)} collective-permute-done((bf16[832,512]{1,0:T(8,128)(2,1)S(1)}, bf16[832,512]{1,0:T(8,128)(2,1)S(1)}, u32[]{:S(2)}, u32[]{:S(2)}) %collective-permute-start.7) | collective-permute-done | bytes 852000 | tf_op jit(solution)/shard_map/ppermute | solution.py:26
  49.5 2.7 %collective-permute-start.9 = (bf16[416,512]{1,0:T(8,128)(2,1)S(1)}, bf16[416,512]{1,0:T(8,128)(2,1)S(1)}, u32[]{:S(2)}, u32[]{:S(2)}) collective-permute-start(bf16[416,512]{1,0:T(8,128)(2,1)S(1)} %slice.55), channel_id=1, source_target_pairs={{0,18},{16,0},{2,16},{18,2},{1,19},{17,1},{3,17},{19,3},{4,22},{20... | collective-permute-start | bytes 1277960 | tf_op jit(solution)/shard_map/ppermute | solution.py:26
  52.3 1.2 collective-permute-start.17
  53.5 1.7 collective-permute-start.18
  55.3 3.3 %collective-permute-done.8.refs_2_ = bf16[416,512]{1,0:T(8,128)(2,1)S(1)} collective-permute-done((bf16[416,512]{1,0:T(8,128)(2,1)S(1)}, bf16[416,512]{1,0:T(8,128)(2,1)S(1)}, u32[]{:S(2)}, u32[]{:S(2)}) %collective-permute-start.8) | collective-permute-done | bytes 426016 | tf_op jit(solution)/shard_map/ppermute | solution.py:26
  58.9 2.3 %collective-permute-done.17.refs_2_ = bf16[416,512]{1,0:T(8,128)(2,1)S(1)} collective-permute-done((bf16[416,512]{1,0:T(8,128)(2,1)S(1)}, bf16[416,512]{1,0:T(8,128)(2,1)S(1)}, u32[]{:S(2)}, u32[]{:S(2)}) %collective-permute-start.17) | collective-permute-done | bytes 426016 | tf_op jit(solution)/shard_map/ppermute | solution.py:27
  61.4 1.8 copy-done.2
  63.2 4.9 %collective-permute-start.19 = (bf16[4,2,160,1664]{3,2,1,0:T(8,128)(2,1)}, bf16[4,2,160,1664]{3,2,1,0:T(8,128)(2,1)}, u32[]{:S(2)}, u32[]{:S(2)}) collective-permute-start(bf16[4,2,160,1664]{3,2,1,0:T(8,128)(2,1)} %all-gather.2.cloned.1.call-done.refs_0_), channel_id=1, source_target_pairs={{0,1},{1,0},{2,3},{3,2},{4,5},{5,4},{6,7},{7,6},{8,9},{9,8},{10,11... | collective-permute-start | bytes 12779528 | tf_op jit(solution)/shard_map/ppermute | solution.py:31
  68.3 2.2 %copy-done = bf16[4,2,160,1664]{3,2,1,0:T(8,128)(2,1)S(1)} copy-done((bf16[4,2,160,1664]{3,2,1,0:T(8,128)(2,1)S(1)}, bf16[4,2,160,1664]{3,2,1,0:T(8,128)(2,1)}, u32[]{:S(2)}) %copy-start) | copy-done | bytes 4259864
  70.5 2.4 %shard_map.121 = (bf16[640,1664]{1,0:T(8,128)(2,1)S(1)}, f32[640,1]{1,0:T(8,128)S(1)}, f32[640,1]{1,0:T(8,128)S(1)}, bf16[1664,1280]{1,0:T(8,128)(2,1)S(1)}, bf16[1664,1280]{1,0:T(8,128)(2,1)S(1)}) custom-call(bf16[4,2,160,1664]{3,2,1,0:T(8,128)(2,1)S(1)} %copy-done, f32[1,1664]{1,0:T(1,128)S(1)} %broadcast_in_dim.7.refs_1_.refs_3_, ...), custom_call_target="tpu_custom_call" | custom-call | flops 1000000 | bytes 1000000 | tf_op jit(solution)/shard_map/pallas_call | solution.py:98
  72.9 2.0 %copy-done.3 = bf16[1664,1024]{1,0:T(8,128)(2,1)S(1)} copy-done((bf16[1664,1024]{1,0:T(8,128)(2,1)S(1)}, bf16[1664,1024]{1,0:T(8,128)(2,1)}, u32[]{:S(2)}) %copy-start.3) | copy-done | bytes 3407896
  74.9 5.9 %shard_map.122 = (f32[1,1024]{1,0:T(1,128)S(1)}, bf16[1280,1024]{1,0:T(8,128)(2,1)S(1)}, bf16[1280,1024]{1,0:T(8,128)(2,1)S(1)}) custom-call(bf16[4,2,160,1664]{3,2,1,0:T(8,128)(2,1)S(1)} %copy-done.1, bf16[640,1664]{1,0:T(8,128)(2,1)S(1)} %get-tuple-element.81.refs_1_, bf16[1664,1024]{1,0:T(8,128)(2,1)S(1)} %get-tuple-element.77.refs_2_.refs_4_.refs_7_, ...), custom_call_target="tpu_custom_call" | custom-call | flops 1000000 | bytes 1000000 | tf_op jit(solution)/shard_map/pallas_call | solution.py:98
  80.7 12.3 %shard_map.123 = (f32[640,1]{1,0:T(8,128)S(1)}, f32[640,1]{1,0:T(8,128)S(1)}, bf16[1664,1280]{1,0:T(8,128)(2,1)S(1)}, bf16[1664,1280]{1,0:T(8,128)(2,1)S(1)}, f3...) custom-call(bf16[4,2,160,1664]{3,2,1,0:T(8,128)(2,1)} %collective-pe, ...), custom_call_target="tpu_custom_call", output_to_operand_aliasing={{2}: (6, {}), {3}: (7, {}), {5}: (8, {}), {6}: (9, {})} | custom-call | flops 1000000 | bytes 1000000 | tf_op jit(solution)/shard_map/pallas_call | solution.py:98
  93.0 8.9 %shard_map.124 = (f32[640,1664]{1,0:T(8,128)S(1)}, bf16[640,1664]{1,0:T(8,128)(2,1)S(1)}, f32[2,1664]{1,0:T(2,128)S(1)}) custom-call(bf16[4,2,160,1664]{3,2,1,0:T(8,128)(2,1)S(1)} %copy-done.1, bf16[4,2,160,1664]{3,2,1,0:T(8,128)(2,1)} %collective-permute-done.19.refs_0_.refs_1_, f32[640,1]{1,0:T(8,128)S(1)} %get-tuple-element.75.refs_2_, ...), custom_call_target="tpu_custom_call" | custom-call | flops 1000000 | bytes 1000000 | tf_op jit(solution)/shard_map/pallas_call | solution.py:98
  102.0 3.3 %shard_map.125 = (bf16[240,1024]{1,0:T(8,128)(2,1)S(1)}, bf16[240,1024]{1,0:T(8,128)(2,1)S(1)}, bf16[416,512]{1,0:T(8,128)(2,1)S(1)}, bf16[416,512]{1,0:T(8,128)(2,1)S(1)}, f32[16,1024]{1,0:T(8,128)S(1)}) custom-call(bf16[1664,1280]{1,0:T(8,128)(2,1)S(1)} %get-tuple-element.90.refs_0_, bf16[1280,1024]{1,0:T(8,128)(2,1)S(1)} %get-tuple-element.91.refs_1_, ...), custom_call_target="tpu_custom_call" | custom-call | flops 1000000 | bytes 1000000 | tf_op jit(solution)/shard_map/pallas_call | solution.py:98
  105.3 1.0 collective-permute-start.21
  106.4 1.9 collective-permute-start.22
  108.2 2.7 %collective-permute-start.24 = (bf16[416,512]{1,0:T(8,128)(2,1)S(1)}, bf16[416,512]{1,0:T(8,128)(2,1)S(1)}, u32[]{:S(2)}, u32[]{:S(2)}) collective-permute-start(bf16[416,512]{1,0:T(8,128)(2,1)S(1)} %get-tuple-element.104), channel_id=1, source_target_pairs={{0,18},{16,0},{2,16},{18,2},{1,19},{17,1},{3,17},{19,3},{4,22},{20... | collective-permute-start | bytes 1277960 | tf_op jit(solution)/shard_map/ppermute | solution.py:26
  110.9 1.8 shard_map.126
  112.7 10.0 %shard_map.127 = (f32[416,1024]{1,0:T(8,128)S(1)}, f32[832,512]{1,0:T(8,128)S(1)}, f32[2,416,1024]{2,1,0:T(8,128)S(1)}, f32[2,832,512]{2,1,0:T(8,128)S(1)}) custom-call(bf16[1664,1280]{1,0:T(8,128)(2,1)S(1)} %get-tuple-element.90.refs_0_, bf16[1280,1024]{1,0:T(8,128)(2,1)S(1)} %get-tuple-element.91.refs_1_, ...), custom_call_target="tpu_custom_call" | custom-call | flops 1000000 | bytes 1000000 | tf_op jit(solution)/shard_map/pallas_call | solution.py:98
  122.7 0.6 shard_map.128
  124.4 0.9 copy-done.13
  125.4 1.0 copy-done.14
  126.3 1.0 copy-done.15
  127.4 2.7 %collective-permute-start.26 = (bf16[416,1024]{1,0:T(8,128)(2,1)}, bf16[416,1024]{1,0:T(8,128)(2,1)S(1)}, u32[]{:S(2)}, u32[]{:S(2)}) collective-permute-start(bf16[416,1024]{1,0:T(8,128)(2,1)} %copy-done.15), channel_id=1, source_target_pairs={{0,96},{32,0},{64,32},{96,64},{1,97},{33,1},{65,33},{97,65},{2,98}... | collective-permute-start | bytes 2555912 | tf_op jit(solution)/shard_map/ppermute | solution.py:27
  130.1 2.7 %collective-permute-start.31 = (bf16[832,512]{1,0:T(8,128)(2,1)}, bf16[832,512]{1,0:T(8,128)(2,1)S(1)}, u32[]{:S(2)}, u32[]{:S(2)}) collective-permute-start(bf16[832,512]{1,0:T(8,128)(2,1)} %copy-done.13), channel_id=1, source_target_pairs={{0,18},{16,0},{2,16},{18,2},{1,19},{17,1},{3,17},{19,3},{4,22},{20... | collective-permute-start | bytes 2555912 | tf_op jit(solution)/shard_map/ppermute | solution.py:26
  132.7 14.1 %collective-permute-done.26.refs_2_ = bf16[416,1024]{1,0:T(8,128)(2,1)S(1)} collective-permute-done((bf16[416,1024]{1,0:T(8,128)(2,1)}, bf16[416,1024]{1,0:T(8,128)(2,1)S(1)}, u32[]{:S(2)}, u32[]{:S(2)}) %collective-permute-start.26) | collective-permute-done | bytes 852000 | tf_op jit(solution)/shard_map/ppermute | solution.py:27
  146.9 2.2 %collective-permute-done.25.refs_1_ = bf16[448,1024]{1,0:T(8,128)(2,1)S(1)} collective-permute-done((bf16[448,1024]{1,0:T(8,128)(2,1)S(1)}, bf16[448,1024]{1,0:T(8,128)(2,1)S(1)}, u32[]{:S(2)}, u32[]{:S(2)}) %collective-permute-start.25) | collective-permute-done | bytes 917536 | tf_op jit(solution)/shard_map/ppermute | solution.py:27
  149.1 1.5 copy-done.9
  150.6 1.1 shard_map.130
  151.7 1.5 collective-permute-start.28
  153.2 1.2 collective-permute-start.29
  154.4 1.0 shard_map.131
  155.4 2.4 %collective-permute-start.33 = (bf16[208,512]{1,0:T(8,128)(2,1)}, bf16[208,512]{1,0:T(8,128)(2,1)S(1)}, u32[]{:S(2)}, u32[]{:S(2)}) collective-permute-start(bf16[208,512]{1,0:T(8,128)(2,1)} %get-tuple-element.122), channel_id=1, source_target_pairs={{0,64},{32,96},{64,0},{96,32},{1,65},{33,97},{65,1},{97,33},{2,66}... | collective-permute-start | bytes 638984 | tf_op jit(solution)/shard_map/ppermute | solution.py:27
  157.8 1.0 copy-done.12
  158.9 2.4 %shard_map.129 = (bf16[160,1664]{1,0:T(8,128)(2,1)}, f32[8,128]{1,0:T(8,128)S(1)}) custom-call(bf16[160,1664]{1,0:T(8,128)(2,1)S(1)} %copy-done.5, bf16[160,1664]{1,0:T(8,128)(2,1)S(1)} %copy-done.7, bf16[160,1664]{1,0:T(8,128)(2,1)S(1)} %copy-done.12, f32[1,1664]{1,0:T(1,128)S(1)} %broadcast_in_dim.7.refs_1_.refs_3_), custom_call_target="tpu_custom_call" | custom-call | flops 1000000 | bytes 1000000 | tf_op jit(solution)/shard_map/pallas_call | solution.py:98
  161.3 2.3 %collective-permute-done.32.refs_1_ = bf16[208,512]{1,0:T(8,128)(2,1)S(1)} collective-permute-done((bf16[208,512]{1,0:T(8,128)(2,1)}, bf16[208,512]{1,0:T(8,128)(2,1)S(1)}, u32[]{:S(2)}, u32[]{:S(2)}) %collective-permute-start.32) | collective-permute-done | bytes 213024 | tf_op jit(solution)/shard_map/ppermute | solution.py:27
  163.6 1.2 collective-permute-done.33.refs_2_
  165.4 1.3 collective-permute-start.34
  166.7 0.9 collective-permute-start.37
  167.6 0.8 collective-permute-done.34
  168.4 3.4 %collective-permute-start.35 = (f32[8,512]{1,0:T(8,128)S(1)}, f32[8,512]{1,0:T(8,128)S(1)}, u32[]{:S(2)}, u32[]{:S(2)}) collective-permute-start(f32[8,512]{1,0:T(8,128)S(1)} %slice_add_fusion), channel_id=1, source_target_pairs={{0,8},{4,12},{8,0},{12,4},{1,9},{5,13},{9,1},{13,5},{2,10},{6,14},... | collective-permute-start | bytes 49160 | tf_op jit(solution)/shard_map/ppermute | solution.py:44
  171.8 5.0 %collective-permute-start.39 = (f32[512]{0:T(512)S(1)}, f32[512]{0:T(512)S(1)}, u32[]{:S(2)}, u32[]{:S(2)}) collective-permute-start(f32[512]{0:T(512)S(1)} %bitcast.17), channel_id=1, source_target_pairs={{0,1},{1,0},{2,3},{3,2},{4,5},{5,4},{6,7},{7,6},{8,9},{9,8},{10,11... | collective-permute-start | bytes 6152 | tf_op jit(solution)/shard_map/ppermute | solution.py:31
  177.5 1.1 collective-permute-start.36
  180.6 0.8 maximum_select_fusion
  181.4 0.8 maximum_select_fusion.1
  (117 shorter events, 6.1 us)
Async XLA Ops:
  7.2 56.1 %all-gather.2.cloned.1.call-start = ((), (), s32[]{:S(2)}) async-start(), calls=%async_computation.1 | async-start | bytes 5324800 | tf_op jit(solution)/shard_map/all_gather | solution.py:412
  7.2 1.0 copy-start.4
  8.3 1.0 copy-start.6
  9.3 3.6 %copy-start.16 = (bf16[104,1024]{1,0:T(8,128)(2,1)S(1)}, bf16[104,1024]{1,0:T(8,128)(2,1)}, u32[]{:S(2)}) copy-start(bf16[104,1024]{1,0:T(8,128)(2,1)} %param.11) | copy-start | bytes 638980
  9.3 10.4 %copy-start.19 = (f32[1024]{0:T(1024)S(1)}, f32[1024]{0:T(1024)}, u32[]{:S(2)}) copy-start(f32[1024]{0:T(1024)} %param.12) | copy-start | bytes 12292
  10.4 147.4 %reduce-scatter.2.cloned.1.call-start = ((), (), s32[]{:S(2)}) async-start(), calls=%async_computation.2 | async-start | bytes 2662400 | tf_op jit(solution)/shard_map/reduce_scatter | solution.py:494
  11.4 2.5 %collective-permute-start.10 = (bf16[104,512]{1,0:T(8,128)(2,1)S(1)}, bf16[104,512]{1,0:T(8,128)(2,1)S(1)}, u32[]{:S(2)}, u32[]{:S(2)}) collective-permute-start(bf16[104,512]{1,0:T(8,128)(2,1)S(1)} %get-tuple-element.136), channel_id=1, source_target_pairs={{0,1},{1,0},{2,3},{3,2},{4,5},{5,4},{6,7},{7,6},{8,9},{9,8},{10,11... | collective-permute-start | bytes 319496 | tf_op jit(solution)/shard_map/ppermute | solution.py:31
  13.0 4.0 %collective-permute-start = (bf16[104,512]{1,0:T(8,128)(2,1)S(1)}, bf16[104,512]{1,0:T(8,128)(2,1)S(1)}, u32[]{:S(2)}, u32[]{:S(2)}) collective-permute-start(bf16[104,512]{1,0:T(8,128)(2,1)S(1)} %get-tuple-element.138), channel_id=1, source_target_pairs={{0,1},{1,0},{2,3},{3,2},{4,5},{5,4},{6,7},{7,6},{8,9},{9,8},{10,11... | collective-permute-start | bytes 319496 | tf_op jit(solution)/shard_map/ppermute | solution.py:31
  13.9 8.1 %collective-permute-start.12 = (bf16[208,512]{1,0:T(8,128)(2,1)S(1)}, bf16[208,512]{1,0:T(8,128)(2,1)S(1)}, u32[]{:S(2)}, u32[]{:S(2)}) collective-permute-start(bf16[208,512]{1,0:T(8,128)(2,1)S(1)} %get-tuple-element.133), channel_id=1, source_target_pairs={{0,16},{16,2},{2,18},{18,0},{1,17},{17,3},{3,19},{19,1},{4,20},{20... | collective-permute-start | bytes 638984 | tf_op jit(solution)/shard_map/ppermute | solution.py:26
  15.4 6.7 %collective-permute-start.11 = (bf16[208,512]{1,0:T(8,128)(2,1)S(1)}, bf16[208,512]{1,0:T(8,128)(2,1)S(1)}, u32[]{:S(2)}, u32[]{:S(2)}) collective-permute-start(bf16[208,512]{1,0:T(8,128)(2,1)S(1)} %get-tuple-element.133), channel_id=1, source_target_pairs={{0,18},{16,0},{2,16},{18,2},{1,19},{17,1},{3,17},{19,3},{4,22},{20... | collective-permute-start | bytes 638984 | tf_op jit(solution)/shard_map/ppermute | solution.py:26
  17.0 7.9 %collective-permute-start.2 = (bf16[208,512]{1,0:T(8,128)(2,1)S(1)}, bf16[208,512]{1,0:T(8,128)(2,1)S(1)}, u32[]{:S(2)}, u32[]{:S(2)}) collective-permute-start(bf16[208,512]{1,0:T(8,128)(2,1)S(1)} %get-tuple-element.135), channel_id=1, source_target_pairs={{0,32},{32,64},{64,96},{96,0},{1,33},{33,65},{65,97},{97,1},{2,34}... | collective-permute-start | bytes 638984 | tf_op jit(solution)/shard_map/ppermute | solution.py:27
  18.2 7.8 %collective-permute-start.1 = (bf16[208,512]{1,0:T(8,128)(2,1)S(1)}, bf16[208,512]{1,0:T(8,128)(2,1)S(1)}, u32[]{:S(2)}, u32[]{:S(2)}) collective-permute-start(bf16[208,512]{1,0:T(8,128)(2,1)S(1)} %get-tuple-element.135), channel_id=1, source_target_pairs={{0,96},{32,0},{64,32},{96,64},{1,97},{33,1},{65,33},{97,65},{2,98}... | collective-permute-start | bytes 638984 | tf_op jit(solution)/shard_map/ppermute | solution.py:27
  19.7 10.5 %collective-permute-start.5 = (f32[1024]{0:T(1024)S(1)}, f32[1024]{0:T(1024)S(1)}, u32[]{:S(2)}, u32[]{:S(2)}) collective-permute-start(f32[1024]{0:T(1024)S(1)} %copy-done.19), channel_id=1, source_target_pairs={{0,16},{16,0},{1,17},{17,1},{2,18},{18,2},{3,19},{19,3},{4,20},{20... | collective-permute-start | bytes 12296 | tf_op jit(solution)/shard_map/ppermute | solution.py:408
  22.0 10.9 %collective-permute-start.13 = (bf16[104,512]{1,0:T(8,128)(2,1)S(1)}, bf16[104,512]{1,0:T(8,128)(2,1)S(1)}, u32[]{:S(2)}, u32[]{:S(2)}) collective-permute-start(bf16[104,512]{1,0:T(8,128)(2,1)S(1)} %slice.56), channel_id=1, source_target_pairs={{0,16},{16,2},{2,18},{18,0},{1,17},{17,3},{3,19},{19,1},{4,20},{20... | collective-permute-start | bytes 319496 | tf_op jit(solution)/shard_map/ppermute | solution.py:26
  22.1 10.8 %collective-permute-start.14 = (bf16[104,512]{1,0:T(8,128)(2,1)S(1)}, bf16[104,512]{1,0:T(8,128)(2,1)S(1)}, u32[]{:S(2)}, u32[]{:S(2)}) collective-permute-start(bf16[104,512]{1,0:T(8,128)(2,1)S(1)} %slice.57), channel_id=1, source_target_pairs={{0,18},{16,0},{2,16},{18,2},{1,19},{17,1},{3,17},{19,3},{4,22},{20... | collective-permute-start | bytes 319496 | tf_op jit(solution)/shard_map/ppermute | solution.py:26
  24.9 5.2 %collective-permute-start.3 = (bf16[104,512]{1,0:T(8,128)(2,1)S(1)}, bf16[104,512]{1,0:T(8,128)(2,1)S(1)}, u32[]{:S(2)}, u32[]{:S(2)}) collective-permute-start(bf16[104,512]{1,0:T(8,128)(2,1)S(1)} %slice.52), channel_id=1, source_target_pairs={{0,32},{32,64},{64,96},{96,0},{1,33},{33,65},{65,97},{97,1},{2,34}... | collective-permute-start | bytes 319496 | tf_op jit(solution)/shard_map/ppermute | solution.py:27
  26.1 4.0 %collective-permute-start.4 = (bf16[104,512]{1,0:T(8,128)(2,1)S(1)}, bf16[104,512]{1,0:T(8,128)(2,1)S(1)}, u32[]{:S(2)}, u32[]{:S(2)}) collective-permute-start(bf16[104,512]{1,0:T(8,128)(2,1)S(1)} %slice.53), channel_id=1, source_target_pairs={{0,96},{32,0},{64,32},{96,64},{1,97},{33,1},{65,33},{97,65},{2,98}... | collective-permute-start | bytes 319496 | tf_op jit(solution)/shard_map/ppermute | solution.py:27
  30.2 19.2 %collective-permute-start.7 = (bf16[832,512]{1,0:T(8,128)(2,1)S(1)}, bf16[832,512]{1,0:T(8,128)(2,1)S(1)}, u32[]{:S(2)}, u32[]{:S(2)}) collective-permute-start(bf16[832,512]{1,0:T(8,128)(2,1)S(1)} %constant_dynamic-update-slice_fusion.refs_0_), channel_id=1, source_target_pairs={{0,16},{16,2},{2,18},{18,0},{1,17},{17,3},{3,19},{19,1},{4,20},{20... | collective-permute-start | bytes 2555912 | tf_op jit(solution)/shard_map/ppermute | solution.py:26
  30.3 19.2 %collective-permute-start.6 = (bf16[832,512]{1,0:T(8,128)(2,1)S(1)}, bf16[832,512]{1,0:T(8,128)(2,1)S(1)}, u32[]{:S(2)}, u32[]{:S(2)}) collective-permute-start(bf16[832,512]{1,0:T(8,128)(2,1)S(1)} %constant_dynamic-update-slice_fusion.refs_0_), channel_id=1, source_target_pairs={{0,18},{16,0},{2,16},{18,2},{1,19},{17,1},{3,17},{19,3},{4,22},{20... | collective-permute-start | bytes 2555912 | tf_op jit(solution)/shard_map/ppermute | solution.py:26
  33.0 19.2 %collective-permute-start.16 = (bf16[832,512]{1,0:T(8,128)(2,1)S(1)}, bf16[832,512]{1,0:T(8,128)(2,1)S(1)}, u32[]{:S(2)}, u32[]{:S(2)}) collective-permute-start(bf16[832,512]{1,0:T(8,128)(2,1)S(1)} %constant_dynamic-update-slice_fusion.5.refs_0_), channel_id=1, source_target_pairs={{0,32},{32,64},{64,96},{96,0},{1,33},{33,65},{65,97},{97,1},{2,34}... | collective-permute-start | bytes 2555912 | tf_op jit(solution)/shard_map/ppermute | solution.py:27
  34.2 19.2 %collective-permute-start.15 = (bf16[832,512]{1,0:T(8,128)(2,1)S(1)}, bf16[832,512]{1,0:T(8,128)(2,1)S(1)}, u32[]{:S(2)}, u32[]{:S(2)}) collective-permute-start(bf16[832,512]{1,0:T(8,128)(2,1)S(1)} %constant_dynamic-update-slice_fusion.5.refs_0_), channel_id=1, source_target_pairs={{0,96},{32,0},{64,32},{96,64},{1,97},{33,1},{65,33},{97,65},{2,98}... | collective-permute-start | bytes 2555912 | tf_op jit(solution)/shard_map/ppermute | solution.py:27
  49.4 9.2 %collective-permute-start.8 = (bf16[416,512]{1,0:T(8,128)(2,1)S(1)}, bf16[416,512]{1,0:T(8,128)(2,1)S(1)}, u32[]{:S(2)}, u32[]{:S(2)}) collective-permute-start(bf16[416,512]{1,0:T(8,128)(2,1)S(1)} %slice.54), channel_id=1, source_target_pairs={{0,16},{16,2},{2,18},{18,0},{1,17},{17,3},{3,19},{19,1},{4,20},{20... | collective-permute-start | bytes 1277960 | tf_op jit(solution)/shard_map/ppermute | solution.py:26
  49.5 9.1 %collective-permute-start.9 = (bf16[416,512]{1,0:T(8,128)(2,1)S(1)}, bf16[416,512]{1,0:T(8,128)(2,1)S(1)}, u32[]{:S(2)}, u32[]{:S(2)}) collective-permute-start(bf16[416,512]{1,0:T(8,128)(2,1)S(1)} %slice.55), channel_id=1, source_target_pairs={{0,18},{16,0},{2,16},{18,2},{1,19},{17,1},{3,17},{19,3},{4,22},{20... | collective-permute-start | bytes 1277960 | tf_op jit(solution)/shard_map/ppermute | solution.py:26
  52.3 8.9 %collective-permute-start.17 = (bf16[416,512]{1,0:T(8,128)(2,1)S(1)}, bf16[416,512]{1,0:T(8,128)(2,1)S(1)}, u32[]{:S(2)}, u32[]{:S(2)}) collective-permute-start(bf16[416,512]{1,0:T(8,128)(2,1)S(1)} %slice.58), channel_id=1, source_target_pairs={{0,32},{32,64},{64,96},{96,0},{1,33},{33,65},{65,97},{97,1},{2,34}... | collective-permute-start | bytes 1277960 | tf_op jit(solution)/shard_map/ppermute | solution.py:27
  53.5 14.7 %copy-start.17 = (f32[1664]{0:T(1024)S(1)}, f32[1664]{0:T(1024)}, u32[]{:S(2)}) copy-start(f32[1664]{0:T(1024)} %param.9) | copy-start | bytes 19972
  53.5 14.7 %copy-start.18 = (f32[1664]{0:T(1024)S(1)}, f32[1664]{0:T(1024)}, u32[]{:S(2)}) copy-start(f32[1664]{0:T(1024)} %param.10) | copy-start | bytes 19972
  53.5 7.6 %collective-permute-start.18 = (bf16[416,512]{1,0:T(8,128)(2,1)S(1)}, bf16[416,512]{1,0:T(8,128)(2,1)S(1)}, u32[]{:S(2)}, u32[]{:S(2)}) collective-permute-start(bf16[416,512]{1,0:T(8,128)(2,1)S(1)} %slice.59), channel_id=1, source_target_pairs={{0,96},{32,0},{64,32},{96,64},{1,97},{33,1},{65,33},{97,65},{2,98}... | collective-permute-start | bytes 1277960 | tf_op jit(solution)/shard_map/ppermute | solution.py:27
  61.4 1.8 copy-start.2
  63.2 17.5 %collective-permute-start.19 = (bf16[4,2,160,1664]{3,2,1,0:T(8,128)(2,1)}, bf16[4,2,160,1664]{3,2,1,0:T(8,128)(2,1)}, u32[]{:S(2)}, u32[]{:S(2)}) collective-permute-start(bf16[4,2,160,1664]{3,2,1,0:T(8,128)(2,1)} %all-gather.2.cloned.1.call-done.refs_0_), channel_id=1, source_target_pairs={{0,1},{1,0},{2,3},{3,2},{4,5},{5,4},{6,7},{7,6},{8,9},{9,8},{10,11... | collective-permute-start | bytes 12779528 | tf_op jit(solution)/shard_map/ppermute | solution.py:31
  68.3 2.2 %copy-start = (bf16[4,2,160,1664]{3,2,1,0:T(8,128)(2,1)S(1)}, bf16[4,2,160,1664]{3,2,1,0:T(8,128)(2,1)}, u32[]{:S(2)}) copy-start(bf16[4,2,160,1664]{3,2,1,0:T(8,128)(2,1)} %all-gather.2.cloned.1.call-done.refs_0_) | copy-start | bytes 12779524
  70.5 2.4 %copy-start.1 = (bf16[4,2,160,1664]{3,2,1,0:T(8,128)(2,1)S(1)}, bf16[4,2,160,1664]{3,2,1,0:T(8,128)(2,1)}, u32[]{:S(2)}) copy-start(bf16[4,2,160,1664]{3,2,1,0:T(8,128)(2,1)} %all-gather.2.cloned.1.call-done.refs_0_) | copy-start | bytes 12779524
  72.9 2.0 %copy-start.3 = (bf16[1664,1024]{1,0:T(8,128)(2,1)S(1)}, bf16[1664,1024]{1,0:T(8,128)(2,1)}, u32[]{:S(2)}) copy-start(bf16[1664,1024]{1,0:T(8,128)(2,1)} %copy-done.2) | copy-start | bytes 10223620
  101.9 9.0 %collective-permute-start.20 = (bf16[640,1664]{1,0:T(8,128)(2,1)S(1)}, bf16[640,1664]{1,0:T(8,128)(2,1)S(1)}, u32[]{:S(2)}, u32[]{:S(2)}) collective-permute-start(bf16[640,1664]{1,0:T(8,128)(2,1)S(1)} %get-tuple-element.89), channel_id=1, source_target_pairs={{0,1},{1,0},{2,3},{3,2},{4,5},{5,4},{6,7},{7,6},{8,9},{9,8},{10,11... | collective-permute-start | bytes 6389768 | tf_op jit(solution)/shard_map/ppermute | solution.py:31
  105.3 17.4 %collective-permute-start.21 = (bf16[240,1024]{1,0:T(8,128)(2,1)S(1)}, bf16[240,1024]{1,0:T(8,128)(2,1)S(1)}, u32[]{:S(2)}, u32[]{:S(2)}) collective-permute-start(bf16[240,1024]{1,0:T(8,128)(2,1)S(1)} %get-tuple-element.101), channel_id=1, source_target_pairs={{0,32},{32,64},{64,96},{96,0},{1,33},{33,65},{65,97},{97,1},{2,34}... | collective-permute-start | bytes 1474568 | tf_op jit(solution)/shard_map/ppermute | solution.py:27
  106.4 16.4 %collective-permute-start.22 = (bf16[240,1024]{1,0:T(8,128)(2,1)S(1)}, bf16[240,1024]{1,0:T(8,128)(2,1)S(1)}, u32[]{:S(2)}, u32[]{:S(2)}) collective-permute-start(bf16[240,1024]{1,0:T(8,128)(2,1)S(1)} %get-tuple-element.102), channel_id=1, source_target_pairs={{0,96},{32,0},{64,32},{96,64},{1,97},{33,1},{65,33},{97,65},{2,98}... | collective-permute-start | bytes 1474568 | tf_op jit(solution)/shard_map/ppermute | solution.py:27
  108.2 14.5 %collective-permute-start.23 = (bf16[416,512]{1,0:T(8,128)(2,1)S(1)}, bf16[416,512]{1,0:T(8,128)(2,1)S(1)}, u32[]{:S(2)}, u32[]{:S(2)}) collective-permute-start(bf16[416,512]{1,0:T(8,128)(2,1)S(1)} %get-tuple-element.103), channel_id=1, source_target_pairs={{0,16},{16,2},{2,18},{18,0},{1,17},{17,3},{3,19},{19,1},{4,20},{20... | collective-permute-start | bytes 1277960 | tf_op jit(solution)/shard_map/ppermute | solution.py:26
  108.2 14.5 %collective-permute-start.24 = (bf16[416,512]{1,0:T(8,128)(2,1)S(1)}, bf16[416,512]{1,0:T(8,128)(2,1)S(1)}, u32[]{:S(2)}, u32[]{:S(2)}) collective-permute-start(bf16[416,512]{1,0:T(8,128)(2,1)S(1)} %get-tuple-element.104), channel_id=1, source_target_pairs={{0,18},{16,0},{2,16},{18,2},{1,19},{17,1},{3,17},{19,3},{4,22},{20... | collective-permute-start | bytes 1277960 | tf_op jit(solution)/shard_map/ppermute | solution.py:26
  122.7 1.3 copy-start.8
  122.7 1.8 copy-start.10
  124.4 0.9 copy-start.13
  125.3 1.0 copy-start.14
  126.3 1.0 copy-start.15
  127.3 21.7 %collective-permute-start.25 = (bf16[448,1024]{1,0:T(8,128)(2,1)S(1)}, bf16[448,1024]{1,0:T(8,128)(2,1)S(1)}, u32[]{:S(2)}, u32[]{:S(2)}) collective-permute-start(bf16[448,1024]{1,0:T(8,128)(2,1)S(1)} %get-tuple-element.109), channel_id=1, source_target_pairs={{0,32},{32,64},{64,96},{96,0},{1,33},{33,65},{65,97},{97,1},{2,34}... | collective-permute-start | bytes 2752520 | tf_op jit(solution)/shard_map/ppermute | solution.py:27
  127.4 19.5 %collective-permute-start.26 = (bf16[416,1024]{1,0:T(8,128)(2,1)}, bf16[416,1024]{1,0:T(8,128)(2,1)S(1)}, u32[]{:S(2)}, u32[]{:S(2)}) collective-permute-start(bf16[416,1024]{1,0:T(8,128)(2,1)} %copy-done.15), channel_id=1, source_target_pairs={{0,96},{32,0},{64,32},{96,64},{1,97},{33,1},{65,33},{97,65},{2,98}... | collective-permute-start | bytes 2555912 | tf_op jit(solution)/shard_map/ppermute | solution.py:27
  130.1 24.3 %collective-permute-start.30 = (bf16[832,512]{1,0:T(8,128)(2,1)}, bf16[832,512]{1,0:T(8,128)(2,1)S(1)}, u32[]{:S(2)}, u32[]{:S(2)}) collective-permute-start(bf16[832,512]{1,0:T(8,128)(2,1)} %copy-done.14), channel_id=1, source_target_pairs={{0,16},{16,2},{2,18},{18,0},{1,17},{17,3},{3,19},{19,1},{4,20},{20... | collective-permute-start | bytes 2555912 | tf_op jit(solution)/shard_map/ppermute | solution.py:26
  130.1 24.3 %collective-permute-start.31 = (bf16[832,512]{1,0:T(8,128)(2,1)}, bf16[832,512]{1,0:T(8,128)(2,1)S(1)}, u32[]{:S(2)}, u32[]{:S(2)}) collective-permute-start(bf16[832,512]{1,0:T(8,128)(2,1)} %copy-done.13), channel_id=1, source_target_pairs={{0,18},{16,0},{2,16},{18,2},{1,19},{17,1},{3,17},{19,3},{4,22},{20... | collective-permute-start | bytes 2555912 | tf_op jit(solution)/shard_map/ppermute | solution.py:26
  149.1 1.5 copy-start.9
  150.6 3.8 %copy-start.11 = (f32[832,512]{1,0:T(8,128)S(1)}, f32[832,512]{1,0:T(8,128)}, u32[]{:S(2)}) copy-start(f32[832,512]{1,0:T(8,128)} %copy-done.10) | copy-start | bytes 5111812
  150.6 7.2 %copy-start.5 = (bf16[160,1664]{1,0:T(8,128)(2,1)S(1)}, bf16[160,1664]{1,0:T(8,128)(2,1)}, u32[]{:S(2)}) copy-start(bf16[160,1664]{1,0:T(8,128)(2,1)} %refs_0_.3) | copy-start | bytes 1597444
  150.6 7.2 %copy-start.7 = (bf16[160,1664]{1,0:T(8,128)(2,1)S(1)}, bf16[160,1664]{1,0:T(8,128)(2,1)}, u32[]{:S(2)}) copy-start(bf16[160,1664]{1,0:T(8,128)(2,1)} %refs_1_.3) | copy-start | bytes 1597444
  151.7 13.2 %collective-permute-start.27 = (bf16[240,512]{1,0:T(8,128)(2,1)}, bf16[240,512]{1,0:T(8,128)(2,1)S(1)}, u32[]{:S(2)}, u32[]{:S(2)}) collective-permute-start(bf16[240,512]{1,0:T(8,128)(2,1)} %get-tuple-element.113), channel_id=1, source_target_pairs={{0,16},{16,2},{2,18},{18,0},{1,17},{17,3},{3,19},{19,1},{4,20},{20... | collective-permute-start | bytes 737288 | tf_op jit(solution)/shard_map/ppermute | solution.py:26
  151.7 13.2 %collective-permute-start.28 = (bf16[240,512]{1,0:T(8,128)(2,1)}, bf16[240,512]{1,0:T(8,128)(2,1)S(1)}, u32[]{:S(2)}, u32[]{:S(2)}) collective-permute-start(bf16[240,512]{1,0:T(8,128)(2,1)} %get-tuple-element.114), channel_id=1, source_target_pairs={{0,2},{16,18},{2,0},{18,16},{1,3},{17,19},{3,1},{19,17},{4,6},{20,... | collective-permute-start | bytes 737288 | tf_op jit(solution)/shard_map/ppermute | solution.py:26
  153.2 12.1 %collective-permute-start.29 = (bf16[240,512]{1,0:T(8,128)(2,1)}, bf16[240,512]{1,0:T(8,128)(2,1)S(1)}, u32[]{:S(2)}, u32[]{:S(2)}) collective-permute-start(bf16[240,512]{1,0:T(8,128)(2,1)} %get-tuple-element.115), channel_id=1, source_target_pairs={{0,18},{16,0},{2,16},{18,2},{1,19},{17,1},{3,17},{19,3},{4,22},{20... | collective-permute-start | bytes 737288 | tf_op jit(solution)/shard_map/ppermute | solution.py:26
  155.4 8.2 %collective-permute-start.32 = (bf16[208,512]{1,0:T(8,128)(2,1)}, bf16[208,512]{1,0:T(8,128)(2,1)S(1)}, u32[]{:S(2)}, u32[]{:S(2)}) collective-permute-start(bf16[208,512]{1,0:T(8,128)(2,1)} %get-tuple-element.121), channel_id=1, source_target_pairs={{0,32},{32,64},{64,96},{96,0},{1,33},{33,65},{65,97},{97,1},{2,34}... | collective-permute-start | bytes 638984 | tf_op jit(solution)/shard_map/ppermute | solution.py:27
  155.4 9.4 %collective-permute-start.33 = (bf16[208,512]{1,0:T(8,128)(2,1)}, bf16[208,512]{1,0:T(8,128)(2,1)S(1)}, u32[]{:S(2)}, u32[]{:S(2)}) collective-permute-start(bf16[208,512]{1,0:T(8,128)(2,1)} %get-tuple-element.122), channel_id=1, source_target_pairs={{0,64},{32,96},{64,0},{96,32},{1,65},{33,97},{65,1},{97,33},{2,66}... | collective-permute-start | bytes 638984 | tf_op jit(solution)/shard_map/ppermute | solution.py:27
  157.8 1.0 copy-start.12
  165.4 3.0 %collective-permute-start.34 = (f32[8,512]{1,0:T(8,128)S(1)}, f32[8,512]{1,0:T(8,128)S(1)}, u32[]{:S(2)}, u32[]{:S(2)}) collective-permute-start(f32[8,512]{1,0:T(8,128)S(1)} %slice.47), channel_id=1, source_target_pairs={{0,4},{4,0},{8,12},{12,8},{1,5},{5,1},{9,13},{13,9},{2,6},{6,2},{1... | collective-permute-start | bytes 49160 | tf_op jit(solution)/shard_map/ppermute | solution.py:44
  166.7 10.1 %collective-permute-start.37 = (bf16[208,512]{1,0:T(8,128)(2,1)S(1)}, bf16[208,512]{1,0:T(8,128)(2,1)S(1)}, u32[]{:S(2)}, u32[]{:S(2)}) collective-permute-start(bf16[208,512]{1,0:T(8,128)(2,1)S(1)} %get-tuple-element.127), channel_id=1, source_target_pairs={{0,96},{32,0},{64,32},{96,64},{1,97},{33,1},{65,33},{97,65},{2,98}... | collective-permute-start | bytes 638984 | tf_op jit(solution)/shard_map/ppermute | solution.py:27
  168.4 9.1 %collective-permute-start.35 = (f32[8,512]{1,0:T(8,128)S(1)}, f32[8,512]{1,0:T(8,128)S(1)}, u32[]{:S(2)}, u32[]{:S(2)}) collective-permute-start(f32[8,512]{1,0:T(8,128)S(1)} %slice_add_fusion), channel_id=1, source_target_pairs={{0,8},{4,12},{8,0},{12,4},{1,9},{5,13},{9,1},{13,5},{2,10},{6,14},... | collective-permute-start | bytes 49160 | tf_op jit(solution)/shard_map/ppermute | solution.py:44
  171.8 6.7 %collective-permute-start.39 = (f32[512]{0:T(512)S(1)}, f32[512]{0:T(512)S(1)}, u32[]{:S(2)}, u32[]{:S(2)}) collective-permute-start(f32[512]{0:T(512)S(1)} %bitcast.17), channel_id=1, source_target_pairs={{0,1},{1,0},{2,3},{3,2},{4,5},{5,4},{6,7},{7,6},{8,9},{9,8},{10,11... | collective-permute-start | bytes 6152 | tf_op jit(solution)/shard_map/ppermute | solution.py:31
  176.9 3.7 %collective-permute-start.38 = (f32[104,512]{1,0:T(8,128)S(1)}, f32[104,512]{1,0:T(8,128)S(1)}, u32[]{:S(2)}, u32[]{:S(2)}) collective-permute-start(f32[104,512]{1,0:T(8,128)S(1)} %get-tuple-element.129), channel_id=1, source_target_pairs={{0,1},{1,0},{2,3},{3,2},{4,5},{5,4},{6,7},{7,6},{8,9},{9,8},{10,11... | collective-permute-start | bytes 638984 | tf_op jit(solution)/shard_map/ppermute | solution.py:31
  177.1 4.3 %collective-permute-start.40 = (f32[104,512]{1,0:T(8,128)S(1)}, f32[104,512]{1,0:T(8,128)S(1)}, u32[]{:S(2)}, u32[]{:S(2)}) collective-permute-start(f32[104,512]{1,0:T(8,128)S(1)} %get-tuple-element.131), channel_id=1, source_target_pairs={{0,1},{1,0},{2,3},{3,2},{4,5},{5,4},{6,7},{7,6},{8,9},{9,8},{10,11... | collective-permute-start | bytes 638984 | tf_op jit(solution)/shard_map/ppermute | solution.py:31
  177.5 1.9 %collective-permute-start.36 = (f32[8,512]{1,0:T(8,128)S(1)}, f32[8,512]{1,0:T(8,128)S(1)}, u32[]{:S(2)}, u32[]{:S(2)}) collective-permute-start(f32[8,512]{1,0:T(8,128)S(1)} %add.33), channel_id=1, source_target_pairs={{0,1},{1,0},{2,3},{3,2},{4,5},{5,4},{6,7},{7,6},{8,9},{9,8},{10,11... | collective-permute-start | bytes 49160 | tf_op jit(solution)/shard_map/ppermute | solution.py:31
Sparse Core Ops, SparseCore 0:
  10.5 52.2 all-gather.1
  127.4 29.5 reduce-scatter.1

commit v4 on v3

--- a/solution.py
+++ b/solution.py
@@ -343,6 +343,19 @@
     given[...] = jnp.where(core == 0, bottom, top)
 
 
+def join_kernel(kept, got, whole):
+    half, core = kept.shape[1], lax.axis_index("core")
+    whole[:, :half] = jnp.where(core == 0, kept[...], got[...])
+    whole[:, half:] = jnp.where(core == 0, got[...], kept[...])
+
+
+def norm_sums_kernel(own, others, gain, plain):
+    for first, to in ((0, gain), (4, plain)):
+        for r in range(to.shape[0]):
+            at = slice(first + r // 4, first + r // 4 + 1), slice(r % 4 * 128, r % 4 * 128 + 128)
+            to[r : r + 1, :] = own[at] + others[at]
+
+
 def inputs_kernel(inputs, upstream, grad, gain, result):
     tokens, width = inputs.shape
 
@@ -513,13 +526,14 @@
     e_kept, e_given = call(last_kernel, [part, part], (e_mine, e_behind))
 
     def by_rows(kept, given):
-        got = swap(given)
-        return jnp.where(core == 0, jnp.concatenate([kept, got], 1), jnp.concatenate([got, kept], 1))
+        return call(join_kernel, [((rows, 2 * half), f32)], (kept, swap(given)))[0]
 
     shrink_grad, expand_grad = by_rows(s_kept, s_given), by_rows(e_kept, e_given)
     norm_sums = pair_sum(vector[:8], "z")
-    norm_sums = norm_sums + swap(norm_sums)
-    gain_grad, shift_grad = (norm_sums[i : i + 4].reshape(-1)[:width] for i in (0, 4))
+    lines = ((width // 128, 128), f32)
+    gain_grad, shift_grad = (
+        part.reshape(width) for part in call(norm_sums_kernel, [lines, lines], (norm_sums, swap(norm_sums)))
+    )
     bias_mine = lax.dynamic_index_in_dim(vector, 8 + ylo, 0, keepdims=False)
     bias_other = swap(bias_mine)
     bias_grad = jnp.where(

time: 189 us -> 186 us (0.984)
  local copies, waits for them, and re-layouts: 17 us -> 11.9 us
  Pallas kernels: 51.5 us -> 55.3 us
    ppermute x15, waiting for transfers between devices: 24.5 us -> 5.97 us  [shift(): return lax.ppermute(value, axis, [(i, (i + by) % 4) for i in range(4)])]
    ppermute x15, waiting for transfers between devices: 19.5 us -> 37.7 us  [shift(): return lax.ppermute(value, PLANE_Y, pairs)]
    unnamed x50 -> x41, local copies, waits for them, and re-layouts: 15.8 us -> 10.7 us
    pallas_call x17 -> x20, Pallas kernels: 51.5 us -> 55.3 us  [call(): pl.pallas_call(body, out_shape=[jax.ShapeDtypeStruct(shape, dtype) for sh...]
  transfers between devices with their start and end apart: 43 -> 43, of which waited for: 13 -> 11; matrix products, arithmetic and copies ran while one was open for 2% -> 1% of each run, Pallas kernels for 15% -> 16%
where the time goes in v4:
time: 186 us; the launch traced here: 185 us
  starting transfers between devices  57.9 us (31%)
  Pallas kernels  55.3 us (30%)
  waiting for transfers between devices  44.8 us (24%)
  between operations  14.5 us (8%)
  local copies, waits for them, and re-layouts  11.9 us (6%)
    pallas_call x20, Pallas kernels, call(): pl.pallas_call(body, out_shape=[jax.ShapeDtypeStruct(shape, dtype) for sh...  55.3 us
    ppermute x15, waiting for transfers between devices, shift(): return lax.ppermute(value, PLANE_Y, pairs)  37.7 us
    ppermute x15, starting transfers between devices, shift(): return lax.ppermute(value, axis, [(i, (i + by) % 4) for i in range(4)])  19.9 us
    ppermute x15, starting transfers between devices, shift(): return lax.ppermute(value, PLANE_Y, pairs)  19.4 us
    ppermute x8, starting transfers between devices, swap(): return lax.ppermute(value, 'core', [(0, 1), (1, 0)])  13.8 us
    unnamed x41, local copies, waits for them, and re-layouts  10.7 us
    ppermute x15, waiting for transfers between devices, shift(): return lax.ppermute(value, axis, [(i, (i + by) % 4) for i in range(4)])  5.97 us
    ppermute x2, starting transfers between devices, pair_sum(): value = value + lax.ppermute(value, axis, [(i, i ^ bit) for i in range(4)])  4.82 us
  transfers between devices with their start and end apart: 43, of which 11 were waited for; matrix products, arithmetic and copies ran while one was open for 1% of the time, Pallas kernels for 16%

profile of v4, /device:TPU:1, one launch (start us, length us, event | category | flops | bytes accessed | tf_op | source)
XLA Modules:
  0.0 185.2 jit_solution(3141808249829076376)
XLA Ops:
  7.2 1.0 copy-done.4
  8.3 1.0 copy-done.6
  9.3 1.1 shard_map.118
  10.5 1.0 constant_dynamic-slice_fusion.1
  11.4 1.5 collective-permute-start.10
  13.1 0.8 collective-permute-done.10
  13.9 1.4 collective-permute-start.12
  15.4 1.5 collective-permute-start.11
  17.0 1.3 collective-permute-start.2
  18.2 1.5 collective-permute-start.1
  19.7 2.3 %collective-permute-done.12 = bf16[208,512]{1,0:T(8,128)(2,1)S(1)} collective-permute-done((bf16[208,512]{1,0:T(8,128)(2,1)S(1)}, bf16[208,512]{1,0:T(8,128)(2,1)S(1)}, u32[]{:S(2)}, u32[]{:S(2)}) %collective-permute-start.12) | collective-permute-done | bytes 213024 | tf_op jit(solution)/shard_map/ppermute | solution.py:26
  22.1 2.7 %collective-permute-start.14 = (bf16[104,512]{1,0:T(8,128)(2,1)S(1)}, bf16[104,512]{1,0:T(8,128)(2,1)S(1)}, u32[]{:S(2)}, u32[]{:S(2)}) collective-permute-start(bf16[104,512]{1,0:T(8,128)(2,1)S(1)} %slice.41), channel_id=1, source_target_pairs={{0,18},{16,0},{2,16},{18,2},{1,19},{17,1},{3,17},{19,3},{4,22},{20... | collective-permute-start | bytes 319496 | tf_op jit(solution)/shard_map/ppermute | solution.py:26
  24.9 1.2 collective-permute-start.3
  26.1 1.6 collective-permute-start.4
  27.7 2.4 %collective-permute-done.3 = bf16[104,512]{1,0:T(8,128)(2,1)S(1)} collective-permute-done((bf16[104,512]{1,0:T(8,128)(2,1)S(1)}, bf16[104,512]{1,0:T(8,128)(2,1)S(1)}, u32[]{:S(2)}, u32[]{:S(2)}) %collective-permute-start.3) | collective-permute-done | bytes 106528 | tf_op jit(solution)/shard_map/ppermute | solution.py:27
  30.3 2.7 %collective-permute-start.6 = (bf16[832,512]{1,0:T(8,128)(2,1)S(1)}, bf16[832,512]{1,0:T(8,128)(2,1)S(1)}, u32[]{:S(2)}, u32[]{:S(2)}) collective-permute-start(bf16[832,512]{1,0:T(8,128)(2,1)S(1)} %constant_dynamic-update-slice_fusion.refs_0_), channel_id=1, source_target_pairs={{0,18},{16,0},{2,16},{18,2},{1,19},{17,1},{3,17},{19,3},{4,22},{20... | collective-permute-start | bytes 2555912 | tf_op jit(solution)/shard_map/ppermute | solution.py:26
  33.0 1.2 collective-permute-start.16
  34.2 1.6 collective-permute-start.15
  35.9 13.5 %collective-permute-done.7.refs_4_ = bf16[832,512]{1,0:T(8,128)(2,1)S(1)} collective-permute-done((bf16[832,512]{1,0:T(8,128)(2,1)S(1)}, bf16[832,512]{1,0:T(8,128)(2,1)S(1)}, u32[]{:S(2)}, u32[]{:S(2)}) %collective-permute-start.7) | collective-permute-done | bytes 852000 | tf_op jit(solution)/shard_map/ppermute | solution.py:26
  49.5 2.7 %collective-permute-start.9 = (bf16[416,512]{1,0:T(8,128)(2,1)S(1)}, bf16[416,512]{1,0:T(8,128)(2,1)S(1)}, u32[]{:S(2)}, u32[]{:S(2)}) collective-permute-start(bf16[416,512]{1,0:T(8,128)(2,1)S(1)} %slice.39), channel_id=1, source_target_pairs={{0,18},{16,0},{2,16},{18,2},{1,19},{17,1},{3,17},{19,3},{4,22},{20... | collective-permute-start | bytes 1277960 | tf_op jit(solution)/shard_map/ppermute | solution.py:26
  52.3 1.2 collective-permute-start.17
  53.5 1.7 collective-permute-start.18
  55.3 3.3 %collective-permute-done.8.refs_2_ = bf16[416,512]{1,0:T(8,128)(2,1)S(1)} collective-permute-done((bf16[416,512]{1,0:T(8,128)(2,1)S(1)}, bf16[416,512]{1,0:T(8,128)(2,1)S(1)}, u32[]{:S(2)}, u32[]{:S(2)}) %collective-permute-start.8) | collective-permute-done | bytes 426016 | tf_op jit(solution)/shard_map/ppermute | solution.py:26
  58.6 0.3 shard_map.119
  58.9 2.3 %collective-permute-done.17.refs_2_ = bf16[416,512]{1,0:T(8,128)(2,1)S(1)} collective-permute-done((bf16[416,512]{1,0:T(8,128)(2,1)S(1)}, bf16[416,512]{1,0:T(8,128)(2,1)S(1)}, u32[]{:S(2)}, u32[]{:S(2)}) %collective-permute-start.17) | collective-permute-done | bytes 426016 | tf_op jit(solution)/shard_map/ppermute | solution.py:27
  61.4 1.8 copy-done.2
  63.2 4.9 %collective-permute-start.19 = (bf16[4,2,160,1664]{3,2,1,0:T(8,128)(2,1)}, bf16[4,2,160,1664]{3,2,1,0:T(8,128)(2,1)}, u32[]{:S(2)}, u32[]{:S(2)}) collective-permute-start(bf16[4,2,160,1664]{3,2,1,0:T(8,128)(2,1)} %all-gather.2.cloned.1.call-done.refs_0_), channel_id=1, source_target_pairs={{0,1},{1,0},{2,3},{3,2},{4,5},{5,4},{6,7},{7,6},{8,9},{9,8},{10,11... | collective-permute-start | bytes 12779528 | tf_op jit(solution)/shard_map/ppermute | solution.py:31
  68.3 2.2 %copy-done = bf16[4,2,160,1664]{3,2,1,0:T(8,128)(2,1)S(1)} copy-done((bf16[4,2,160,1664]{3,2,1,0:T(8,128)(2,1)S(1)}, bf16[4,2,160,1664]{3,2,1,0:T(8,128)(2,1)}, u32[]{:S(2)}) %copy-start) | copy-done | bytes 4259864
  70.5 2.4 %shard_map.121 = (bf16[640,1664]{1,0:T(8,128)(2,1)S(1)}, f32[640,1]{1,0:T(8,128)S(1)}, f32[640,1]{1,0:T(8,128)S(1)}, bf16[1664,1280]{1,0:T(8,128)(2,1)S(1)}, bf16[1664,1280]{1,0:T(8,128)(2,1)S(1)}) custom-call(bf16[4,2,160,1664]{3,2,1,0:T(8,128)(2,1)S(1)} %copy-done, f32[1,1664]{1,0:T(1,128)S(1)} %broadcast_in_dim.7.refs_1_.refs_3_, ...), custom_call_target="tpu_custom_call" | custom-call | flops 1000000 | bytes 1000000 | tf_op jit(solution)/shard_map/pallas_call | solution.py:98
  72.9 2.0 %copy-done.3 = bf16[1664,1024]{1,0:T(8,128)(2,1)S(1)} copy-done((bf16[1664,1024]{1,0:T(8,128)(2,1)S(1)}, bf16[1664,1024]{1,0:T(8,128)(2,1)}, u32[]{:S(2)}) %copy-start.3) | copy-done | bytes 3407896
  74.8 5.9 %shard_map.122 = (f32[1,1024]{1,0:T(1,128)S(1)}, bf16[1280,1024]{1,0:T(8,128)(2,1)S(1)}, bf16[1280,1024]{1,0:T(8,128)(2,1)S(1)}) custom-call(bf16[4,2,160,1664]{3,2,1,0:T(8,128)(2,1)S(1)} %copy-done.1, bf16[640,1664]{1,0:T(8,128)(2,1)S(1)} %get-tuple-element.83.refs_1_, bf16[1664,1024]{1,0:T(8,128)(2,1)S(1)} %get-tuple-element.79.refs_2_.refs_4_.refs_7_, ...), custom_call_target="tpu_custom_call" | custom-call | flops 1000000 | bytes 1000000 | tf_op jit(solution)/shard_map/pallas_call | solution.py:98
  80.7 12.3 %shard_map.123 = (f32[640,1]{1,0:T(8,128)S(1)}, f32[640,1]{1,0:T(8,128)S(1)}, bf16[1664,1280]{1,0:T(8,128)(2,1)S(1)}, bf16[1664,1280]{1,0:T(8,128)(2,1)S(1)}, f3...) custom-call(bf16[4,2,160,1664]{3,2,1,0:T(8,128)(2,1)} %collective-pe, ...), custom_call_target="tpu_custom_call", output_to_operand_aliasing={{2}: (6, {}), {3}: (7, {}), {5}: (8, {}), {6}: (9, {})} | custom-call | flops 1000000 | bytes 1000000 | tf_op jit(solution)/shard_map/pallas_call | solution.py:98
  93.0 8.9 %shard_map.124 = (f32[640,1664]{1,0:T(8,128)S(1)}, bf16[640,1664]{1,0:T(8,128)(2,1)S(1)}, f32[2,1664]{1,0:T(2,128)S(1)}) custom-call(bf16[4,2,160,1664]{3,2,1,0:T(8,128)(2,1)S(1)} %copy-done.1, bf16[4,2,160,1664]{3,2,1,0:T(8,128)(2,1)} %collective-permute-done.19.refs_0_.refs_1_, f32[640,1]{1,0:T(8,128)S(1)} %get-tuple-element.77.refs_2_, ...), custom_call_target="tpu_custom_call" | custom-call | flops 1000000 | bytes 1000000 | tf_op jit(solution)/shard_map/pallas_call | solution.py:98
  102.0 3.3 %shard_map.125 = (bf16[240,1024]{1,0:T(8,128)(2,1)S(1)}, bf16[240,1024]{1,0:T(8,128)(2,1)S(1)}, bf16[416,512]{1,0:T(8,128)(2,1)S(1)}, bf16[416,512]{1,0:T(8,128)(2,1)S(1)}, f32[16,1024]{1,0:T(8,128)S(1)}) custom-call(bf16[1664,1280]{1,0:T(8,128)(2,1)S(1)} %get-tuple-element.92.refs_0_, bf16[1280,1024]{1,0:T(8,128)(2,1)S(1)} %get-tuple-element.93.refs_1_, ...), custom_call_target="tpu_custom_call" | custom-call | flops 1000000 | bytes 1000000 | tf_op jit(solution)/shard_map/pallas_call | solution.py:98
  105.3 1.0 collective-permute-start.21
  106.3 1.9 %collective-permute-start.22 = (bf16[240,1024]{1,0:T(8,128)(2,1)S(1)}, bf16[240,1024]{1,0:T(8,128)(2,1)S(1)}, u32[]{:S(2)}, u32[]{:S(2)}) collective-permute-start(bf16[240,1024]{1,0:T(8,128)(2,1)S(1)} %get-tuple-element.104), channel_id=1, source_target_pairs={{0,96},{32,0},{64,32},{96,64},{1,97},{33,1},{65,33},{97,65},{2,98}... | collective-permute-start | bytes 1474568 | tf_op jit(solution)/shard_map/ppermute | solution.py:27
  108.2 2.7 %collective-permute-start.24 = (bf16[416,512]{1,0:T(8,128)(2,1)S(1)}, bf16[416,512]{1,0:T(8,128)(2,1)S(1)}, u32[]{:S(2)}, u32[]{:S(2)}) collective-permute-start(bf16[416,512]{1,0:T(8,128)(2,1)S(1)} %get-tuple-element.106), channel_id=1, source_target_pairs={{0,18},{16,0},{2,16},{18,2},{1,19},{17,1},{3,17},{19,3},{4,22},{20... | collective-permute-start | bytes 1277960 | tf_op jit(solution)/shard_map/ppermute | solution.py:26
  110.9 1.8 shard_map.126
  112.7 10.0 %shard_map.127 = (f32[416,1024]{1,0:T(8,128)S(1)}, f32[832,512]{1,0:T(8,128)S(1)}, f32[2,416,1024]{2,1,0:T(8,128)S(1)}, f32[2,832,512]{2,1,0:T(8,128)S(1)}) custom-call(bf16[1664,1280]{1,0:T(8,128)(2,1)S(1)} %get-tuple-element.92.refs_0_, bf16[1280,1024]{1,0:T(8,128)(2,1)S(1)} %get-tuple-element.93.refs_1_, ...), custom_call_target="tpu_custom_call" | custom-call | flops 1000000 | bytes 1000000 | tf_op jit(solution)/shard_map/pallas_call | solution.py:98
  122.8 2.2 %shard_map.128 = (bf16[448,1024]{1,0:T(8,128)(2,1)}, bf16[416,1024]{1,0:T(8,128)(2,1)}, bf16[832,512]{1,0:T(8,128)(2,1)S(1)}, bf16[832,512]{1,0:T(8,128)(2,1)S(1)}, f32[8,128]{1,0:T(8,128)S(1)}) custom-call(f32[2,416,1024]{2,1,0:T(8,128)S(1)} %get-tuple-element.101.refs_0_, f32[2,832,512]{2,1,0:T(8,128)S(1)} %get-tuple-element.102.refs_1_, ...), custom_call_target="tpu_custom_call" | custom-call | flops 1000000 | bytes 1000000 | tf_op jit(solution)/shard_map/pallas_call | solution.py:98
  125.1 2.7 %collective-permute-start.31 = (bf16[832,512]{1,0:T(8,128)(2,1)S(1)}, bf16[832,512]{1,0:T(8,128)(2,1)S(1)}, u32[]{:S(2)}, u32[]{:S(2)}) collective-permute-start(bf16[832,512]{1,0:T(8,128)(2,1)S(1)} %get-tuple-element.121), channel_id=1, source_target_pairs={{0,18},{16,0},{2,16},{18,2},{1,19},{17,1},{3,17},{19,3},{4,22},{20... | collective-permute-start | bytes 2555912 | tf_op jit(solution)/shard_map/ppermute | solution.py:26
  127.8 2.7 %collective-permute-start.26 = (bf16[416,1024]{1,0:T(8,128)(2,1)}, bf16[416,1024]{1,0:T(8,128)(2,1)S(1)}, u32[]{:S(2)}, u32[]{:S(2)}) collective-permute-start(bf16[416,1024]{1,0:T(8,128)(2,1)} %get-tuple-element.112), channel_id=1, source_target_pairs={{0,96},{32,0},{64,32},{96,64},{1,97},{33,1},{65,33},{97,65},{2,98}... | collective-permute-start | bytes 2555912 | tf_op jit(solution)/shard_map/ppermute | solution.py:27
  130.4 14.9 %collective-permute-done.30.refs_1_ = bf16[832,512]{1,0:T(8,128)(2,1)S(1)} collective-permute-done((bf16[832,512]{1,0:T(8,128)(2,1)S(1)}, bf16[832,512]{1,0:T(8,128)(2,1)S(1)}, u32[]{:S(2)}, u32[]{:S(2)}) %collective-permute-start.30) | collective-permute-done | bytes 852000 | tf_op jit(solution)/shard_map/ppermute | solution.py:26
  145.4 1.5 copy-done.11
  146.9 0.9 shard_map.131
  147.8 1.3 collective-permute-done.25.refs_1_
  149.1 1.1 shard_map.130
  150.3 2.3 %collective-permute-start.28 = (bf16[240,512]{1,0:T(8,128)(2,1)}, bf16[240,512]{1,0:T(8,128)(2,1)S(1)}, u32[]{:S(2)}, u32[]{:S(2)}) collective-permute-start(bf16[240,512]{1,0:T(8,128)(2,1)} %get-tuple-element.116), channel_id=1, source_target_pairs={{0,2},{16,18},{2,0},{18,16},{1,3},{17,19},{3,1},{19,17},{4,6},{20,... | collective-permute-start | bytes 737288 | tf_op jit(solution)/shard_map/ppermute | solution.py:26
  152.6 0.4 collective-permute-start.29
  152.9 2.0 %collective-permute-start.33 = (bf16[208,512]{1,0:T(8,128)(2,1)}, bf16[208,512]{1,0:T(8,128)(2,1)S(1)}, u32[]{:S(2)}, u32[]{:S(2)}) collective-permute-start(bf16[208,512]{1,0:T(8,128)(2,1)} %get-tuple-element.124), channel_id=1, source_target_pairs={{0,64},{32,96},{64,0},{96,32},{1,65},{33,97},{65,1},{97,33},{2,66}... | collective-permute-start | bytes 638984 | tf_op jit(solution)/shard_map/ppermute | solution.py:27
  155.0 0.9 collective-permute-start.37
  155.9 1.0 copy-done.12
  156.9 2.4 %shard_map.129 = (bf16[160,1664]{1,0:T(8,128)(2,1)}, f32[8,128]{1,0:T(8,128)S(1)}) custom-call(bf16[160,1664]{1,0:T(8,128)(2,1)S(1)} %copy-done.5, bf16[160,1664]{1,0:T(8,128)(2,1)S(1)} %copy-done.7, bf16[160,1664]{1,0:T(8,128)(2,1)S(1)} %copy-done.12, f32[1,1664]{1,0:T(1,128)S(1)} %broadcast_in_dim.7.refs_1_.refs_3_), custom_call_target="tpu_custom_call" | custom-call | flops 1000000 | bytes 1000000 | tf_op jit(solution)/shard_map/pallas_call | solution.py:98
  159.4 2.0 %collective-permute-done.28.refs_2_ = bf16[240,512]{1,0:T(8,128)(2,1)S(1)} collective-permute-done((bf16[240,512]{1,0:T(8,128)(2,1)}, bf16[240,512]{1,0:T(8,128)(2,1)S(1)}, u32[]{:S(2)}, u32[]{:S(2)}) %collective-permute-start.28) | collective-permute-done | bytes 245792 | tf_op jit(solution)/shard_map/ppermute | solution.py:26
  161.5 1.7 collective-permute-done.29.refs_3_
  163.3 1.4 collective-permute-start.34
  164.7 3.3 %collective-permute-start.38 = (f32[104,512]{1,0:T(8,128)S(1)}, f32[104,512]{1,0:T(8,128)S(1)}, u32[]{:S(2)}, u32[]{:S(2)}) collective-permute-start(f32[104,512]{1,0:T(8,128)S(1)} %get-tuple-element.133), channel_id=1, source_target_pairs={{0,1},{1,0},{2,3},{3,2},{4,5},{5,4},{6,7},{7,6},{8,9},{9,8},{10,11... | collective-permute-start | bytes 638984 | tf_op jit(solution)/shard_map/ppermute | solution.py:31
  168.1 3.4 %collective-permute-start.35 = (f32[8,512]{1,0:T(8,128)S(1)}, f32[8,512]{1,0:T(8,128)S(1)}, u32[]{:S(2)}, u32[]{:S(2)}) collective-permute-start(f32[8,512]{1,0:T(8,128)S(1)} %slice_add_fusion), channel_id=1, source_target_pairs={{0,8},{4,12},{8,0},{12,4},{1,9},{5,13},{9,1},{13,5},{2,10},{6,14},... | collective-permute-start | bytes 49160 | tf_op jit(solution)/shard_map/ppermute | solution.py:44
  171.6 2.1 %collective-permute-start.39 = (f32[512]{0:T(512)S(1)}, f32[512]{0:T(512)S(1)}, u32[]{:S(2)}, u32[]{:S(2)}) collective-permute-start(f32[512]{0:T(512)S(1)} %bitcast.11), channel_id=1, source_target_pairs={{0,1},{1,0},{2,3},{3,2},{4,5},{5,4},{6,7},{7,6},{8,9},{9,8},{10,11... | collective-permute-start | bytes 6152 | tf_op jit(solution)/shard_map/ppermute | solution.py:31
  173.6 1.7 collective-permute-start.36
  175.3 0.6 maximum_select_fusion.2
  176.2 0.6 shard_map.134
  176.8 0.8 shard_map.136
  177.6 0.8 shard_map.137
  (108 shorter events, 2.1 us)
Async XLA Ops:
  7.2 56.1 %all-gather.2.cloned.1.call-start = ((), (), s32[]{:S(2)}) async-start(), calls=%async_computation.1 | async-start | bytes 5324800 | tf_op jit(solution)/shard_map/all_gather | solution.py:425
  7.2 1.0 copy-start.4
  8.3 1.0 copy-start.6
  9.3 3.6 %copy-start.13 = (bf16[104,1024]{1,0:T(8,128)(2,1)S(1)}, bf16[104,1024]{1,0:T(8,128)(2,1)}, u32[]{:S(2)}) copy-start(bf16[104,1024]{1,0:T(8,128)(2,1)} %param.11) | copy-start | bytes 638980
  9.3 10.4 %copy-start.16 = (f32[1024]{0:T(1024)S(1)}, f32[1024]{0:T(1024)}, u32[]{:S(2)}) copy-start(f32[1024]{0:T(1024)} %param.12) | copy-start | bytes 12292
  10.4 145.5 %reduce-scatter.2.cloned.1.call-start = ((), (), s32[]{:S(2)}) async-start(), calls=%async_computation.2 | async-start | bytes 2662400 | tf_op jit(solution)/shard_map/reduce_scatter | solution.py:507
  11.4 2.5 %collective-permute-start.10 = (bf16[104,512]{1,0:T(8,128)(2,1)S(1)}, bf16[104,512]{1,0:T(8,128)(2,1)S(1)}, u32[]{:S(2)}, u32[]{:S(2)}) collective-permute-start(bf16[104,512]{1,0:T(8,128)(2,1)S(1)} %get-tuple-element.140), channel_id=1, source_target_pairs={{0,1},{1,0},{2,3},{3,2},{4,5},{5,4},{6,7},{7,6},{8,9},{9,8},{10,11... | collective-permute-start | bytes 319496 | tf_op jit(solution)/shard_map/ppermute | solution.py:31
  13.0 4.0 %collective-permute-start = (bf16[104,512]{1,0:T(8,128)(2,1)S(1)}, bf16[104,512]{1,0:T(8,128)(2,1)S(1)}, u32[]{:S(2)}, u32[]{:S(2)}) collective-permute-start(bf16[104,512]{1,0:T(8,128)(2,1)S(1)} %get-tuple-element.142), channel_id=1, source_target_pairs={{0,1},{1,0},{2,3},{3,2},{4,5},{5,4},{6,7},{7,6},{8,9},{9,8},{10,11... | collective-permute-start | bytes 319496 | tf_op jit(solution)/shard_map/ppermute | solution.py:31
  13.9 8.1 %collective-permute-start.12 = (bf16[208,512]{1,0:T(8,128)(2,1)S(1)}, bf16[208,512]{1,0:T(8,128)(2,1)S(1)}, u32[]{:S(2)}, u32[]{:S(2)}) collective-permute-start(bf16[208,512]{1,0:T(8,128)(2,1)S(1)} %get-tuple-element.137), channel_id=1, source_target_pairs={{0,16},{16,2},{2,18},{18,0},{1,17},{17,3},{3,19},{19,1},{4,20},{20... | collective-permute-start | bytes 638984 | tf_op jit(solution)/shard_map/ppermute | solution.py:26
  15.4 6.7 %collective-permute-start.11 = (bf16[208,512]{1,0:T(8,128)(2,1)S(1)}, bf16[208,512]{1,0:T(8,128)(2,1)S(1)}, u32[]{:S(2)}, u32[]{:S(2)}) collective-permute-start(bf16[208,512]{1,0:T(8,128)(2,1)S(1)} %get-tuple-element.137), channel_id=1, source_target_pairs={{0,18},{16,0},{2,16},{18,2},{1,19},{17,1},{3,17},{19,3},{4,22},{20... | collective-permute-start | bytes 638984 | tf_op jit(solution)/shard_map/ppermute | solution.py:26
  17.0 7.9 %collective-permute-start.2 = (bf16[208,512]{1,0:T(8,128)(2,1)S(1)}, bf16[208,512]{1,0:T(8,128)(2,1)S(1)}, u32[]{:S(2)}, u32[]{:S(2)}) collective-permute-start(bf16[208,512]{1,0:T(8,128)(2,1)S(1)} %get-tuple-element.139), channel_id=1, source_target_pairs={{0,32},{32,64},{64,96},{96,0},{1,33},{33,65},{65,97},{97,1},{2,34}... | collective-permute-start | bytes 638984 | tf_op jit(solution)/shard_map/ppermute | solution.py:27
  18.2 7.8 %collective-permute-start.1 = (bf16[208,512]{1,0:T(8,128)(2,1)S(1)}, bf16[208,512]{1,0:T(8,128)(2,1)S(1)}, u32[]{:S(2)}, u32[]{:S(2)}) collective-permute-start(bf16[208,512]{1,0:T(8,128)(2,1)S(1)} %get-tuple-element.139), channel_id=1, source_target_pairs={{0,96},{32,0},{64,32},{96,64},{1,97},{33,1},{65,33},{97,65},{2,98}... | collective-permute-start | bytes 638984 | tf_op jit(solution)/shard_map/ppermute | solution.py:27
  19.7 10.5 %collective-permute-start.5 = (f32[1024]{0:T(1024)S(1)}, f32[1024]{0:T(1024)S(1)}, u32[]{:S(2)}, u32[]{:S(2)}) collective-permute-start(f32[1024]{0:T(1024)S(1)} %copy-done.16), channel_id=1, source_target_pairs={{0,16},{16,0},{1,17},{17,1},{2,18},{18,2},{3,19},{19,3},{4,20},{20... | collective-permute-start | bytes 12296 | tf_op jit(solution)/shard_map/ppermute | solution.py:421
  22.0 10.9 %collective-permute-start.13 = (bf16[104,512]{1,0:T(8,128)(2,1)S(1)}, bf16[104,512]{1,0:T(8,128)(2,1)S(1)}, u32[]{:S(2)}, u32[]{:S(2)}) collective-permute-start(bf16[104,512]{1,0:T(8,128)(2,1)S(1)} %slice.40), channel_id=1, source_target_pairs={{0,16},{16,2},{2,18},{18,0},{1,17},{17,3},{3,19},{19,1},{4,20},{20... | collective-permute-start | bytes 319496 | tf_op jit(solution)/shard_map/ppermute | solution.py:26
  22.1 10.8 %collective-permute-start.14 = (bf16[104,512]{1,0:T(8,128)(2,1)S(1)}, bf16[104,512]{1,0:T(8,128)(2,1)S(1)}, u32[]{:S(2)}, u32[]{:S(2)}) collective-permute-start(bf16[104,512]{1,0:T(8,128)(2,1)S(1)} %slice.41), channel_id=1, source_target_pairs={{0,18},{16,0},{2,16},{18,2},{1,19},{17,1},{3,17},{19,3},{4,22},{20... | collective-permute-start | bytes 319496 | tf_op jit(solution)/shard_map/ppermute | solution.py:26
  24.9 5.2 %collective-permute-start.3 = (bf16[104,512]{1,0:T(8,128)(2,1)S(1)}, bf16[104,512]{1,0:T(8,128)(2,1)S(1)}, u32[]{:S(2)}, u32[]{:S(2)}) collective-permute-start(bf16[104,512]{1,0:T(8,128)(2,1)S(1)} %slice.36), channel_id=1, source_target_pairs={{0,32},{32,64},{64,96},{96,0},{1,33},{33,65},{65,97},{97,1},{2,34}... | collective-permute-start | bytes 319496 | tf_op jit(solution)/shard_map/ppermute | solution.py:27
  26.1 4.0 %collective-permute-start.4 = (bf16[104,512]{1,0:T(8,128)(2,1)S(1)}, bf16[104,512]{1,0:T(8,128)(2,1)S(1)}, u32[]{:S(2)}, u32[]{:S(2)}) collective-permute-start(bf16[104,512]{1,0:T(8,128)(2,1)S(1)} %slice.37), channel_id=1, source_target_pairs={{0,96},{32,0},{64,32},{96,64},{1,97},{33,1},{65,33},{97,65},{2,98}... | collective-permute-start | bytes 319496 | tf_op jit(solution)/shard_map/ppermute | solution.py:27
  30.2 19.2 %collective-permute-start.7 = (bf16[832,512]{1,0:T(8,128)(2,1)S(1)}, bf16[832,512]{1,0:T(8,128)(2,1)S(1)}, u32[]{:S(2)}, u32[]{:S(2)}) collective-permute-start(bf16[832,512]{1,0:T(8,128)(2,1)S(1)} %constant_dynamic-update-slice_fusion.refs_0_), channel_id=1, source_target_pairs={{0,16},{16,2},{2,18},{18,0},{1,17},{17,3},{3,19},{19,1},{4,20},{20... | collective-permute-start | bytes 2555912 | tf_op jit(solution)/shard_map/ppermute | solution.py:26
  30.3 19.2 %collective-permute-start.6 = (bf16[832,512]{1,0:T(8,128)(2,1)S(1)}, bf16[832,512]{1,0:T(8,128)(2,1)S(1)}, u32[]{:S(2)}, u32[]{:S(2)}) collective-permute-start(bf16[832,512]{1,0:T(8,128)(2,1)S(1)} %constant_dynamic-update-slice_fusion.refs_0_), channel_id=1, source_target_pairs={{0,18},{16,0},{2,16},{18,2},{1,19},{17,1},{3,17},{19,3},{4,22},{20... | collective-permute-start | bytes 2555912 | tf_op jit(solution)/shard_map/ppermute | solution.py:26
  33.0 19.2 %collective-permute-start.16 = (bf16[832,512]{1,0:T(8,128)(2,1)S(1)}, bf16[832,512]{1,0:T(8,128)(2,1)S(1)}, u32[]{:S(2)}, u32[]{:S(2)}) collective-permute-start(bf16[832,512]{1,0:T(8,128)(2,1)S(1)} %constant_dynamic-update-slice_fusion.5.refs_0_), channel_id=1, source_target_pairs={{0,32},{32,64},{64,96},{96,0},{1,33},{33,65},{65,97},{97,1},{2,34}... | collective-permute-start | bytes 2555912 | tf_op jit(solution)/shard_map/ppermute | solution.py:27
  34.2 19.2 %collective-permute-start.15 = (bf16[832,512]{1,0:T(8,128)(2,1)S(1)}, bf16[832,512]{1,0:T(8,128)(2,1)S(1)}, u32[]{:S(2)}, u32[]{:S(2)}) collective-permute-start(bf16[832,512]{1,0:T(8,128)(2,1)S(1)} %constant_dynamic-update-slice_fusion.5.refs_0_), channel_id=1, source_target_pairs={{0,96},{32,0},{64,32},{96,64},{1,97},{33,1},{65,33},{97,65},{2,98}... | collective-permute-start | bytes 2555912 | tf_op jit(solution)/shard_map/ppermute | solution.py:27
  49.4 9.2 %collective-permute-start.8 = (bf16[416,512]{1,0:T(8,128)(2,1)S(1)}, bf16[416,512]{1,0:T(8,128)(2,1)S(1)}, u32[]{:S(2)}, u32[]{:S(2)}) collective-permute-start(bf16[416,512]{1,0:T(8,128)(2,1)S(1)} %slice.38), channel_id=1, source_target_pairs={{0,16},{16,2},{2,18},{18,0},{1,17},{17,3},{3,19},{19,1},{4,20},{20... | collective-permute-start | bytes 1277960 | tf_op jit(solution)/shard_map/ppermute | solution.py:26
  49.5 9.1 %collective-permute-start.9 = (bf16[416,512]{1,0:T(8,128)(2,1)S(1)}, bf16[416,512]{1,0:T(8,128)(2,1)S(1)}, u32[]{:S(2)}, u32[]{:S(2)}) collective-permute-start(bf16[416,512]{1,0:T(8,128)(2,1)S(1)} %slice.39), channel_id=1, source_target_pairs={{0,18},{16,0},{2,16},{18,2},{1,19},{17,1},{3,17},{19,3},{4,22},{20... | collective-permute-start | bytes 1277960 | tf_op jit(solution)/shard_map/ppermute | solution.py:26
  52.3 8.9 %collective-permute-start.17 = (bf16[416,512]{1,0:T(8,128)(2,1)S(1)}, bf16[416,512]{1,0:T(8,128)(2,1)S(1)}, u32[]{:S(2)}, u32[]{:S(2)}) collective-permute-start(bf16[416,512]{1,0:T(8,128)(2,1)S(1)} %slice.42), channel_id=1, source_target_pairs={{0,32},{32,64},{64,96},{96,0},{1,33},{33,65},{65,97},{97,1},{2,34}... | collective-permute-start | bytes 1277960 | tf_op jit(solution)/shard_map/ppermute | solution.py:27
  53.5 14.7 %copy-start.14 = (f32[1664]{0:T(1024)S(1)}, f32[1664]{0:T(1024)}, u32[]{:S(2)}) copy-start(f32[1664]{0:T(1024)} %param.9) | copy-start | bytes 19972
  53.5 14.7 %copy-start.15 = (f32[1664]{0:T(1024)S(1)}, f32[1664]{0:T(1024)}, u32[]{:S(2)}) copy-start(f32[1664]{0:T(1024)} %param.10) | copy-start | bytes 19972
  53.5 7.6 %collective-permute-start.18 = (bf16[416,512]{1,0:T(8,128)(2,1)S(1)}, bf16[416,512]{1,0:T(8,128)(2,1)S(1)}, u32[]{:S(2)}, u32[]{:S(2)}) collective-permute-start(bf16[416,512]{1,0:T(8,128)(2,1)S(1)} %slice.43), channel_id=1, source_target_pairs={{0,96},{32,0},{64,32},{96,64},{1,97},{33,1},{65,33},{97,65},{2,98}... | collective-permute-start | bytes 1277960 | tf_op jit(solution)/shard_map/ppermute | solution.py:27
  61.4 1.8 copy-start.2
  63.2 17.5 %collective-permute-start.19 = (bf16[4,2,160,1664]{3,2,1,0:T(8,128)(2,1)}, bf16[4,2,160,1664]{3,2,1,0:T(8,128)(2,1)}, u32[]{:S(2)}, u32[]{:S(2)}) collective-permute-start(bf16[4,2,160,1664]{3,2,1,0:T(8,128)(2,1)} %all-gather.2.cloned.1.call-done.refs_0_), channel_id=1, source_target_pairs={{0,1},{1,0},{2,3},{3,2},{4,5},{5,4},{6,7},{7,6},{8,9},{9,8},{10,11... | collective-permute-start | bytes 12779528 | tf_op jit(solution)/shard_map/ppermute | solution.py:31
  68.3 2.2 %copy-start = (bf16[4,2,160,1664]{3,2,1,0:T(8,128)(2,1)S(1)}, bf16[4,2,160,1664]{3,2,1,0:T(8,128)(2,1)}, u32[]{:S(2)}) copy-start(bf16[4,2,160,1664]{3,2,1,0:T(8,128)(2,1)} %all-gather.2.cloned.1.call-done.refs_0_) | copy-start | bytes 12779524
  70.5 2.4 %copy-start.1 = (bf16[4,2,160,1664]{3,2,1,0:T(8,128)(2,1)S(1)}, bf16[4,2,160,1664]{3,2,1,0:T(8,128)(2,1)}, u32[]{:S(2)}) copy-start(bf16[4,2,160,1664]{3,2,1,0:T(8,128)(2,1)} %all-gather.2.cloned.1.call-done.refs_0_) | copy-start | bytes 12779524
  72.9 2.0 %copy-start.3 = (bf16[1664,1024]{1,0:T(8,128)(2,1)S(1)}, bf16[1664,1024]{1,0:T(8,128)(2,1)}, u32[]{:S(2)}) copy-start(bf16[1664,1024]{1,0:T(8,128)(2,1)} %copy-done.2) | copy-start | bytes 10223620
  101.9 9.0 %collective-permute-start.20 = (bf16[640,1664]{1,0:T(8,128)(2,1)S(1)}, bf16[640,1664]{1,0:T(8,128)(2,1)S(1)}, u32[]{:S(2)}, u32[]{:S(2)}) collective-permute-start(bf16[640,1664]{1,0:T(8,128)(2,1)S(1)} %get-tuple-element.91), channel_id=1, source_target_pairs={{0,1},{1,0},{2,3},{3,2},{4,5},{5,4},{6,7},{7,6},{8,9},{9,8},{10,11... | collective-permute-start | bytes 6389768 | tf_op jit(solution)/shard_map/ppermute | solution.py:31
  105.3 17.4 %collective-permute-start.21 = (bf16[240,1024]{1,0:T(8,128)(2,1)S(1)}, bf16[240,1024]{1,0:T(8,128)(2,1)S(1)}, u32[]{:S(2)}, u32[]{:S(2)}) collective-permute-start(bf16[240,1024]{1,0:T(8,128)(2,1)S(1)} %get-tuple-element.103), channel_id=1, source_target_pairs={{0,32},{32,64},{64,96},{96,0},{1,33},{33,65},{65,97},{97,1},{2,34}... | collective-permute-start | bytes 1474568 | tf_op jit(solution)/shard_map/ppermute | solution.py:27
  106.3 16.4 %collective-permute-start.22 = (bf16[240,1024]{1,0:T(8,128)(2,1)S(1)}, bf16[240,1024]{1,0:T(8,128)(2,1)S(1)}, u32[]{:S(2)}, u32[]{:S(2)}) collective-permute-start(bf16[240,1024]{1,0:T(8,128)(2,1)S(1)} %get-tuple-element.104), channel_id=1, source_target_pairs={{0,96},{32,0},{64,32},{96,64},{1,97},{33,1},{65,33},{97,65},{2,98}... | collective-permute-start | bytes 1474568 | tf_op jit(solution)/shard_map/ppermute | solution.py:27
  108.2 14.5 %collective-permute-start.23 = (bf16[416,512]{1,0:T(8,128)(2,1)S(1)}, bf16[416,512]{1,0:T(8,128)(2,1)S(1)}, u32[]{:S(2)}, u32[]{:S(2)}) collective-permute-start(bf16[416,512]{1,0:T(8,128)(2,1)S(1)} %get-tuple-element.105), channel_id=1, source_target_pairs={{0,16},{16,2},{2,18},{18,0},{1,17},{17,3},{3,19},{19,1},{4,20},{20... | collective-permute-start | bytes 1277960 | tf_op jit(solution)/shard_map/ppermute | solution.py:26
  108.2 14.5 %collective-permute-start.24 = (bf16[416,512]{1,0:T(8,128)(2,1)S(1)}, bf16[416,512]{1,0:T(8,128)(2,1)S(1)}, u32[]{:S(2)}, u32[]{:S(2)}) collective-permute-start(bf16[416,512]{1,0:T(8,128)(2,1)S(1)} %get-tuple-element.106), channel_id=1, source_target_pairs={{0,18},{16,0},{2,16},{18,2},{1,19},{17,1},{3,17},{19,3},{4,22},{20... | collective-permute-start | bytes 1277960 | tf_op jit(solution)/shard_map/ppermute | solution.py:26
  122.7 2.3 %copy-start.8 = (f32[416,1024]{1,0:T(8,128)}, f32[416,1024]{1,0:T(8,128)S(1)}, u32[]{:S(2)}) copy-start(f32[416,1024]{1,0:T(8,128)S(1)} %get-tuple-element.110.refs_0_) | copy-start | bytes 5111812
  122.7 2.3 %copy-start.10 = (f32[832,512]{1,0:T(8,128)}, f32[832,512]{1,0:T(8,128)S(1)}, u32[]{:S(2)}) copy-start(f32[832,512]{1,0:T(8,128)S(1)} %get-tuple-element.119.refs_0_) | copy-start | bytes 5111812
  125.0 24.1 %copy-start.9 = (f32[416,1024]{1,0:T(8,128)S(1)}, f32[416,1024]{1,0:T(8,128)}, u32[]{:S(2)}) copy-start(f32[416,1024]{1,0:T(8,128)} %copy-done.8) | copy-start | bytes 5111812
  125.0 20.4 %collective-permute-start.30 = (bf16[832,512]{1,0:T(8,128)(2,1)S(1)}, bf16[832,512]{1,0:T(8,128)(2,1)S(1)}, u32[]{:S(2)}, u32[]{:S(2)}) collective-permute-start(bf16[832,512]{1,0:T(8,128)(2,1)S(1)} %get-tuple-element.120), channel_id=1, source_target_pairs={{0,16},{16,2},{2,18},{18,0},{1,17},{17,3},{3,19},{19,1},{4,20},{20... | collective-permute-start | bytes 2555912 | tf_op jit(solution)/shard_map/ppermute | solution.py:26
  125.1 20.3 %collective-permute-start.31 = (bf16[832,512]{1,0:T(8,128)(2,1)S(1)}, bf16[832,512]{1,0:T(8,128)(2,1)S(1)}, u32[]{:S(2)}, u32[]{:S(2)}) collective-permute-start(bf16[832,512]{1,0:T(8,128)(2,1)S(1)} %get-tuple-element.121), channel_id=1, source_target_pairs={{0,18},{16,0},{2,16},{18,2},{1,19},{17,1},{3,17},{19,3},{4,22},{20... | collective-permute-start | bytes 2555912 | tf_op jit(solution)/shard_map/ppermute | solution.py:26
  127.8 21.3 %collective-permute-start.25 = (bf16[448,1024]{1,0:T(8,128)(2,1)}, bf16[448,1024]{1,0:T(8,128)(2,1)S(1)}, u32[]{:S(2)}, u32[]{:S(2)}) collective-permute-start(bf16[448,1024]{1,0:T(8,128)(2,1)} %get-tuple-element.111), channel_id=1, source_target_pairs={{0,32},{32,64},{64,96},{96,0},{1,33},{33,65},{65,97},{97,1},{2,34}... | collective-permute-start | bytes 2752520 | tf_op jit(solution)/shard_map/ppermute | solution.py:27
  127.8 20.0 %collective-permute-start.26 = (bf16[416,1024]{1,0:T(8,128)(2,1)}, bf16[416,1024]{1,0:T(8,128)(2,1)S(1)}, u32[]{:S(2)}, u32[]{:S(2)}) collective-permute-start(bf16[416,1024]{1,0:T(8,128)(2,1)} %get-tuple-element.112), channel_id=1, source_target_pairs={{0,96},{32,0},{64,32},{96,64},{1,97},{33,1},{65,33},{97,65},{2,98}... | collective-permute-start | bytes 2555912 | tf_op jit(solution)/shard_map/ppermute | solution.py:27
  145.4 1.5 copy-start.11
  146.9 9.0 %copy-start.5 = (bf16[160,1664]{1,0:T(8,128)(2,1)S(1)}, bf16[160,1664]{1,0:T(8,128)(2,1)}, u32[]{:S(2)}) copy-start(bf16[160,1664]{1,0:T(8,128)(2,1)} %refs_0_.3) | copy-start | bytes 1597444
  146.9 9.0 %copy-start.7 = (bf16[160,1664]{1,0:T(8,128)(2,1)S(1)}, bf16[160,1664]{1,0:T(8,128)(2,1)}, u32[]{:S(2)}) copy-start(bf16[160,1664]{1,0:T(8,128)(2,1)} %refs_1_.3) | copy-start | bytes 1597444
  147.8 7.2 %collective-permute-start.32 = (bf16[208,512]{1,0:T(8,128)(2,1)S(1)}, bf16[208,512]{1,0:T(8,128)(2,1)S(1)}, u32[]{:S(2)}, u32[]{:S(2)}) collective-permute-start(bf16[208,512]{1,0:T(8,128)(2,1)S(1)} %get-tuple-element.123), channel_id=1, source_target_pairs={{0,32},{32,64},{64,96},{96,0},{1,33},{33,65},{65,97},{97,1},{2,34}... | collective-permute-start | bytes 638984 | tf_op jit(solution)/shard_map/ppermute | solution.py:27
  150.3 9.2 %collective-permute-start.27 = (bf16[240,512]{1,0:T(8,128)(2,1)}, bf16[240,512]{1,0:T(8,128)(2,1)S(1)}, u32[]{:S(2)}, u32[]{:S(2)}) collective-permute-start(bf16[240,512]{1,0:T(8,128)(2,1)} %get-tuple-element.115), channel_id=1, source_target_pairs={{0,16},{16,2},{2,18},{18,0},{1,17},{17,3},{3,19},{19,1},{4,20},{20... | collective-permute-start | bytes 737288 | tf_op jit(solution)/shard_map/ppermute | solution.py:26
  150.3 11.2 %collective-permute-start.28 = (bf16[240,512]{1,0:T(8,128)(2,1)}, bf16[240,512]{1,0:T(8,128)(2,1)S(1)}, u32[]{:S(2)}, u32[]{:S(2)}) collective-permute-start(bf16[240,512]{1,0:T(8,128)(2,1)} %get-tuple-element.116), channel_id=1, source_target_pairs={{0,2},{16,18},{2,0},{18,16},{1,3},{17,19},{3,1},{19,17},{4,6},{20,... | collective-permute-start | bytes 737288 | tf_op jit(solution)/shard_map/ppermute | solution.py:26
  152.6 10.6 %collective-permute-start.29 = (bf16[240,512]{1,0:T(8,128)(2,1)}, bf16[240,512]{1,0:T(8,128)(2,1)S(1)}, u32[]{:S(2)}, u32[]{:S(2)}) collective-permute-start(bf16[240,512]{1,0:T(8,128)(2,1)} %get-tuple-element.117), channel_id=1, source_target_pairs={{0,18},{16,0},{2,16},{18,2},{1,19},{17,1},{3,17},{19,3},{4,22},{20... | collective-permute-start | bytes 737288 | tf_op jit(solution)/shard_map/ppermute | solution.py:26
  152.9 6.4 %collective-permute-start.33 = (bf16[208,512]{1,0:T(8,128)(2,1)}, bf16[208,512]{1,0:T(8,128)(2,1)S(1)}, u32[]{:S(2)}, u32[]{:S(2)}) collective-permute-start(bf16[208,512]{1,0:T(8,128)(2,1)} %get-tuple-element.124), channel_id=1, source_target_pairs={{0,64},{32,96},{64,0},{96,32},{1,65},{33,97},{65,1},{97,33},{2,66}... | collective-permute-start | bytes 638984 | tf_op jit(solution)/shard_map/ppermute | solution.py:27
  155.0 9.7 %collective-permute-start.37 = (bf16[208,512]{1,0:T(8,128)(2,1)}, bf16[208,512]{1,0:T(8,128)(2,1)S(1)}, u32[]{:S(2)}, u32[]{:S(2)}) collective-permute-start(bf16[208,512]{1,0:T(8,128)(2,1)} %get-tuple-element.131), channel_id=1, source_target_pairs={{0,96},{32,0},{64,32},{96,64},{1,97},{33,1},{65,33},{97,65},{2,98}... | collective-permute-start | bytes 638984 | tf_op jit(solution)/shard_map/ppermute | solution.py:27
  155.9 1.0 copy-start.12
  163.3 4.9 %collective-permute-start.34 = (f32[8,512]{1,0:T(8,128)S(1)}, f32[8,512]{1,0:T(8,128)S(1)}, u32[]{:S(2)}, u32[]{:S(2)}) collective-permute-start(f32[8,512]{1,0:T(8,128)S(1)} %slice.35), channel_id=1, source_target_pairs={{0,4},{4,0},{8,12},{12,8},{1,5},{5,1},{9,13},{13,9},{2,6},{6,2},{1... | collective-permute-start | bytes 49160 | tf_op jit(solution)/shard_map/ppermute | solution.py:44
  164.7 12.0 %collective-permute-start.38 = (f32[104,512]{1,0:T(8,128)S(1)}, f32[104,512]{1,0:T(8,128)S(1)}, u32[]{:S(2)}, u32[]{:S(2)}) collective-permute-start(f32[104,512]{1,0:T(8,128)S(1)} %get-tuple-element.133), channel_id=1, source_target_pairs={{0,1},{1,0},{2,3},{3,2},{4,5},{5,4},{6,7},{7,6},{8,9},{9,8},{10,11... | collective-permute-start | bytes 638984 | tf_op jit(solution)/shard_map/ppermute | solution.py:31
  168.0 9.6 %collective-permute-start.40 = (f32[104,512]{1,0:T(8,128)S(1)}, f32[104,512]{1,0:T(8,128)S(1)}, u32[]{:S(2)}, u32[]{:S(2)}) collective-permute-start(f32[104,512]{1,0:T(8,128)S(1)} %get-tuple-element.135), channel_id=1, source_target_pairs={{0,1},{1,0},{2,3},{3,2},{4,5},{5,4},{6,7},{7,6},{8,9},{9,8},{10,11... | collective-permute-start | bytes 638984 | tf_op jit(solution)/shard_map/ppermute | solution.py:31
  168.1 5.5 %collective-permute-start.35 = (f32[8,512]{1,0:T(8,128)S(1)}, f32[8,512]{1,0:T(8,128)S(1)}, u32[]{:S(2)}, u32[]{:S(2)}) collective-permute-start(f32[8,512]{1,0:T(8,128)S(1)} %slice_add_fusion), channel_id=1, source_target_pairs={{0,8},{4,12},{8,0},{12,4},{1,9},{5,13},{9,1},{13,5},{2,10},{6,14},... | collective-permute-start | bytes 49160 | tf_op jit(solution)/shard_map/ppermute | solution.py:44
  171.6 3.8 %collective-permute-start.39 = (f32[512]{0:T(512)S(1)}, f32[512]{0:T(512)S(1)}, u32[]{:S(2)}, u32[]{:S(2)}) collective-permute-start(f32[512]{0:T(512)S(1)} %bitcast.11), channel_id=1, source_target_pairs={{0,1},{1,0},{2,3},{3,2},{4,5},{5,4},{6,7},{7,6},{8,9},{9,8},{10,11... | collective-permute-start | bytes 6152 | tf_op jit(solution)/shard_map/ppermute | solution.py:31
  173.6 2.5 %collective-permute-start.36 = (f32[8,512]{1,0:T(8,128)S(1)}, f32[8,512]{1,0:T(8,128)S(1)}, u32[]{:S(2)}, u32[]{:S(2)}) collective-permute-start(f32[8,512]{1,0:T(8,128)S(1)} %add.30.refs_0_), channel_id=1, source_target_pairs={{0,1},{1,0},{2,3},{3,2},{4,5},{5,4},{6,7},{7,6},{8,9},{9,8},{10,11... | collective-permute-start | bytes 49160 | tf_op jit(solution)/shard_map/ppermute | solution.py:31
Sparse Core Ops, SparseCore 0:
  10.5 52.2 all-gather.1
  125.1 29.4 reduce-scatter.1
